TPU v7x, 512 devices: a whole 4x4x16 slice. The times are simulated.
512 devices in a mesh: rep: 32 (over y_hi, z), fsdp: 16 (over y_lo, x, core).
Axes of the slice: x: 4, y: 4 (y_hi: 2, y_lo: 2; y = y_hi * 2 + y_lo), z: 16, core: 2. Of those that a mesh axis runs over, the one named last changes fastest.
Arguments:
- hidden: bfloat16 [512, 128, 5120], P(('rep', 'fsdp')), may hold values from -6 to 6
- norm_gain: float32 [5120], replicated, may hold values from 0.1 to 1.9
- quant_ref: bfloat16 [5120, 512], P('fsdp'), may hold values from -6 to 6
- scale_ref: float32 [4, 5120], P(None, 'fsdp'), may hold values from 0.007 to 0.028
- weight_prm: bfloat16 [5120, 512], P('fsdp'), may hold values from -0.078125 to 0.078125
- readout: bfloat16 [512, 128, 512], P(('rep', 'fsdp')), may hold values from -0.59765625 to 0.59765625
- lengths: int32 [512], P(('rep', 'fsdp')), may hold values from 32 to 128
- bounds: int32 [512, 8], P(('rep', 'fsdp')), may hold values from 0 to 127, as said below
- labels: int32 [512], P(('rep', 'fsdp')), may hold values from 0 to 1
Outputs:
- step_rewards: float32 [512, 8], P(('rep', 'fsdp'))
- grad_prm: float32 [5120, 512], P('fsdp')
Inputs may be any that keep to these rules, and one draw needn't show every extreme that they name: bounds[s, 0] is 0 and bounds[s, j] lies in [j * 16, (j + 1) * 16).
All inputs are finite; a program needn't handle non-finite values.
Results may differ from a plain program's by a relative error of at most 0.0051.
Values may be sent and summed in bfloat16 or wider, within the bound.
No kernel may reach another device: no remote copies, remote signals or barrier semaphores. Data moves between devices by JAX's collectives and lax.ppermute only.
A program may use at most 64 MiB of HBM per device.

v0:
```python
import jax
import jax.numpy as jnp
from jax import lax
from jax.sharding import PartitionSpec as P

epsilon = 1e-06
beta_scale = 0.05


def on_device(
    hidden, norm_gain, quant_ref, scale_ref, weight_prm, readout, lengths, bounds, labels
):
    seq_count, seq_len, width = hidden.shape
    features = readout.shape[2]
    heads_count = scale_ref.shape[0]
    head_size = features // heads_count
    steps_count = bounds.shape[1]
    group_size = lax.axis_size("fsdp")
    wide = hidden.astype(jnp.float32)
    mean_square = jnp.mean(wide * wide, axis=-1, keepdims=True)
    normed = (wide * lax.rsqrt(mean_square + epsilon) * norm_gain).astype(jnp.bfloat16)
    flat_rows = normed.reshape(seq_count * seq_len, width)
    expanded = jnp.repeat(scale_ref.T, head_size, axis=1)
    ref_local = (quant_ref.astype(jnp.float32) * expanded).astype(jnp.bfloat16)
    columns = lax.all_to_all(flat_rows, "fsdp", split_axis=1, concat_axis=0, tiled=True)
    position = jnp.arange(seq_len, dtype=jnp.int32)
    prm_all, ref_all = (
        lax.all_gather(weight_prm, "fsdp", axis=0, tiled=True),
        lax.all_gather(ref_local, "fsdp", axis=0, tiled=True),
    )
    value_prm = jnp.dot(flat_rows, prm_all, preferred_element_type=jnp.float32)
    value_ref = jnp.dot(flat_rows, ref_all, preferred_element_type=jnp.float32)
    read_wide = readout.astype(jnp.float32).reshape(seq_count * seq_len, features)
    margin = jnp.sum((value_prm - value_ref) * read_wide, axis=-1).reshape(seq_count, seq_len)
    live = (position[None, :] < lengths[:, None]).astype(jnp.float32)
    reward = beta_scale * margin * live
    total = jnp.sum(reward, axis=1)
    weight_seq = beta_scale * (jax.nn.sigmoid(total) - labels.astype(jnp.float32))
    slope = (weight_seq[:, None, None] * live[:, :, None] * readout.astype(jnp.float32)).astype(
        jnp.bfloat16
    )
    slope_group = lax.all_gather(slope, "fsdp", axis=0, tiled=True)
    step_index = (
        jnp.sum((position[None, :, None] >= bounds[:, None, :]).astype(jnp.int32), axis=-1) - 1
    )
    onehot = (
        step_index[:, :, None] == jnp.arange(steps_count, dtype=jnp.int32)[None, None, :]
    ).astype(jnp.float32)
    step_rewards = jnp.sum(reward[:, :, None] * onehot, axis=1)
    slope_rows = slope_group.reshape(group_size * seq_count * seq_len, features)
    local_grad = lax.dot_general(
        columns, slope_rows, (((0,), (0,)), ((), ())), preferred_element_type=jnp.float32
    )
    grad_prm = lax.psum(local_grad, "rep")
    return (step_rewards, grad_prm)


def solution(mesh):
    in_specs = (
        P(("rep", "fsdp"), None, None),
        P(),
        P("fsdp", None),
        P(None, "fsdp"),
        P("fsdp", None),
        P(("rep", "fsdp"), None, None),
        P(("rep", "fsdp")),
        P(("rep", "fsdp"), None),
        P(("rep", "fsdp")),
    )
    out_specs = (P(("rep", "fsdp"), None), P("fsdp", None))
    return jax.shard_map(
        on_device, mesh=mesh, in_specs=in_specs, out_specs=out_specs, check_vma=False
    )
```

profile of v0, /device:TPU:38, one launch (start us, length us, event | category | flops | bytes accessed | tf_op | source)
XLA Modules:
  0.0 468.2 jit_solution(6344959853360565114)
XLA Ops:
  7.2 0.0 copy-start
  7.2 0.0 all-gather.6.cloned.1.call-start
  7.2 0.9 copy.15
  8.1 0.0 copy-start.2
  8.2 0.4 broadcast_in_dim.2
  8.6 1.8 fusion.21
  10.4 0.0 all-gather.6.cloned.1.call-update
  10.4 0.0 all-gather.4.cloned.1.call-start
  10.4 0.7 all-gather.4.cloned.1.call-update
  11.1 0.0 all-gather.8.cloned.1.call-start
  12.5 0.0 copy-done
  12.5 0.3 fusion
  12.8 0.0 copy-done.2
  12.8 0.4 fusion.2
  13.2 0.0 copy-start.1
  13.3 47.3 %all-gather.6.cloned.1.call-done = bf16[5120,512]{1,0:T(8,128)(2,1)} async-done(((bf16[320,512]{1,0:T(8,128)(2,1)}), bf16[5120,512]{1,0:T(8,128)(2,1)}) %all-gather.6.cloned.1.call-update) | async-done | bytes 5242896 | tf_op jit(solution)/shard_map/all_gather | solution.py:29
  60.6 3.3 fusion.5
  63.9 46.2 %all-gather.4.cloned.1.call-done = bf16[5120,512]{1,0:T(8,128)(2,1)} async-done(((bf16[320,512]{1,0:T(8,128)(2,1)}), bf16[5120,512]{1,0:T(8,128)(2,1)}) %all-gather.4.cloned.1.call-update) | async-done | bytes 5242896 | tf_op jit(solution)/shard_map/all_gather | solution.py:28
  110.1 0.0 copy-done.1
  110.1 3.4 fusion.18
  113.5 0.6 fusion.23
  114.9 0.7 fusion.22
  115.7 0.0 all-gather.8.cloned.1.call-update
  115.7 0.0 all-reduce.2.cloned.1.call-start
  115.7 0.8 copy.16
  116.5 22.7 %all_to_all.16 = bf16[128,16,320]{0,2,1:T(8,128)(2,1)S(1)} all-to-all(bf16[128,16,320]{0,2,1:T(8,128)(2,1)S(1)} %bitcast.39), channel_id=1, replica_groups=mesh['rep'=32,'fsdp'=16] {'fsdp'}, dimensions={1} | all-to-all | bytes 2621440 | tf_op jit(solution)/shard_map/all_to_all | solution.py:25
  139.2 0.0 copy-start.3
  139.2 20.0 %all-gather.8.cloned.1.call-done = bf16[16,128,512]{2,1,0:T(8,128)(2,1)} async-done(((bf16[1,128,512]{2,1,0:T(8,128)(2,1)}), bf16[16,128,512]{2,1,0:T(8,128)(2,1)}) %all-gather.8.cloned.1.call-update) | async-done | bytes 2097168 | tf_op jit(solution)/shard_map/all_gather | solution.py:42
  159.2 3.3 fusion.9
  162.4 0.0 all-reduce.2.cloned.1.call-update
  162.5 0.0 copy-done.3
  162.5 0.1 convert_reduce_fusion
  162.6 0.6 select_reduce_fusion
  163.2 296.5 %all-reduce.2.cloned.1.call-done = f32[320,512]{1,0:T(8,128)} async-done(((f32[320,512]{1,0:T(8,128)}), f32[320,512]{1,0:T(8,128)}) %all-reduce.2.cloned.1.call-update) | async-done | bytes 655376 | tf_op jit(solution)/shard_map/psum | solution.py:54
  459.7 2.0 copy.22
  (3 shorter events, 0.0 us)
Async XLA Ops:
  7.2 5.3 %copy-start = (bf16[1,128,5120]{2,1,0:T(8,128)(2,1)S(1)}, bf16[1,128,5120]{2,1,0:T(8,128)(2,1)}, u32[]{:S(2)}) copy-start(bf16[1,128,5120]{2,1,0:T(8,128)(2,1)} %param.9) | copy-start | bytes 3932164
  7.2 53.4 %all-gather.6.cloned.1.call-start = ((), (), s32[]{:S(2)}) async-start(), calls=%async_computation.2 | async-start | bytes 5570560 | tf_op jit(solution)/shard_map/all_gather | solution.py:29
  8.1 4.7 %copy-start.2 = (f32[5120]{0:T(1024)S(1)}, f32[5120]{0:T(1024)}, u32[]{:S(2)}) copy-start(f32[5120]{0:T(1024)} %param.10) | copy-start | bytes 61444
  10.4 99.7 %all-gather.4.cloned.1.call-start = ((), (), s32[]{:S(2)}) async-start(), calls=%async_computation.1 | async-start | bytes 5570560 | tf_op jit(solution)/shard_map/all_gather | solution.py:28
  11.1 148.0 %all-gather.8.cloned.1.call-start = ((), (), s32[]{:S(2)}) async-start(), calls=%async_computation.3 | async-start | bytes 2228224 | tf_op jit(solution)/shard_map/all_gather | solution.py:42
  13.2 96.9 %copy-start.1 = (bf16[1,128,512]{2,1,0:T(8,128)(2,1)S(1)}, bf16[1,128,512]{2,1,0:T(8,128)(2,1)}, u32[]{:S(2)}) copy-start(bf16[1,128,512]{2,1,0:T(8,128)(2,1)} %param.14) | copy-start | bytes 393220
  115.7 344.0 %all-reduce.2.cloned.1.call-start = ((), (), s32[]{:S(2)}) async-start(), calls=%async_computation.4 | async-start | bytes 1310720 | tf_op jit(solution)/shard_map/psum | solution.py:54
  139.2 23.3 %copy-start.3 = (s32[1,8]{1,0:T(1,128)S(1)}, s32[1,8]{1,0:T(1,128)}, u32[]{:S(2)}) copy-start(s32[1,8]{1,0:T(1,128)} %param.16) | copy-start | bytes 100
Sparse Core Ops, SparseCore 0:
  10.7 49.8 all-gather.5
  62.7 47.3 all-gather.3
  115.8 43.3 all-gather.7
  162.6 297.0 all-reduce.1
where the time goes:
time: 469 us; the launch traced here: 468 us
  waiting for transfers between devices  411 us (88%)
  blocking collectives  22.7 us (5%)
  between operations  15.9 us (3%)
  matrix products  10 us (2%)
    psum x1, waiting for transfers between devices, on_device(): grad_prm = lax.psum(local_grad, 'rep')  296 us
    all_gather x1, waiting for transfers between devices, on_device(): lax.all_gather(ref_local, 'fsdp', axis=0, tiled=True)  47.3 us
    all_gather x1, waiting for transfers between devices, on_device(): lax.all_gather(weight_prm, 'fsdp', axis=0, tiled=True)  46.2 us
    all_to_all x1, blocking collectives, on_device(): lax.all_to_all(flat_rows, 'fsdp', split_axis=1, concat_axis=0, tiled=True)  22.7 us
    all_gather x1, waiting for transfers between devices, on_device(): slope_group = lax.all_gather(slope, 'fsdp', axis=0, tiled=True)  20 us
  transfers between devices with their start and end apart: 4, of which 4 were waited for; matrix products, arithmetic and copies ran while one was open for 1% of the time, Pallas kernels for 0%

commit v1 on v0

v1 whole, which is shorter than its diff:
```python
import jax
import jax.numpy as jnp
from jax import lax
from jax.sharding import Mesh, PartitionSpec as P

epsilon = 1e-06
beta_scale = 0.05

AXES = ("yh", "zh", "zl", "yl", "x", "c")
REP = ("yh", "zh", "zl")
FSDP = ("yl", "x", "c")
GROUP = ("x", "c")


def exchange(pieces, axes):
    return lax.all_to_all(pieces, axes, 0, 0, tiled=False)


def spread(block, axes):
    count = lax.axis_size(axes)
    return exchange(jnp.broadcast_to(block[None], (count,) + block.shape), axes)


def on_device(
    hidden, norm_gain, quant_ref, scale_ref, weight_prm, readout, lengths, bounds, labels
):
    seq_len, width = hidden.shape[1:]
    features = readout.shape[2]
    head_size = features // scale_ref.shape[0]
    steps_count = bounds.shape[1]
    rows = quant_ref.shape[0]
    group = lax.axis_size(GROUP)
    f32, bf16 = jnp.float32, jnp.bfloat16
    expanded = jnp.repeat(scale_ref.T, head_size, axis=1)
    ref_local = (quant_ref.astype(f32) * expanded).astype(bf16)
    delta = (weight_prm.astype(f32) - ref_local.astype(f32)).astype(bf16)
    delta_other = lax.ppermute(delta, "yl", [(0, 1), (1, 0)])
    y_lo = lax.axis_index("yl")
    delta_pair = jnp.where(
        y_lo == 0,
        jnp.concatenate([delta, delta_other], axis=0),
        jnp.concatenate([delta_other, delta], axis=0),
    )
    position = jnp.arange(seq_len, dtype=jnp.int32)
    live = position < lengths[0]
    masked = jnp.where(live[:, None], readout[0], jnp.zeros((), bf16))
    masked_group = lax.all_gather(masked, GROUP).reshape(group * seq_len, features)
    wide = hidden[0].astype(f32)
    mean_square = jnp.mean(wide * wide, axis=-1, keepdims=True)
    normed = (wide * lax.rsqrt(mean_square + epsilon) * norm_gain).astype(bf16)
    pieces = normed.reshape(seq_len, 2, group, rows).transpose(2, 0, 1, 3)
    columns = exchange(pieces.reshape(group, seq_len, 2 * rows), GROUP)
    columns = columns.reshape(group * seq_len, 2 * rows)
    value = jnp.dot(columns, delta_pair, preferred_element_type=f32)
    partial = jnp.sum(value * masked_group.astype(f32), axis=-1).reshape(group, seq_len)
    me = lax.axis_index(GROUP)
    own = (jnp.arange(group) == me).astype(f32) * labels[0].astype(f32)
    tags = jnp.pad(own[None, :], ((0, 7), (0, seq_len - group)))
    small = jnp.concatenate([partial, tags], axis=0)
    small = jnp.sum(spread(small, GROUP), axis=0)
    margin = small[:group]
    label_group = small[group, :group]
    total = jnp.sum(beta_scale * margin, axis=1)
    weight_seq = beta_scale * (jax.nn.sigmoid(total) - label_group)
    reward = beta_scale * lax.dynamic_slice_in_dim(margin, me, 1, axis=0)
    step_index = jnp.sum((position[:, None] >= bounds[0][None, :]).astype(jnp.int32), axis=-1) - 1
    onehot = (step_index[:, None] == jnp.arange(steps_count)[None, :]).astype(f32)
    step_rewards = jnp.sum(reward[0][:, None] * onehot, axis=0)[None]
    slope = (
        weight_seq[:, None, None] * masked_group.reshape(group, seq_len, features).astype(f32)
    ).astype(bf16)
    grad = lax.dot_general(
        columns,
        slope.reshape(group * seq_len, features),
        (((0,), (0,)), ((), ())),
        preferred_element_type=f32,
    )
    yh, zl = lax.axis_size("yh"), lax.axis_size("zl")
    part = rows // (yh * zl)
    grad = grad.astype(bf16).reshape(2, yh, zl, part, features).transpose(1, 0, 2, 3, 4)
    grad = exchange(grad.reshape(2 * yh * zl, part, features), ("yh", "yl", "zl"))
    grad = jnp.sum(grad.astype(f32), axis=0).astype(bf16)
    grad = jnp.sum(spread(grad, ("zh",)).astype(f32), axis=0).astype(bf16)
    grad = spread(grad, ("yh", "zl"))
    return step_rewards, grad.reshape(rows, features).astype(f32)


def solution(mesh):
    fine = Mesh(mesh.devices.reshape(2, 4, 4, 2, 4, 2), AXES)
    every = REP + FSDP
    in_specs = (
        P(every, None, None),
        P(),
        P(FSDP, None),
        P(None, FSDP),
        P(FSDP, None),
        P(every, None, None),
        P(every),
        P(every, None),
        P(every),
    )
    out_specs = (P(every, None), P(FSDP, None))
    return jax.shard_map(
        on_device, mesh=fine, in_specs=in_specs, out_specs=out_specs, check_vma=False
    )
```

time: 469 us -> 139 us (0.30)
  the two profiles are of different devices: /device:TPU:38 before, /device:TPU:8 now
where the time goes in v1:
time: 139 us; the launch traced here: 138 us
  blocking collectives  59.7 us (43%)
  waiting for transfers between devices  27.1 us (19%)
  starting transfers between devices  17.2 us (12%)
  between operations  15.5 us (11%)
  local copies, waits for them, and re-layouts  8.01 us (6%)
  other arithmetic  5.99 us (4%)
  matrix products  4.87 us (4%)
    all_to_all x3, blocking collectives, exchange(): return lax.all_to_all(pieces, axes, 0, 0, tiled=False)  59.7 us
    all_to_all x2, waiting for transfers between devices, exchange(): return lax.all_to_all(pieces, axes, 0, 0, tiled=False)  21.7 us
    all_to_all x2, starting transfers between devices, exchange(): return lax.all_to_all(pieces, axes, 0, 0, tiled=False)  10.2 us
    ppermute x1, starting transfers between devices, on_device(): delta_other = lax.ppermute(delta, 'yl', [(0, 1), (1, 0)])  7 us
    all_gather x1, waiting for transfers between devices, on_device(): lax.all_gather(masked, GROUP).reshape(group * seq_len, features)  5.38 us
  transfers between devices with their start and end apart: 4, of which 3 were waited for; matrix products, arithmetic and copies ran while one was open for 7% of the time, Pallas kernels for 0%

profile of v1, /device:TPU:8, one launch (start us, length us, event | category | flops | bytes accessed | tf_op | source)
XLA Modules:
  0.0 138.4 jit_solution(8348785959757889303)
XLA Ops:
  7.2 0.0 all-gather.2.cloned.1.call-start
  7.9 1.6 %broadcast_select_fusion = bf16[1,128,512]{2,1,0:T(8,128)(2,1)} fusion(bf16[1,128,512]{2,1,0:T(8,128)(2,1)} %param.14, pred[128]{0:T(512)(128)(4,1)S(1)} %iota_compare_fusion.3), kind=kLoop, calls=%fused_computation.20 | loop fusion | flops 65536 | bytes 262272 | tf_op jit(solution)/shard_map/jit(_where)/select_n | solution.py:46
  9.5 0.0 all-gather.2.cloned.1.call-update
  9.5 0.8 mul.79
  10.3 1.8 %copy.26 = bf16[1,128,5120]{1,2,0:T(8,128)(2,1)S(1)} copy(bf16[1,128,5120]{2,1,0:T(8,128)(2,1)} %param.9) | data formatting | bytes 2621440 | tf_op args[0]
  12.1 0.7 multiply_reduce_fusion
  12.8 0.8 fusion.1
  13.6 1.2 copy.27
  14.8 0.0 copy-start.2
  14.8 0.0 copy-start
  14.8 0.0 copy-start.1
  14.8 4.4 %all-to-all-start = ((bf16[8,128,640]{1,2,0:T(8,128)(2,1)}), bf16[8,128,640]{1,2,0:T(8,128)(2,1)S(1)}, u32[]{:S(2)}, u32[]{:S(2)}) async-start(bf16[8,128,640]{1,2,0:T(8,128)(2,1)} %bitcast.3), calls=%async_computation | async-start | bytes 2621440 | tf_op jit(solution)/shard_map/all_to_all | solution.py:16
  19.2 0.0 copy-done.2
  19.2 0.1 copy.29
  19.4 0.4 broadcast_in_dim.22
  19.8 0.0 copy-done
  19.8 0.0 copy-done.1
  19.8 0.9 subtract_convert_fusion
  20.7 7.0 %collective-permute-start = (bf16[320,512]{1,0:T(8,128)(2,1)}, bf16[320,512]{1,0:T(8,128)(2,1)}, u32[]{:S(2)}, u32[]{:S(2)}) collective-permute-start(bf16[320,512]{1,0:T(8,128)(2,1)} %subtract_convert_fusion), channel_id=1, source_target_pairs={{0,8},{8,0},{1,9},{9,1},{2,10},{10,2},{3,11},{11,3},{4,12},{12,4},... | collective-permute-start | bytes 983048 | tf_op jit(solution)/shard_map/ppermute | solution.py:37
  28.4 11.8 %all-to-all-done = bf16[8,128,640]{1,2,0:T(8,128)(2,1)S(1)} async-done(((bf16[8,128,640]{1,2,0:T(8,128)(2,1)}), bf16[8,128,640]{1,2,0:T(8,128)(2,1)S(1)}, u32[]{:S(2)}, u32[]{:S(2)}) %all-to-all-start) | async-done | bytes 1310752 | tf_op jit(solution)/shard_map/all_to_all | solution.py:16
  40.2 1.5 %copy.28 = bf16[8,128,640]{2,1,0:T(8,128)(2,1)} copy(bf16[8,128,640]{1,2,0:T(8,128)(2,1)S(1)} %all-to-all-done) | data formatting | bytes 2621440 | tf_op jit(solution)/shard_map/all_to_all | solution.py:16
  41.6 5.4 %all-gather.2.cloned.1.call-done = bf16[8,128,512]{2,1,0:T(8,128)(2,1)} async-done(((bf16[1,128,512]{2,1,0:T(8,128)(2,1)}), bf16[8,128,512]{2,1,0:T(8,128)(2,1)}) %all-gather.2.cloned.1.call-update) | async-done | bytes 1048592 | tf_op jit(solution)/shard_map/all_gather | solution.py:47
  47.0 1.5 %copy.32 = f32[1024,512]{0,1:T(8,128)S(1)} copy(bf16[1024,512]{1,0:T(8,128)(2,1)} %bitcast.47) | data formatting | bytes 3145728 | tf_op jit(solution)/shard_map/convert_element_type | solution.py:55
  48.5 0.0 collective-permute-done
  48.5 2.7 %multiply_reduce_fusion.1 = f32[1024]{0:T(1024)S(1)} fusion(f32[1024,512]{0,1:T(8,128)S(1)} %copy.32, bf16[1024,640]{1,0:T(8,128)(2,1)} %bitcast.46, bf16[320,512]{1,0:T(8,128)(2,1)} %collective-permute-done, bf16[320,512]{1,0:T(8,128)(2,1)} %subtract_convert_fusion, pred[]{:T(512)S(6)} %eq.32), kind=kOutput, calls=%fused_computation.3 | convolution fusion | flops 675085312 | bytes 4067329 | tf_op jit(solution)/shard_map/dot_general | solution.py:54
  51.3 8.8 %all_to_all.25 = f32[8,16,128]{2,1,0:T(8,128)S(1)} all-to-all(f32[8,16,128]{2,1,0:T(8,128)S(1)} %broadcast_in_dim.25), channel_id=1, replica_groups=mesh['yh'=2,'zh'=4,'zl'=4,'yl'=2,'x'=4,'c'=2] {'x','c'}, dimensions={0} | all-to-all | bytes 131072 | tf_op jit(solution)/shard_map/all_to_all | solution.py:16
  60.1 0.1 multiply_reduce_fusion.2
  60.2 2.2 %fusion = bf16[640,512]{1,0:T(8,128)(2,1)S(1)} fusion(bf16[8,128,640]{1,2,0:T(8,128)(2,1)S(1)} %all-to-all-done, f32[8]{0:T(128)S(1)} %fusion.11, bf16[8,128,512]{2,1,0:T(8,128)(2,1)} %all-gather.2.cloned.1.call-done), kind=kOutput, calls=%fused_computation.5 | convolution fusion | flops 672989184 | bytes 3014688 | tf_op jit(solution)/shard_map/dot_general | solution.py:72
  62.5 25.1 %all_to_all.26 = bf16[16,40,512]{2,1,0:T(8,128)(2,1)S(1)} all-to-all(bf16[16,40,512]{2,1,0:T(8,128)(2,1)S(1)} %bitcast.45), channel_id=1, replica_groups=mesh['yh'=2,'zh'=4,'zl'=4,'yl'=2,'x'=4,'c'=2] {'yh','yl','zl'}, dimensions={0} | all-to-all | bytes 1310720 | tf_op jit(solution)/shard_map/all_to_all | solution.py:16
  87.6 0.0 copy-start.3
  87.6 0.1 reduce_sum.84
  87.7 25.7 %all_to_all.27 = bf16[4,40,512]{2,1,0:T(8,128)(2,1)S(1)} all-to-all(bf16[4,40,512]{2,1,0:T(8,128)(2,1)S(1)} %broadcast_in_dim.27), channel_id=1, replica_groups=mesh['yh'=2,'zh'=4,'zl'=4,'yl'=2,'x'=4,'c'=2] {'zh'}, dimensions={0} | all-to-all | bytes 327680 | tf_op jit(solution)/shard_map/all_to_all | solution.py:16
  113.5 0.7 broadcast_in_dim.28
  114.2 5.8 %all-to-all-start.4 = ((bf16[8,40,512]{2,1,0:T(8,128)(2,1)}), bf16[8,40,512]{2,1,0:T(8,128)(2,1)S(1)}, u32[]{:S(2)}, u32[]{:S(2)}) async-start(bf16[8,40,512]{2,1,0:T(8,128)(2,1)} %broadcast_in_dim.28), calls=%async_computation.4 | async-start | bytes 655360 | tf_op jit(solution)/shard_map/all_to_all | solution.py:16
  120.0 0.0 copy-done.3
  120.0 0.1 convert_reduce_fusion
  120.1 0.6 select_reduce_fusion
  120.7 9.9 %all-to-all-done.4 = bf16[8,40,512]{2,1,0:T(8,128)(2,1)S(1)} async-done(((bf16[8,40,512]{2,1,0:T(8,128)(2,1)}), bf16[8,40,512]{2,1,0:T(8,128)(2,1)S(1)}, u32[]{:S(2)}, u32[]{:S(2)}) %all-to-all-start.4) | async-done | bytes 327712 | tf_op jit(solution)/shard_map/all_to_all | solution.py:16
  130.6 0.9 bitcast_convert_fusion
  (12 shorter events, 0.2 us)
Async XLA Ops:
  7.2 39.9 %all-gather.2.cloned.1.call-start = ((), (), s32[]{:S(2)}) async-start(), calls=%async_computation.5 | async-start | bytes 1179648 | tf_op jit(solution)/shard_map/all_gather | solution.py:47
  14.8 4.4 %copy-start.2 = (f32[4,320]{1,0:T(4,128)S(1)}, f32[4,320]{1,0:T(4,128)}, u32[]{:S(2)}) copy-start(f32[4,320]{1,0:T(4,128)} %param.12) | copy-start | bytes 15364
  14.8 5.0 %copy-start = (bf16[320,512]{1,0:T(8,128)(2,1)S(1)}, bf16[320,512]{1,0:T(8,128)(2,1)}, u32[]{:S(2)}) copy-start(bf16[320,512]{1,0:T(8,128)(2,1)} %param.13) | copy-start | bytes 983044
  14.8 5.0 %copy-start.1 = (bf16[320,512]{1,0:T(8,128)(2,1)S(1)}, bf16[320,512]{1,0:T(8,128)(2,1)}, u32[]{:S(2)}) copy-start(bf16[320,512]{1,0:T(8,128)(2,1)} %param.11) | copy-start | bytes 983044
  14.8 25.4 %all-to-all-start = ((bf16[8,128,640]{1,2,0:T(8,128)(2,1)}), bf16[8,128,640]{1,2,0:T(8,128)(2,1)S(1)}, u32[]{:S(2)}, u32[]{:S(2)}) async-start(bf16[8,128,640]{1,2,0:T(8,128)(2,1)} %bitcast.3), calls=%async_computation | async-start | bytes 2621440 | tf_op jit(solution)/shard_map/all_to_all | solution.py:16
  20.7 27.8 %collective-permute-start = (bf16[320,512]{1,0:T(8,128)(2,1)}, bf16[320,512]{1,0:T(8,128)(2,1)}, u32[]{:S(2)}, u32[]{:S(2)}) collective-permute-start(bf16[320,512]{1,0:T(8,128)(2,1)} %subtract_convert_fusion), channel_id=1, source_target_pairs={{0,8},{8,0},{1,9},{9,1},{2,10},{10,2},{3,11},{11,3},{4,12},{12,4},... | collective-permute-start | bytes 983048 | tf_op jit(solution)/shard_map/ppermute | solution.py:37
  87.6 32.4 %copy-start.3 = (s32[1,8]{1,0:T(1,128)S(1)}, s32[1,8]{1,0:T(1,128)}, u32[]{:S(2)}) copy-start(s32[1,8]{1,0:T(1,128)} %param.16) | copy-start | bytes 100
  114.2 16.4 %all-to-all-start.4 = ((bf16[8,40,512]{2,1,0:T(8,128)(2,1)}), bf16[8,40,512]{2,1,0:T(8,128)(2,1)S(1)}, u32[]{:S(2)}, u32[]{:S(2)}) async-start(bf16[8,40,512]{2,1,0:T(8,128)(2,1)} %broadcast_in_dim.28), calls=%async_computation.4 | async-start | bytes 655360 | tf_op jit(solution)/shard_map/all_to_all | solution.py:16
Sparse Core Ops, SparseCore 0:
  10.1 36.8 all-gather.1

commit v2 on v1

v2 whole, which is shorter than its diff:
```python
import jax
import jax.numpy as jnp
from jax import lax
from jax.experimental import pallas as pl
from jax.experimental.pallas import tpu as pltpu
from jax.sharding import Mesh, PartitionSpec as P

epsilon = 1e-06
beta_scale = 0.05

AXES = ("yh", "zh", "zl", "yl", "x", "c")
REP = ("yh", "zh", "zl")
FSDP = ("yl", "x", "c")
GROUP = ("x", "c")
VMEM_LIMIT = 24 * 1024 * 1024
VMEM = pl.BlockSpec(memory_space=pltpu.VMEM)
SMEM = pl.BlockSpec(memory_space=pltpu.SMEM)
f32, bf16 = jnp.float32, jnp.bfloat16


def exchange(pieces, axes):
    return lax.all_to_all(pieces, axes, 0, 0, tiled=False)


def spread(block, axes):
    count = lax.axis_size(axes)
    return exchange(jnp.broadcast_to(block[None], (count,) + block.shape), axes)


def wide_sum(parts):
    total = parts[0].astype(f32)
    for k in range(1, parts.shape[0]):
        total = total + parts[k].astype(f32)
    return total


def mask_kernel(lengths_ref, readout_ref, out_ref):
    position = lax.broadcasted_iota(jnp.int32, readout_ref.shape, 0)
    read = readout_ref[...].astype(f32)
    masked = jnp.where(position < lengths_ref[0], read, 0.0).astype(bf16)
    for k in range(out_ref.shape[0]):
        out_ref[k] = masked


def mask_call(lengths, readout, copies):
    return pl.pallas_call(
        mask_kernel,
        in_specs=[SMEM, VMEM],
        out_specs=VMEM,
        out_shape=jax.ShapeDtypeStruct((copies,) + readout.shape, bf16),
        compiler_params=pltpu.CompilerParams(vmem_limit_bytes=60 * 1024 * 1024),
    )(lengths, readout)


def norm_kernel(hidden_ref, gain_ref, pieces_ref):
    width = hidden_ref.shape[1]
    groups, _, two_rows = pieces_ref.shape
    rows = two_rows // 2
    wide = hidden_ref[...].astype(f32)
    mean_square = jnp.sum(wide * wide, axis=-1, keepdims=True) * (1.0 / width)
    scale = lax.rsqrt(mean_square + epsilon)
    normed = (wide * scale * gain_ref[...]).astype(bf16)
    for g in range(groups):
        low = normed[:, rows * g : rows * (g + 1)]
        high = normed[:, rows * (groups + g) : rows * (groups + g + 1)]
        pieces_ref[g] = jnp.concatenate([low, high], axis=1)


def norm_call(hidden, gain, groups):
    seq_len, width = hidden.shape
    share = width // groups
    block = 32
    return pl.pallas_call(
        norm_kernel,
        grid=(seq_len // block,),
        in_specs=[
            pl.BlockSpec((block, width), lambda i: (i, 0)),
            pl.BlockSpec((1, width), lambda i: (0, 0)),
        ],
        out_specs=pl.BlockSpec((groups, block, share), lambda i: (0, i, 0)),
        out_shape=jax.ShapeDtypeStruct((groups, seq_len, share), bf16),
        cost_estimate=pl.CostEstimate(
            flops=6 * seq_len * width, bytes_accessed=8 * seq_len * width, transcendentals=0
        ),
        compiler_params=pltpu.CompilerParams(vmem_limit_bytes=VMEM_LIMIT),
    )(hidden, gain)


def place_kernel(pieces_ref, out_ref):
    for k in range(pieces_ref.shape[0]):
        out_ref[:, 128 * k : 128 * (k + 1)] = pieces_ref[k].astype(f32)


def place_call(pieces, halves):
    count, part, lanes = pieces.shape
    across = count // halves
    return pl.pallas_call(
        place_kernel,
        grid=(halves,),
        in_specs=[pl.BlockSpec((across, part, lanes), lambda i: (i, 0, 0))],
        out_specs=pl.BlockSpec((part, across * lanes), lambda i: (i, 0)),
        out_shape=jax.ShapeDtypeStruct((halves * part, across * lanes), f32),
        compiler_params=pltpu.CompilerParams(vmem_limit_bytes=VMEM_LIMIT),
    )(pieces)


def seq_of(place_ref, j, swapped):
    core = place_ref[1]
    return 2 * j + (1 - core if swapped else core)


def margin_kernel(place_ref, tags_ref, columns_ref, own_ref, other_ref, near_ref, far_ref, out_ref):
    core, y_lo = place_ref[1], place_ref[2]
    me = 2 * place_ref[0] + core
    own, other = own_ref[...], other_ref[...]
    first = y_lo == 0
    delta = jnp.concatenate([jnp.where(first, own, other), jnp.where(first, other, own)], axis=0)
    groups, seq_len, _ = columns_ref.shape
    row = lax.broadcasted_iota(jnp.int32, (groups, seq_len), 0)
    acc = jnp.zeros((groups, seq_len), f32)
    for swapped, read_ref in ((False, near_ref), (True, far_ref)):
        for j in range(4):
            seq = seq_of(place_ref, j, swapped)
            value = jnp.dot(columns_ref[seq], delta, preferred_element_type=f32)
            prod = value * read_ref[j].astype(f32)
            lanes = prod.shape[1] // 128
            part = prod[:, :128]
            for k in range(1, lanes):
                part = part + prod[:, 128 * k : 128 * (k + 1)]
            line = jnp.sum(part.T, axis=0, keepdims=True)
            acc = jnp.where(row == seq, line, acc)
    label = tags_ref[0].astype(f32)
    tags = jnp.where(row == me, label, 0.0)
    for g in range(out_ref.shape[0]):
        out_ref[g, :groups, :] = acc
        out_ref[g, groups:, :] = tags


def margin_call(place, labels, columns, delta, delta_other, near, far):
    groups, seq_len, _ = columns.shape
    return pl.pallas_call(
        margin_kernel,
        in_specs=[SMEM, SMEM] + [VMEM] * 5,
        out_specs=VMEM,
        out_shape=jax.ShapeDtypeStruct((groups, 2 * groups, seq_len), f32),
        compiler_params=pltpu.CompilerParams(vmem_limit_bytes=VMEM_LIMIT),
    )(place, labels, columns, delta, delta_other, near, far)


def grad_kernel(place_ref, small_ref, columns_ref, near_ref, far_ref, grad_ref, margin_ref, slope_ref):
    groups, seq_len, depth = columns_ref.shape
    features = near_ref.shape[2]
    small = small_ref[0]
    for g in range(1, groups):
        small = small + small_ref[g]
    margin = small[:groups]
    margin_ref[...] = margin
    label = small[groups:, :1]
    total = jnp.sum(beta_scale * margin, axis=1, keepdims=True)
    weight = beta_scale * (1.0 / (1.0 + jnp.exp(-total)) - label)
    row = lax.broadcasted_iota(jnp.int32, weight.shape, 0)
    for swapped, read_ref in ((False, near_ref), (True, far_ref)):
        for j in range(4):
            seq = seq_of(place_ref, j, swapped)
            w = jnp.sum(jnp.where(row == seq, weight, 0.0), axis=0, keepdims=True)
            slope_ref[seq] = (w * read_ref[j].astype(f32)).astype(bf16)
    columns = columns_ref[...].reshape(groups * seq_len, depth)
    slope = slope_ref[...].reshape(groups * seq_len, features)
    grad = lax.dot_general(
        columns, slope, (((0,), (0,)), ((), ())), preferred_element_type=f32
    ).astype(bf16)
    y_hi, y_all = 2, 4
    part = depth // y_all
    for yh in range(y_hi):
        for yl in range(y_all // y_hi):
            at = (yl * y_hi + yh) * part
            grad_ref[yh * (y_all // y_hi) + yl] = grad[at : at + part]


def grad_call(place, small, columns, near, far):
    groups, seq_len, depth = columns.shape
    features = near.shape[2]
    return pl.pallas_call(
        grad_kernel,
        in_specs=[SMEM] + [VMEM] * 4,
        out_specs=[VMEM, VMEM],
        out_shape=[
            jax.ShapeDtypeStruct((4, depth // 4, features), bf16),
            jax.ShapeDtypeStruct((groups, seq_len), f32),
        ],
        scratch_shapes=[pltpu.VMEM((groups, seq_len, features), bf16)],
        compiler_params=pltpu.CompilerParams(vmem_limit_bytes=VMEM_LIMIT),
    )(place, small, columns, near, far)


def on_device(
    hidden, norm_gain, quant_ref, scale_ref, weight_prm, readout, lengths, bounds, labels
):
    seq_len, width = hidden.shape[1:]
    features = readout.shape[2]
    head_size = features // scale_ref.shape[0]
    steps_count = bounds.shape[1]
    group = lax.axis_size(GROUP)
    x, core, y_lo = lax.axis_index("x"), lax.axis_index("c"), lax.axis_index("yl")
    place = jnp.stack([x, core, y_lo]).astype(jnp.int32)
    pieces = norm_call(hidden[0], norm_gain[None], group)
    near = exchange(mask_call(lengths, readout[0], lax.axis_size("x")), ("x",))
    far = lax.ppermute(near, "c", [(0, 1), (1, 0)])
    columns = exchange(pieces, GROUP)
    expanded = jnp.repeat(scale_ref.T, head_size, axis=1)
    ref_local = (quant_ref.astype(f32) * expanded).astype(bf16)
    delta = (weight_prm.astype(f32) - ref_local.astype(f32)).astype(bf16)
    delta_other = lax.ppermute(delta, "yl", [(0, 1), (1, 0)])
    small = exchange(margin_call(place, labels, columns, delta, delta_other, near, far), GROUP)
    grad, margin = grad_call(place, small, columns, near, far)
    grad = wide_sum(exchange(grad, ("yh", "yl"))).astype(bf16)
    zl = lax.axis_size("zl")
    grad = grad.reshape(grad.shape[0], zl, features // zl).transpose(1, 0, 2)
    grad = wide_sum(exchange(grad, ("zl",))).astype(bf16)
    grad = wide_sum(spread(grad, ("zh",))).astype(bf16)
    grad = place_call(spread(grad, ("yh", "zl")), lax.axis_size("yh"))
    position = jnp.arange(seq_len, dtype=jnp.int32)
    reward = beta_scale * lax.dynamic_slice_in_dim(margin, 2 * x + core, 1, axis=0)
    step_index = jnp.sum((position[:, None] >= bounds[0][None, :]).astype(jnp.int32), axis=-1) - 1
    onehot = (step_index[:, None] == jnp.arange(steps_count)[None, :]).astype(f32)
    step_rewards = jnp.sum(reward[0][:, None] * onehot, axis=0)[None]
    return step_rewards, grad


def solution(mesh):
    fine = Mesh(mesh.devices.reshape(2, 4, 4, 2, 4, 2), AXES)
    every = REP + FSDP
    in_specs = (
        P(every, None, None),
        P(),
        P(FSDP, None),
        P(None, FSDP),
        P(FSDP, None),
        P(every, None, None),
        P(every),
        P(every, None),
        P(every),
    )
    out_specs = (P(every, None), P(FSDP, None))
    return jax.shard_map(
        on_device, mesh=fine, in_specs=in_specs, out_specs=out_specs, check_vma=False
    )
```

time: 139 us -> 121 us (0.87)
  between operations: 15.5 us -> 2.17 us
  Pallas kernels: 0 us -> 8.47 us
  local copies, waits for them, and re-layouts: 8.01 us -> 1.42 us
  other arithmetic: 5.99 us -> 1.09 us
  matrix products: 4.87 us -> 0 us
  starting transfers between devices: 17.2 us -> 20.6 us
    pallas_call x0 -> x5, Pallas kernels: none -> 8.47 us  [the longest x1 2.4 us: norm_call(): pl.pallas_call(norm_kernel, grid=(seq_len // block,), in_specs=[pl.BlockS...]
    ppermute x1, waiting for transfers between devices: 0.01 us -> 7.24 us  [on_device(): delta_other = lax.ppermute(delta, 'yl', [(0, 1), (1, 0)])]
    all_gather x1 -> x0, waiting for transfers between devices: 5.38 us -> none  [on_device(): lax.all_gather(masked, GROUP).reshape(group * seq_len, features)]
    dot_general x2 -> x0, matrix products: 4.87 us -> none  [the longest x1 2.7 us: on_device(): value = jnp.dot(columns, delta_pair, preferred_element_type=f32)]
    all_to_all x2 -> x3, starting transfers between devices: 10.2 us -> 12.8 us  [exchange(): return lax.all_to_all(pieces, axes, 0, 0, tiled=False)]
    all_to_all x2 -> x3, waiting for transfers between devices: 21.7 us -> 19.1 us  [exchange(): return lax.all_to_all(pieces, axes, 0, 0, tiled=False)]
    ppermute x0 -> x1, starting transfers between devices: none -> 2.3 us  [on_device(): far = lax.ppermute(near, 'c', [(0, 1), (1, 0)])]
    unnamed x9 -> x12, local copies, waits for them, and re-layouts: 1.77 us -> 0.03 us
  transfers between devices with their start and end apart: 4 -> 5, of which waited for: 3 -> 4; matrix products, arithmetic and copies ran while one was open for 7% -> 1% of each run, Pallas kernels for 0% -> 2%
where the time goes in v2:
time: 121 us; the launch traced here: 120 us
  blocking collectives  60.1 us (50%)
  waiting for transfers between devices  26.4 us (22%)
  starting transfers between devices  20.6 us (17%)
  Pallas kernels  8.47 us (7%)
  between operations  2.17 us (2%)
  local copies, waits for them, and re-layouts  1.42 us (1%)
    all_to_all x4, blocking collectives, exchange(): return lax.all_to_all(pieces, axes, 0, 0, tiled=False)  60.1 us
    all_to_all x3, waiting for transfers between devices, exchange(): return lax.all_to_all(pieces, axes, 0, 0, tiled=False)  19.1 us
    all_to_all x3, starting transfers between devices, exchange(): return lax.all_to_all(pieces, axes, 0, 0, tiled=False)  12.8 us
    ppermute x1, waiting for transfers between devices, on_device(): delta_other = lax.ppermute(delta, 'yl', [(0, 1), (1, 0)])  7.24 us
    ppermute x1, starting transfers between devices, on_device(): delta_other = lax.ppermute(delta, 'yl', [(0, 1), (1, 0)])  5.49 us
  transfers between devices with their start and end apart: 5, of which 4 were waited for; matrix products, arithmetic and copies ran while one was open for 1% of the time, Pallas kernels for 2%

profile of v2, /device:TPU:8, one launch (start us, length us, event | category | flops | bytes accessed | tf_op | source)
XLA Modules:
  0.0 120.2 jit_solution(2478170098480790613)
XLA Ops:
  0.6 0.0 copy-start
  0.6 0.0 copy-start.1
  1.4 1.7 %shard_map.105 = bf16[4,128,512]{2,1,0:T(8,128)(2,1)} custom-call(s32[1]{0:T(128)S(6)} %copy.22.lengths_ref, bf16[128,512]{1,0:T(8,128)(2,1)} %bitcast.29), custom_call_target="tpu_custom_call" | custom-call | tf_op jit(solution)/shard_map/pallas_call | solution.py:46
  3.1 4.3 %all-to-all-start.1 = ((bf16[4,128,512]{2,1,0:T(8,128)(2,1)}), bf16[4,128,512]{2,1,0:T(8,128)(2,1)S(1)}, u32[]{:S(2)}, u32[]{:S(2)}) async-start(bf16[4,128,512]{2,1,0:T(8,128)(2,1)} %shard_map.105), calls=%async_computation.1 | async-start | bytes 1048576 | tf_op jit(solution)/shard_map/all_to_all | solution.py:22
  7.4 0.0 copy-done
  7.4 0.0 copy-done.1
  7.4 2.4 %shard_map.104 = bf16[8,128,640]{2,1,0:T(8,128)(2,1)} custom-call(bf16[128,5120]{1,0:T(8,128)(2,1)S(1)} %bitcast.25, f32[1,5120]{1,0:T(1,128)S(1)} %bitcast.26), custom_call_target="tpu_custom_call" | custom-call | flops 3932160 | bytes 5242880 | tf_op jit(solution)/shard_map/pallas_call | solution.py:73
  9.8 0.0 copy-start.4
  9.8 0.0 copy-start.2
  9.8 0.0 copy-start.3
  9.8 7.1 %all-to-all-done.1.near_ref = bf16[4,128,512]{2,1,0:T(8,128)(2,1)S(1)} async-done(((bf16[4,128,512]{2,1,0:T(8,128)(2,1)}), bf16[4,128,512]{2,1,0:T(8,128)(2,1)S(1)}, u32[]{:S(2)}, u32[]{:S(2)}) %all-to-all-start.1) | async-done | bytes 524320 | tf_op jit(solution)/shard_map/all_to_all | solution.py:22
  16.9 3.6 %all-to-all-start = ((bf16[8,128,640]{2,1,0:T(8,128)(2,1)}), bf16[8,128,640]{2,1,0:T(8,128)(2,1)S(1)}, u32[]{:S(2)}, u32[]{:S(2)}) async-start(bf16[8,128,640]{2,1,0:T(8,128)(2,1)} %shard_map.104), calls=%async_computation | async-start | bytes 2621440 | tf_op jit(solution)/shard_map/all_to_all | solution.py:22
  20.5 0.0 copy-done.4
  20.5 0.1 copy.14
  20.6 2.3 %collective-permute-start.1 = (bf16[4,128,512]{2,1,0:T(8,128)(2,1)S(1)}, bf16[4,128,512]{2,1,0:T(8,128)(2,1)S(1)}, u32[]{:S(2)}, u32[]{:S(2)}) collective-permute-start(bf16[4,128,512]{2,1,0:T(8,128)(2,1)S(1)} %all-to-all-done.1.near_ref), channel_id=1, source_target_pairs={{0,1},{1,0},{2,3},{3,2},{4,5},{5,4},{6,7},{7,6},{8,9},{9,8},{10,11... | collective-permute-start | bytes 1572872 | tf_op jit(solution)/shard_map/ppermute | solution.py:208
  22.9 0.4 broadcast_in_dim.29
  23.3 0.0 copy-done.2
  23.4 0.0 copy-done.3
  23.4 0.2 subtract_convert_fusion.own_ref
  23.5 5.5 %collective-permute-start = (bf16[320,512]{1,0:T(8,128)(2,1)S(1)}, bf16[320,512]{1,0:T(8,128)(2,1)S(1)}, u32[]{:S(2)}, u32[]{:S(2)}) collective-permute-start(bf16[320,512]{1,0:T(8,128)(2,1)S(1)} %subtract_convert_fusion.own_ref), channel_id=1, source_target_pairs={{0,8},{8,0},{1,9},{9,1},{2,10},{10,2},{3,11},{11,3},{4,12},{12,4},... | collective-permute-start | bytes 983048 | tf_op jit(solution)/shard_map/ppermute | solution.py:213
  29.7 0.1 pad_add_fusion.place_ref
  29.8 7.2 %collective-permute-done.other_ref = bf16[320,512]{1,0:T(8,128)(2,1)S(1)} collective-permute-done((bf16[320,512]{1,0:T(8,128)(2,1)S(1)}, bf16[320,512]{1,0:T(8,128)(2,1)S(1)}, u32[]{:S(2)}, u32[]{:S(2)}) %collective-permute-start) | collective-permute-done | bytes 327712 | tf_op jit(solution)/shard_map/ppermute | solution.py:213
  37.0 0.0 collective-permute-done.1.far_ref
  37.0 2.2 %all-to-all-done.columns_ref = bf16[8,128,640]{2,1,0:T(8,128)(2,1)S(1)} async-done(((bf16[8,128,640]{2,1,0:T(8,128)(2,1)}), bf16[8,128,640]{2,1,0:T(8,128)(2,1)S(1)}, u32[]{:S(2)}, u32[]{:S(2)}) %all-to-all-start) | async-done | bytes 1310752 | tf_op jit(solution)/shard_map/all_to_all | solution.py:22
  39.2 1.6 %shard_map.106 = f32[8,16,128]{2,1,0:T(8,128)S(1)} custom-call(s32[3]{0:T(128)S(1)} %pad_add_fusion.place_ref, s32[1]{0:T(128)S(6)} %copy.23.tags_ref, bf16[8,128,640]{2,1,0:T(8,128)(2,1)S(1)} %all-to-all-done.columns_ref, bf16[320,512]{1,0:T(8,128)(2,1)S(1)} %subtract_convert_fusion.own_ref, bf16[320,512]{1,0:T(8,128)(2,1)S(1)} %collective-permute-done.other_ref, ...), custom_call_target="tpu_custom_call" | custom-call | tf_op jit(solution)/shard_map/pallas_call | solution.py:141
  40.8 8.0 %all_to_all.35.small_ref = f32[8,16,128]{2,1,0:T(8,128)S(1)} all-to-all(f32[8,16,128]{2,1,0:T(8,128)S(1)} %shard_map.106), channel_id=1, replica_groups=mesh['yh'=2,'zh'=4,'zl'=4,'yl'=2,'x'=4,'c'=2] {'x','c'}, dimensions={0} | all-to-all | bytes 131072 | tf_op jit(solution)/shard_map/all_to_all | solution.py:22
  48.8 1.8 %shard_map.107 = (bf16[4,160,512]{2,1,0:T(8,128)(2,1)S(1)}, f32[8,128]{1,0:T(8,128)S(1)}) custom-call(s32[3]{0:T(128)S(1)} %pad_add_fusion.place_ref, f32[8,16,128]{2,1,0:T(8,128)S(1)} %all_to_all.35.small_ref, bf16[8,128,640]{2,1,0:T(8,128)(2,1)S(1)} %all-to-all-done.columns_ref, bf16[4,128,512]{2,1,0:T(8,128)(2,1)S(1)} %all-to-all-done.1.near_ref, ...), custom_call_target="tpu_custom_call" | custom-call | tf_op jit(solution)/shard_map/pallas_call | solution.py:183
  50.6 15.6 %all_to_all.36 = bf16[4,160,512]{2,1,0:T(8,128)(2,1)S(1)} all-to-all(bf16[4,160,512]{2,1,0:T(8,128)(2,1)S(1)} %get-tuple-element.5), channel_id=1, replica_groups=mesh['yh'=2,'zh'=4,'zl'=4,'yl'=2,'x'=4,'c'=2] {'yh','yl'}, dimensions={0} | all-to-all | bytes 1310720 | tf_op jit(solution)/shard_map/all_to_all | solution.py:22
  66.2 0.1 add_convert_fusion
  66.4 0.0 copy-start.5
  66.4 10.9 %all_to_all.37 = bf16[4,160,128]{2,1,0:T(8,128)(2,1)S(1)} all-to-all(bf16[4,160,128]{2,1,0:T(8,128)(2,1)S(1)} %bitcast.28), channel_id=1, replica_groups=mesh['yh'=2,'zh'=4,'zl'=4,'yl'=2,'x'=4,'c'=2] {'zl'}, dimensions={0} | all-to-all | bytes 327680 | tf_op jit(solution)/shard_map/all_to_all | solution.py:22
  77.3 25.7 %all_to_all.38 = bf16[4,160,128]{2,1,0:T(8,128)(2,1)S(1)} all-to-all(bf16[4,160,128]{2,1,0:T(8,128)(2,1)S(1)} %broadcast_in_dim.32), channel_id=1, replica_groups=mesh['yh'=2,'zh'=4,'zl'=4,'yl'=2,'x'=4,'c'=2] {'zh'}, dimensions={0} | all-to-all | bytes 327680 | tf_op jit(solution)/shard_map/all_to_all | solution.py:22
  103.0 0.8 broadcast_in_dim.34
  103.8 5.0 %all-to-all-start.6 = ((bf16[8,160,128]{2,1,0:T(8,128)(2,1)}), bf16[8,160,128]{2,1,0:T(8,128)(2,1)S(1)}, u32[]{:S(2)}, u32[]{:S(2)}) async-start(bf16[8,160,128]{2,1,0:T(8,128)(2,1)} %broadcast_in_dim.34), calls=%async_computation.6 | async-start | bytes 655360 | tf_op jit(solution)/shard_map/all_to_all | solution.py:22
  108.8 0.0 copy-done.5
  108.8 0.1 convert_reduce_fusion
  108.9 0.6 select_reduce_fusion
  109.5 9.9 %all-to-all-done.6.pieces_ref = bf16[8,160,128]{2,1,0:T(8,128)(2,1)S(1)} async-done(((bf16[8,160,128]{2,1,0:T(8,128)(2,1)}), bf16[8,160,128]{2,1,0:T(8,128)(2,1)S(1)}, u32[]{:S(2)}, u32[]{:S(2)}) %all-to-all-start.6) | async-done | bytes 327712 | tf_op jit(solution)/shard_map/all_to_all | solution.py:22
  119.4 0.9 shard_map.108
  (7 shorter events, 0.2 us)
Async XLA Ops:
  0.6 6.8 %copy-start = (bf16[1,128,5120]{2,1,0:T(8,128)(2,1)S(1)}, bf16[1,128,5120]{2,1,0:T(8,128)(2,1)}, u32[]{:S(2)}) copy-start(bf16[1,128,5120]{2,1,0:T(8,128)(2,1)} %param.9) | copy-start | bytes 3932164
  0.6 6.8 %copy-start.1 = (f32[5120]{0:T(1024)S(1)}, f32[5120]{0:T(1024)}, u32[]{:S(2)}) copy-start(f32[5120]{0:T(1024)} %param.10) | copy-start | bytes 61444
  3.1 13.8 %all-to-all-start.1 = ((bf16[4,128,512]{2,1,0:T(8,128)(2,1)}), bf16[4,128,512]{2,1,0:T(8,128)(2,1)S(1)}, u32[]{:S(2)}, u32[]{:S(2)}) async-start(bf16[4,128,512]{2,1,0:T(8,128)(2,1)} %shard_map.105), calls=%async_computation.1 | async-start | bytes 1048576 | tf_op jit(solution)/shard_map/all_to_all | solution.py:22
  9.8 10.7 %copy-start.4 = (f32[4,320]{1,0:T(4,128)S(1)}, f32[4,320]{1,0:T(4,128)}, u32[]{:S(2)}) copy-start(f32[4,320]{1,0:T(4,128)} %param.12) | copy-start | bytes 15364
  9.8 13.5 %copy-start.2 = (bf16[320,512]{1,0:T(8,128)(2,1)S(1)}, bf16[320,512]{1,0:T(8,128)(2,1)}, u32[]{:S(2)}) copy-start(bf16[320,512]{1,0:T(8,128)(2,1)} %param.13) | copy-start | bytes 983044
  9.8 13.5 %copy-start.3 = (bf16[320,512]{1,0:T(8,128)(2,1)S(1)}, bf16[320,512]{1,0:T(8,128)(2,1)}, u32[]{:S(2)}) copy-start(bf16[320,512]{1,0:T(8,128)(2,1)} %param.11) | copy-start | bytes 983044
  16.9 22.3 %all-to-all-start = ((bf16[8,128,640]{2,1,0:T(8,128)(2,1)}), bf16[8,128,640]{2,1,0:T(8,128)(2,1)S(1)}, u32[]{:S(2)}, u32[]{:S(2)}) async-start(bf16[8,128,640]{2,1,0:T(8,128)(2,1)} %shard_map.104), calls=%async_computation | async-start | bytes 2621440 | tf_op jit(solution)/shard_map/all_to_all | solution.py:22
  20.6 16.4 %collective-permute-start.1 = (bf16[4,128,512]{2,1,0:T(8,128)(2,1)S(1)}, bf16[4,128,512]{2,1,0:T(8,128)(2,1)S(1)}, u32[]{:S(2)}, u32[]{:S(2)}) collective-permute-start(bf16[4,128,512]{2,1,0:T(8,128)(2,1)S(1)} %all-to-all-done.1.near_ref), channel_id=1, source_target_pairs={{0,1},{1,0},{2,3},{3,2},{4,5},{5,4},{6,7},{7,6},{8,9},{9,8},{10,11... | collective-permute-start | bytes 1572872 | tf_op jit(solution)/shard_map/ppermute | solution.py:208
  23.5 13.5 %collective-permute-start = (bf16[320,512]{1,0:T(8,128)(2,1)S(1)}, bf16[320,512]{1,0:T(8,128)(2,1)S(1)}, u32[]{:S(2)}, u32[]{:S(2)}) collective-permute-start(bf16[320,512]{1,0:T(8,128)(2,1)S(1)} %subtract_convert_fusion.own_ref), channel_id=1, source_target_pairs={{0,8},{8,0},{1,9},{9,1},{2,10},{10,2},{3,11},{11,3},{4,12},{12,4},... | collective-permute-start | bytes 983048 | tf_op jit(solution)/shard_map/ppermute | solution.py:213
  66.4 42.4 %copy-start.5 = (s32[1,8]{1,0:T(1,128)S(1)}, s32[1,8]{1,0:T(1,128)}, u32[]{:S(2)}) copy-start(s32[1,8]{1,0:T(1,128)} %param.16) | copy-start | bytes 100
  103.8 15.6 %all-to-all-start.6 = ((bf16[8,160,128]{2,1,0:T(8,128)(2,1)}), bf16[8,160,128]{2,1,0:T(8,128)(2,1)S(1)}, u32[]{:S(2)}, u32[]{:S(2)}) async-start(bf16[8,160,128]{2,1,0:T(8,128)(2,1)} %broadcast_in_dim.34), calls=%async_computation.6 | async-start | bytes 655360 | tf_op jit(solution)/shard_map/all_to_all | solution.py:22

commit v3 on v2

v3 whole, which is shorter than its diff:
```python
import jax
import jax.numpy as jnp
from jax import lax
from jax.experimental import pallas as pl
from jax.experimental.pallas import tpu as pltpu
from jax.sharding import Mesh, PartitionSpec as P

epsilon = 1e-06
beta_scale = 0.05

AXES = ("yh", "zh", "zl", "yl", "x", "c")
REP = ("yh", "zh", "zl")
FSDP = ("yl", "x", "c")
GROUP = ("x", "c")
OFFSETS = (0, -1, 1, 2)
VMEM_LIMIT = 24 * 1024 * 1024
VMEM = pl.BlockSpec(memory_space=pltpu.VMEM)
SMEM = pl.BlockSpec(memory_space=pltpu.SMEM)
f32, bf16 = jnp.float32, jnp.bfloat16


def exchange(pieces, axes):
    return lax.all_to_all(pieces, axes, 0, 0, tiled=False)


def spread(block, axes):
    count = lax.axis_size(axes)
    return exchange(jnp.broadcast_to(block[None], (count,) + block.shape), axes)


def wide_sum(parts):
    total = parts[0].astype(f32)
    for k in range(1, parts.shape[0]):
        total = total + parts[k].astype(f32)
    return total


def norm_kernel(lengths_ref, hidden_ref, gain_ref, readout_ref, pieces_ref, masked_ref):
    block, width = hidden_ref.shape
    groups, _, share = pieces_ref.shape
    part = share // 2
    wide = hidden_ref[...].astype(f32)
    mean_square = jnp.sum(wide * wide, axis=-1, keepdims=True) * (1.0 / width)
    scale = lax.rsqrt(mean_square + epsilon)
    normed = (wide * scale * gain_ref[...]).astype(bf16)
    for g in range(groups):
        starts = [(yl * groups + g) * part for yl in range(2)]
        pieces_ref[g] = jnp.concatenate([normed[:, at : at + part] for at in starts], axis=1)
    position = lax.broadcasted_iota(jnp.int32, readout_ref.shape, 0) + pl.program_id(0) * block
    read = readout_ref[...].astype(f32)
    masked_ref[...] = jnp.where(position < lengths_ref[0], read, 0.0).astype(bf16)


def norm_call(lengths, hidden, gain, readout, groups):
    seq_len, width = hidden.shape
    features = readout.shape[1]
    share = width // groups
    block = 64
    return pl.pallas_call(
        norm_kernel,
        grid=(seq_len // block,),
        in_specs=[
            SMEM,
            pl.BlockSpec((block, width), lambda i: (i, 0)),
            pl.BlockSpec((1, width), lambda i: (0, 0)),
            pl.BlockSpec((block, features), lambda i: (i, 0)),
        ],
        out_specs=[
            pl.BlockSpec((groups, block, share), lambda i: (0, i, 0)),
            pl.BlockSpec((block, features), lambda i: (i, 0)),
        ],
        out_shape=[
            jax.ShapeDtypeStruct((groups, seq_len, share), bf16),
            jax.ShapeDtypeStruct((seq_len, features), bf16),
        ],
        compiler_params=pltpu.CompilerParams(vmem_limit_bytes=60 * 1024 * 1024),
    )(lengths, hidden, gain, readout)


def place_kernel(pieces_ref, out_ref):
    for k in range(pieces_ref.shape[0]):
        out_ref[:, 128 * k : 128 * (k + 1)] = pieces_ref[k].astype(f32)


def place_call(pieces, halves):
    count, part, lanes = pieces.shape
    across = count // halves
    return pl.pallas_call(
        place_kernel,
        grid=(halves,),
        in_specs=[pl.BlockSpec((across, part, lanes), lambda i: (i, 0, 0))],
        out_specs=pl.BlockSpec((part, across * lanes), lambda i: (i, 0)),
        out_shape=jax.ShapeDtypeStruct((halves * part, across * lanes), f32),
        compiler_params=pltpu.CompilerParams(vmem_limit_bytes=VMEM_LIMIT),
    )(pieces)


def seq_of(place_ref, j, swapped):
    x_from = lax.rem(place_ref[0] + (OFFSETS[j] + 4), 4)
    core = place_ref[2]
    return 2 * x_from + (1 - core if swapped else core)


def add_margins(acc, place_ref, columns_ref, delta, reads, swapped):
    row = lax.broadcasted_iota(jnp.int32, acc.shape, 0)
    for j in range(4):
        seq = seq_of(place_ref, j, swapped)
        value = jnp.dot(columns_ref[seq], delta, preferred_element_type=f32)
        prod = value * reads[j].astype(f32)
        part = prod[:, :128]
        for k in range(1, prod.shape[1] // 128):
            part = part + prod[:, 128 * k : 128 * (k + 1)]
        line = jnp.sum(part.T, axis=0, keepdims=True)
        acc = jnp.where(row == seq, line, acc)
    return acc


def margin_kernel(
    place_ref, tags_ref, own, other, columns_ref, n0, n1, n2, n3, f0, f3, out_ref, delta_ref
):
    groups, seq_len, share = columns_ref.shape
    delta_ref[place_ref[1]] = own[...]
    delta_ref[1 - place_ref[1]] = other[...]
    delta = delta_ref[...].reshape(share, delta_ref.shape[2])
    row = lax.broadcasted_iota(jnp.int32, (2 * groups, seq_len), 0)
    me = seq_of(place_ref, 0, False)
    acc = jnp.where(row == me + groups, tags_ref[0].astype(f32), 0.0)
    near = [ref[...] for ref in (n0, n1, n2, n3)]
    far = [f0[...]] + [f3[j] for j in range(3)]
    acc = add_margins(acc, place_ref, columns_ref, delta, near, False)
    acc = add_margins(acc, place_ref, columns_ref, delta, far, True)
    for g in range(out_ref.shape[0]):
        out_ref[g] = acc


def margin_call(place, labels, deltas, columns, near, far):
    groups, seq_len, _ = columns.shape
    return pl.pallas_call(
        margin_kernel,
        in_specs=[SMEM, SMEM] + [VMEM] * 9,
        out_specs=VMEM,
        out_shape=jax.ShapeDtypeStruct((groups, 2 * groups, seq_len), f32),
        scratch_shapes=[pltpu.VMEM((2,) + deltas[0].shape, bf16)],
        compiler_params=pltpu.CompilerParams(vmem_limit_bytes=VMEM_LIMIT),
    )(place, labels, *deltas, columns, *near, *far)


def grad_kernel(
    place_ref, small_ref, columns_ref, n0, n1, n2, n3, f0, f3, grad_ref, margin_ref, slope_ref
):
    groups, seq_len, share = columns_ref.shape
    small = small_ref[0]
    for g in range(1, groups):
        small = small + small_ref[g]
    margin = small[:groups]
    margin_ref[...] = margin
    label = small[groups:, :1]
    total = jnp.sum(beta_scale * margin, axis=1, keepdims=True)
    weight = beta_scale * (1.0 / (1.0 + jnp.exp(-total)) - label)
    row = lax.broadcasted_iota(jnp.int32, weight.shape, 0)
    near = [ref[...] for ref in (n0, n1, n2, n3)]
    far = [f0[...]] + [f3[j] for j in range(3)]
    for swapped, reads in ((False, near), (True, far)):
        for j in range(4):
            seq = seq_of(place_ref, j, swapped)
            w = jnp.sum(jnp.where(row == seq, weight, 0.0), axis=0, keepdims=True)
            slope_ref[seq] = (w * reads[j].astype(f32)).astype(bf16)
    columns = columns_ref[...].reshape(groups * seq_len, share)
    slope = slope_ref[...].reshape(groups * seq_len, slope_ref.shape[2])
    grad = lax.dot_general(
        columns, slope, (((0,), (0,)), ((), ())), preferred_element_type=f32
    ).astype(bf16)
    part = grad_ref.shape[1]
    for yh in range(2):
        for yl in range(2):
            at = (2 * yl + yh) * part
            grad_ref[2 * yh + yl] = grad[at : at + part]


def grad_call(place, small, columns, near, far):
    groups, seq_len, share = columns.shape
    features = near[0].shape[1]
    return pl.pallas_call(
        grad_kernel,
        in_specs=[SMEM] + [VMEM] * 8,
        out_specs=[VMEM, VMEM],
        out_shape=[
            jax.ShapeDtypeStruct((4, share // 4, features), bf16),
            jax.ShapeDtypeStruct((groups, seq_len), f32),
        ],
        scratch_shapes=[pltpu.VMEM((groups, seq_len, features), bf16)],
        compiler_params=pltpu.CompilerParams(vmem_limit_bytes=VMEM_LIMIT),
    )(place, small, columns, *near, *far)


def shifted(block, axes):
    pairs = [[(i, (i - shift) % 4) for i in range(4)] for shift in OFFSETS[1:]]
    return [block] + [lax.ppermute(block, axes, pair) for pair in pairs]


def on_device(
    hidden, norm_gain, quant_ref, scale_ref, weight_prm, readout, lengths, bounds, labels
):
    seq_len, width = hidden.shape[1:]
    features = readout.shape[2]
    head_size = features // scale_ref.shape[0]
    steps_count = bounds.shape[1]
    group = lax.axis_size(GROUP)
    x, y_lo, core = lax.axis_index("x"), lax.axis_index("yl"), lax.axis_index("c")
    me = 2 * x + core
    place = jnp.stack([x, y_lo, core]).astype(jnp.int32)
    swap = [(0, 1), (1, 0)]
    pieces, masked = norm_call(lengths, hidden[0], norm_gain[None], readout[0], group)
    columns = exchange(pieces, GROUP)
    expanded = jnp.repeat(scale_ref.T, head_size, axis=1)
    ref_local = (quant_ref.astype(f32) * expanded).astype(bf16)
    delta = (weight_prm.astype(f32) - ref_local.astype(f32)).astype(bf16)
    delta_other = lax.ppermute(delta, "yl", swap)
    near = shifted(masked, ("x",))
    far_own = lax.ppermute(masked, "c", swap)
    moved = jnp.stack(near[1:])
    moved, delta_other, far_own = lax.optimization_barrier((moved, delta_other, far_own))
    far = [far_own, lax.ppermute(moved, "c", swap)]
    deltas = [delta, delta_other]
    small = exchange(margin_call(place, labels, deltas, columns, near, far), GROUP)
    grad, margin = grad_call(place, small, columns, near, far)
    grad = wide_sum(exchange(grad, ("yh", "yl"))).astype(bf16)
    zl = lax.axis_size("zl")
    grad = grad.reshape(grad.shape[0], zl, features // zl).transpose(1, 0, 2)
    grad = wide_sum(exchange(grad, ("zl",))).astype(bf16)
    grad = wide_sum(spread(grad, ("zh",))).astype(bf16)
    grad = place_call(spread(grad, ("yh", "zl")), lax.axis_size("yh"))
    position = jnp.arange(seq_len, dtype=jnp.int32)
    reward = beta_scale * lax.dynamic_slice_in_dim(margin, me, 1, axis=0)
    step_index = jnp.sum((position[:, None] >= bounds[0][None, :]).astype(jnp.int32), axis=-1) - 1
    onehot = (step_index[:, None] == jnp.arange(steps_count)[None, :]).astype(f32)
    step_rewards = jnp.sum(reward[0][:, None] * onehot, axis=0)[None]
    return step_rewards, grad


def solution(mesh):
    fine = Mesh(mesh.devices.reshape(2, 4, 4, 2, 4, 2), AXES)
    every = REP + FSDP
    in_specs = (
        P(every, None, None),
        P(),
        P(FSDP, None),
        P(None, FSDP),
        P(FSDP, None),
        P(every, None, None),
        P(every),
        P(every, None),
        P(every),
    )
    out_specs = (P(every, None), P(FSDP, None))
    return jax.shard_map(
        on_device, mesh=fine, in_specs=in_specs, out_specs=out_specs, check_vma=False
    )
```

time: 121 us -> 118 us (0.975)
  waiting for transfers between devices: 26.4 us -> 14.4 us
  starting transfers between devices: 20.6 us -> 31.5 us
  Pallas kernels: 8.47 us -> 7.13 us
    ppermute x2 -> x6, starting transfers between devices: 7.79 us -> 22 us  [the longest x3 11.2 us: shifted(): return [block] + [lax.ppermute(block, axes, pair) for pair in pairs]]
    all_to_all x3 -> x2, waiting for transfers between devices: 19.1 us -> 9.87 us  [exchange(): return lax.all_to_all(pieces, axes, 0, 0, tiled=False)]
    all_to_all x3 -> x2, starting transfers between devices: 12.8 us -> 9.42 us  [exchange(): return lax.all_to_all(pieces, axes, 0, 0, tiled=False)]
    ppermute x2 -> x6, waiting for transfers between devices: 7.25 us -> 4.49 us  [the longest x3 3.53 us: shifted(): return [block] + [lax.ppermute(block, axes, pair) for pair in pairs]]
    pallas_call x4 -> x3, Pallas kernels: 7.6 us -> 6.26 us  [the longest x1 2.8 us: norm_call(): pl.pallas_call(norm_kernel, grid=(seq_len // block,), in_specs=[SMEM, pl....]
  transfers between devices with their start and end apart: 5 -> 8, of which waited for: 4 -> 5; matrix products, arithmetic and copies ran while one was open for 1% -> 1% of each run, Pallas kernels for 2% -> 0%
where the time goes in v3:
time: 118 us
  blocking collectives  60.1 us (51%)
  starting transfers between devices  31.5 us (27%)
  waiting for transfers between devices  14.4 us (12%)
  Pallas kernels  7.13 us (6%)
  between operations  2.12 us (2%)
  local copies, waits for them, and re-layouts  1.42 us (1%)
    all_to_all x4, blocking collectives, exchange(): return lax.all_to_all(pieces, axes, 0, 0, tiled=False)  60.1 us
    ppermute x3, starting transfers between devices, shifted(): return [block] + [lax.ppermute(block, axes, pair) for pair in pairs]  11.2 us
    all_to_all x2, waiting for transfers between devices, exchange(): return lax.all_to_all(pieces, axes, 0, 0, tiled=False)  9.87 us
    all_to_all x2, starting transfers between devices, exchange(): return lax.all_to_all(pieces, axes, 0, 0, tiled=False)  9.42 us
    ppermute x1, starting transfers between devices, on_device(): delta_other = lax.ppermute(delta, 'yl', swap)  7.04 us
    ppermute x3, waiting for transfers between devices, shifted(): return [block] + [lax.ppermute(block, axes, pair) for pair in pairs]  3.53 us
    pallas_call x1, Pallas kernels, norm_call(): pl.pallas_call(norm_kernel, grid=(seq_len // block,), in_specs=[SMEM, pl....  2.8 us
  transfers between devices with their start and end apart: 8, of which 5 were waited for; matrix products, arithmetic and copies ran while one was open for 1% of the time, Pallas kernels for 0%

profile of v3, /device:TPU:8, one launch (start us, length us, event | category | flops | bytes accessed | tf_op | source)
XLA Modules:
  0.0 117.7 jit_solution(1942675095776035254)
XLA Ops:
  1.3 2.8 %shard_map.104 = (bf16[8,128,640]{2,1,0:T(8,128)(2,1)}, bf16[128,512]{1,0:T(8,128)(2,1)}) custom-call(s32[1]{0:T(128)S(6)} %copy.22.lengths_ref, bf16[128,5120]{1,0:T(8,128)(2,1)} %bitcast.32, f32[1,5120]{1,0:T(1,128)} %bitcast.35, bf16[128,512]{1,0:T(8,128)(2,1)} %bitcast.34), custom_call_target="tpu_custom_call" | custom-call | tf_op jit(solution)/shard_map/pallas_call | solution.py:59
  4.1 0.0 copy-start.3
  4.1 0.0 copy-start.1
  4.1 0.0 copy-start.2
  4.1 4.4 %all-to-all-start = ((bf16[8,128,640]{2,1,0:T(8,128)(2,1)}), bf16[8,128,640]{2,1,0:T(8,128)(2,1)S(1)}, u32[]{:S(2)}, u32[]{:S(2)}) async-start(bf16[8,128,640]{2,1,0:T(8,128)(2,1)} %get-tuple-element.11), calls=%async_computation | async-start | bytes 2621440 | tf_op jit(solution)/shard_map/all_to_all | solution.py:23
  8.5 0.0 copy-done.3
  8.5 0.0 copy-start
  8.6 0.1 copy.14
  8.7 0.4 broadcast_in_dim.28
  9.1 0.0 copy-done.1
  9.1 0.0 copy-done.2
  9.1 0.2 subtract_convert_fusion.own
  9.3 7.0 %collective-permute-start.3 = (bf16[320,512]{1,0:T(8,128)(2,1)S(1)}, bf16[320,512]{1,0:T(8,128)(2,1)S(1)}, u32[]{:S(2)}, u32[]{:S(2)}) collective-permute-start(bf16[320,512]{1,0:T(8,128)(2,1)S(1)} %subtract_convert_fusion.own), channel_id=1, source_target_pairs={{0,8},{8,0},{1,9},{9,1},{2,10},{10,2},{3,11},{11,3},{4,12},{12,4},... | collective-permute-start | bytes 983048 | tf_op jit(solution)/shard_map/ppermute | solution.py:218
  16.3 0.0 copy-done
  16.3 5.3 %collective-permute-start.2 = (bf16[128,512]{1,0:T(8,128)(2,1)S(1)}, bf16[128,512]{1,0:T(8,128)(2,1)S(1)}, u32[]{:S(2)}, u32[]{:S(2)}) collective-permute-start(bf16[128,512]{1,0:T(8,128)(2,1)S(1)} %copy-done), channel_id=1, source_target_pairs={{0,4},{2,6},{4,0},{6,2},{1,5},{3,7},{5,1},{7,3},{8,12},{10,14},{12... | collective-permute-start | bytes 393224 | tf_op jit(solution)/shard_map/ppermute | solution.py:198
  21.7 3.1 %collective-permute-start.1 = (bf16[128,512]{1,0:T(8,128)(2,1)S(1)}, bf16[128,512]{1,0:T(8,128)(2,1)S(1)}, u32[]{:S(2)}, u32[]{:S(2)}) collective-permute-start(bf16[128,512]{1,0:T(8,128)(2,1)S(1)} %copy-done), channel_id=1, source_target_pairs={{0,6},{2,0},{4,2},{6,4},{1,7},{3,1},{5,3},{7,5},{8,14},{10,8},{12,... | collective-permute-start | bytes 393224 | tf_op jit(solution)/shard_map/ppermute | solution.py:198
  24.7 2.8 %collective-permute-start = (bf16[128,512]{1,0:T(8,128)(2,1)S(1)}, bf16[128,512]{1,0:T(8,128)(2,1)S(1)}, u32[]{:S(2)}, u32[]{:S(2)}) collective-permute-start(bf16[128,512]{1,0:T(8,128)(2,1)S(1)} %copy-done), channel_id=1, source_target_pairs={{0,2},{2,4},{4,6},{6,0},{1,3},{3,5},{5,7},{7,1},{8,10},{10,12},{12... | collective-permute-start | bytes 393224 | tf_op jit(solution)/shard_map/ppermute | solution.py:198
  27.5 1.9 %collective-permute-start.4 = (bf16[128,512]{1,0:T(8,128)(2,1)S(1)}, bf16[128,512]{1,0:T(8,128)(2,1)S(1)}, u32[]{:S(2)}, u32[]{:S(2)}) collective-permute-start(bf16[128,512]{1,0:T(8,128)(2,1)S(1)} %copy-done), channel_id=1, source_target_pairs={{0,1},{1,0},{2,3},{3,2},{4,5},{5,4},{6,7},{7,6},{8,9},{9,8},{10,11... | collective-permute-start | bytes 393224 | tf_op jit(solution)/shard_map/ppermute | solution.py:220
  29.5 1.1 collective-permute-done.2.n3
  30.6 0.9 collective-permute-done.1.n2
  31.5 1.5 %collective-permute-done.n1 = bf16[128,512]{1,0:T(8,128)(2,1)S(1)} collective-permute-done((bf16[128,512]{1,0:T(8,128)(2,1)S(1)}, bf16[128,512]{1,0:T(8,128)(2,1)S(1)}, u32[]{:S(2)}, u32[]{:S(2)}) %collective-permute-start) | collective-permute-done | bytes 131104 | tf_op jit(solution)/shard_map/ppermute | solution.py:198
  33.0 0.0 collective-permute-done.4.f0
  33.0 0.0 collective-permute-done.3.other
  33.1 1.9 %collective-permute-start.5 = (bf16[3,128,512]{2,1,0:T(8,128)(2,1)S(1)}, bf16[3,128,512]{2,1,0:T(8,128)(2,1)S(1)}, u32[]{:S(2)}, u32[]{:S(2)}) collective-permute-start(bf16[3,128,512]{2,1,0:T(8,128)(2,1)S(1)} %pad_maximum_fusion), channel_id=1, source_target_pairs={{0,1},{1,0},{2,3},{3,2},{4,5},{5,4},{6,7},{7,6},{8,9},{9,8},{10,11... | collective-permute-start | bytes 1179656 | tf_op jit(solution)/shard_map/ppermute | solution.py:223
  35.6 0.1 pad_add_fusion.place_ref
  35.7 1.0 collective-permute-done.5.f3
  36.7 0.0 all-to-all-done.columns_ref
  36.7 1.7 %shard_map.105 = f32[8,16,128]{2,1,0:T(8,128)S(1)} custom-call(s32[3]{0:T(128)S(1)} %pad_add_fusion.place_ref, s32[1]{0:T(128)S(6)} %copy.23.tags_ref, bf16[320,512]{1,0:T(8,128)(2,1)S(1)} %subtract_convert_fusion.own, bf16[320,512]{1,0:T(8,128)(2,1)S(1)} %collective-permute-done.3.other, bf16[8,128,640]{2,1,0:T(8,128)(2,1)S(1)} %all-to-all-done.columns_ref, ...), custom_call_target="tpu_custom_call" | custom-call | tf_op jit(solution)/shard_map/pallas_call | solution.py:138
  38.3 8.0 %all_to_all.30.small_ref = f32[8,16,128]{2,1,0:T(8,128)S(1)} all-to-all(f32[8,16,128]{2,1,0:T(8,128)S(1)} %shard_map.105), channel_id=1, replica_groups=mesh['yh'=2,'zh'=4,'zl'=4,'yl'=2,'x'=4,'c'=2] {'x','c'}, dimensions={0} | all-to-all | bytes 131072 | tf_op jit(solution)/shard_map/all_to_all | solution.py:23
  46.3 1.8 %shard_map.106 = (bf16[4,160,512]{2,1,0:T(8,128)(2,1)S(1)}, f32[8,128]{1,0:T(8,128)S(1)}) custom-call(s32[3]{0:T(128)S(1)} %pad_add_fusion.place_ref, f32[8,16,128]{2,1,0:T(8,128)S(1)} %all_to_all.30.small_ref, bf16[8,128,640]{2,1,0:T(8,128)(2,1)S(1)} %all-to-all-done.columns_ref, bf16[128,512]{1,0:T(8,128)(2,1)S(1)} %copy-done, ...), custom_call_target="tpu_custom_call" | custom-call | tf_op jit(solution)/shard_map/pallas_call | solution.py:183
  48.1 17.0 %all_to_all.31 = bf16[4,160,512]{2,1,0:T(8,128)(2,1)S(1)} all-to-all(bf16[4,160,512]{2,1,0:T(8,128)(2,1)S(1)} %get-tuple-element.15), channel_id=1, replica_groups=mesh['yh'=2,'zh'=4,'zl'=4,'yl'=2,'x'=4,'c'=2] {'yh','yl'}, dimensions={0} | all-to-all | bytes 1310720 | tf_op jit(solution)/shard_map/all_to_all | solution.py:23
  65.1 0.1 add_convert_fusion
  65.3 0.0 copy-start.4
  65.3 9.4 %all_to_all.32 = bf16[4,160,128]{2,1,0:T(8,128)(2,1)S(1)} all-to-all(bf16[4,160,128]{2,1,0:T(8,128)(2,1)S(1)} %bitcast.33), channel_id=1, replica_groups=mesh['yh'=2,'zh'=4,'zl'=4,'yl'=2,'x'=4,'c'=2] {'zl'}, dimensions={0} | all-to-all | bytes 327680 | tf_op jit(solution)/shard_map/all_to_all | solution.py:23
  74.8 25.7 %all_to_all.33 = bf16[4,160,128]{2,1,0:T(8,128)(2,1)S(1)} all-to-all(bf16[4,160,128]{2,1,0:T(8,128)(2,1)S(1)} %broadcast_in_dim.32), channel_id=1, replica_groups=mesh['yh'=2,'zh'=4,'zl'=4,'yl'=2,'x'=4,'c'=2] {'zh'}, dimensions={0} | all-to-all | bytes 327680 | tf_op jit(solution)/shard_map/all_to_all | solution.py:23
  100.5 0.8 broadcast_in_dim.34
  101.2 5.0 %all-to-all-start.5 = ((bf16[8,160,128]{2,1,0:T(8,128)(2,1)}), bf16[8,160,128]{2,1,0:T(8,128)(2,1)S(1)}, u32[]{:S(2)}, u32[]{:S(2)}) async-start(bf16[8,160,128]{2,1,0:T(8,128)(2,1)} %broadcast_in_dim.34), calls=%async_computation.5 | async-start | bytes 655360 | tf_op jit(solution)/shard_map/all_to_all | solution.py:23
  106.2 0.0 copy-done.4
  106.2 0.1 convert_reduce_fusion
  106.3 0.6 select_reduce_fusion
  107.0 9.9 %all-to-all-done.5.pieces_ref = bf16[8,160,128]{2,1,0:T(8,128)(2,1)S(1)} async-done(((bf16[8,160,128]{2,1,0:T(8,128)(2,1)}), bf16[8,160,128]{2,1,0:T(8,128)(2,1)S(1)}, u32[]{:S(2)}, u32[]{:S(2)}) %all-to-all-start.5) | async-done | bytes 327712 | tf_op jit(solution)/shard_map/all_to_all | solution.py:23
  116.8 0.9 shard_map.107
  (8 shorter events, 0.2 us)
Async XLA Ops:
  4.1 4.5 %copy-start.3 = (f32[4,320]{1,0:T(4,128)S(1)}, f32[4,320]{1,0:T(4,128)}, u32[]{:S(2)}) copy-start(f32[4,320]{1,0:T(4,128)} %param.12) | copy-start | bytes 15364
  4.1 5.0 %copy-start.1 = (bf16[320,512]{1,0:T(8,128)(2,1)S(1)}, bf16[320,512]{1,0:T(8,128)(2,1)}, u32[]{:S(2)}) copy-start(bf16[320,512]{1,0:T(8,128)(2,1)} %param.13) | copy-start | bytes 983044
  4.1 5.0 %copy-start.2 = (bf16[320,512]{1,0:T(8,128)(2,1)S(1)}, bf16[320,512]{1,0:T(8,128)(2,1)}, u32[]{:S(2)}) copy-start(bf16[320,512]{1,0:T(8,128)(2,1)} %param.11) | copy-start | bytes 983044
  4.1 32.6 %all-to-all-start = ((bf16[8,128,640]{2,1,0:T(8,128)(2,1)}), bf16[8,128,640]{2,1,0:T(8,128)(2,1)S(1)}, u32[]{:S(2)}, u32[]{:S(2)}) async-start(bf16[8,128,640]{2,1,0:T(8,128)(2,1)} %get-tuple-element.11), calls=%async_computation | async-start | bytes 2621440 | tf_op jit(solution)/shard_map/all_to_all | solution.py:23
  8.5 7.8 %copy-start = (bf16[128,512]{1,0:T(8,128)(2,1)S(1)}, bf16[128,512]{1,0:T(8,128)(2,1)}, u32[]{:S(2)}) copy-start(bf16[128,512]{1,0:T(8,128)(2,1)} %get-tuple-element.9.n0) | copy-start | bytes 393220
  9.3 23.8 %collective-permute-start.3 = (bf16[320,512]{1,0:T(8,128)(2,1)S(1)}, bf16[320,512]{1,0:T(8,128)(2,1)S(1)}, u32[]{:S(2)}, u32[]{:S(2)}) collective-permute-start(bf16[320,512]{1,0:T(8,128)(2,1)S(1)} %subtract_convert_fusion.own), channel_id=1, source_target_pairs={{0,8},{8,0},{1,9},{9,1},{2,10},{10,2},{3,11},{11,3},{4,12},{12,4},... | collective-permute-start | bytes 983048 | tf_op jit(solution)/shard_map/ppermute | solution.py:218
  16.3 14.3 %collective-permute-start.2 = (bf16[128,512]{1,0:T(8,128)(2,1)S(1)}, bf16[128,512]{1,0:T(8,128)(2,1)S(1)}, u32[]{:S(2)}, u32[]{:S(2)}) collective-permute-start(bf16[128,512]{1,0:T(8,128)(2,1)S(1)} %copy-done), channel_id=1, source_target_pairs={{0,4},{2,6},{4,0},{6,2},{1,5},{3,7},{5,1},{7,3},{8,12},{10,14},{12... | collective-permute-start | bytes 393224 | tf_op jit(solution)/shard_map/ppermute | solution.py:198
  21.7 9.8 %collective-permute-start.1 = (bf16[128,512]{1,0:T(8,128)(2,1)S(1)}, bf16[128,512]{1,0:T(8,128)(2,1)S(1)}, u32[]{:S(2)}, u32[]{:S(2)}) collective-permute-start(bf16[128,512]{1,0:T(8,128)(2,1)S(1)} %copy-done), channel_id=1, source_target_pairs={{0,6},{2,0},{4,2},{6,4},{1,7},{3,1},{5,3},{7,5},{8,14},{10,8},{12,... | collective-permute-start | bytes 393224 | tf_op jit(solution)/shard_map/ppermute | solution.py:198
  24.7 8.2 %collective-permute-start = (bf16[128,512]{1,0:T(8,128)(2,1)S(1)}, bf16[128,512]{1,0:T(8,128)(2,1)S(1)}, u32[]{:S(2)}, u32[]{:S(2)}) collective-permute-start(bf16[128,512]{1,0:T(8,128)(2,1)S(1)} %copy-done), channel_id=1, source_target_pairs={{0,2},{2,4},{4,6},{6,0},{1,3},{3,5},{5,7},{7,1},{8,10},{10,12},{12... | collective-permute-start | bytes 393224 | tf_op jit(solution)/shard_map/ppermute | solution.py:198
  27.5 5.5 %collective-permute-start.4 = (bf16[128,512]{1,0:T(8,128)(2,1)S(1)}, bf16[128,512]{1,0:T(8,128)(2,1)S(1)}, u32[]{:S(2)}, u32[]{:S(2)}) collective-permute-start(bf16[128,512]{1,0:T(8,128)(2,1)S(1)} %copy-done), channel_id=1, source_target_pairs={{0,1},{1,0},{2,3},{3,2},{4,5},{5,4},{6,7},{7,6},{8,9},{9,8},{10,11... | collective-permute-start | bytes 393224 | tf_op jit(solution)/shard_map/ppermute | solution.py:220
  33.1 3.6 %collective-permute-start.5 = (bf16[3,128,512]{2,1,0:T(8,128)(2,1)S(1)}, bf16[3,128,512]{2,1,0:T(8,128)(2,1)S(1)}, u32[]{:S(2)}, u32[]{:S(2)}) collective-permute-start(bf16[3,128,512]{2,1,0:T(8,128)(2,1)S(1)} %pad_maximum_fusion), channel_id=1, source_target_pairs={{0,1},{1,0},{2,3},{3,2},{4,5},{5,4},{6,7},{7,6},{8,9},{9,8},{10,11... | collective-permute-start | bytes 1179656 | tf_op jit(solution)/shard_map/ppermute | solution.py:223
  65.3 41.0 %copy-start.4 = (s32[1,8]{1,0:T(1,128)S(1)}, s32[1,8]{1,0:T(1,128)}, u32[]{:S(2)}) copy-start(s32[1,8]{1,0:T(1,128)} %param.16) | copy-start | bytes 100
  101.2 15.6 %all-to-all-start.5 = ((bf16[8,160,128]{2,1,0:T(8,128)(2,1)}), bf16[8,160,128]{2,1,0:T(8,128)(2,1)S(1)}, u32[]{:S(2)}, u32[]{:S(2)}) async-start(bf16[8,160,128]{2,1,0:T(8,128)(2,1)} %broadcast_in_dim.34), calls=%async_computation.5 | async-start | bytes 655360 | tf_op jit(solution)/shard_map/all_to_all | solution.py:23

commit v4 on v3

--- a/solution.py
+++ b/solution.py
@@ -35,8 +35,8 @@
     return total
 
 
-def norm_kernel(lengths_ref, hidden_ref, gain_ref, readout_ref, pieces_ref, masked_ref):
-    block, width = hidden_ref.shape
+def norm_kernel(hidden_ref, gain_ref, pieces_ref):
+    width = hidden_ref.shape[1]
     groups, _, share = pieces_ref.shape
     part = share // 2
     wide = hidden_ref[...].astype(f32)
@@ -46,35 +46,23 @@
     for g in range(groups):
         starts = [(yl * groups + g) * part for yl in range(2)]
         pieces_ref[g] = jnp.concatenate([normed[:, at : at + part] for at in starts], axis=1)
-    position = lax.broadcasted_iota(jnp.int32, readout_ref.shape, 0) + pl.program_id(0) * block
-    read = readout_ref[...].astype(f32)
-    masked_ref[...] = jnp.where(position < lengths_ref[0], read, 0.0).astype(bf16)
-
-
-def norm_call(lengths, hidden, gain, readout, groups):
+
+
+def norm_call(hidden, gain, groups):
     seq_len, width = hidden.shape
-    features = readout.shape[1]
     share = width // groups
     block = 64
     return pl.pallas_call(
         norm_kernel,
         grid=(seq_len // block,),
         in_specs=[
-            SMEM,
             pl.BlockSpec((block, width), lambda i: (i, 0)),
             pl.BlockSpec((1, width), lambda i: (0, 0)),
-            pl.BlockSpec((block, features), lambda i: (i, 0)),
         ],
-        out_specs=[
-            pl.BlockSpec((groups, block, share), lambda i: (0, i, 0)),
-            pl.BlockSpec((block, features), lambda i: (i, 0)),
-        ],
-        out_shape=[
-            jax.ShapeDtypeStruct((groups, seq_len, share), bf16),
-            jax.ShapeDtypeStruct((seq_len, features), bf16),
-        ],
+        out_specs=pl.BlockSpec((groups, block, share), lambda i: (0, i, 0)),
+        out_shape=jax.ShapeDtypeStruct((groups, seq_len, share), bf16),
         compiler_params=pltpu.CompilerParams(vmem_limit_bytes=60 * 1024 * 1024),
-    )(lengths, hidden, gain, readout)
+    )(hidden, gain)
 
 
 def place_kernel(pieces_ref, out_ref):
@@ -115,34 +103,41 @@
     return acc
 
 
-def margin_kernel(
-    place_ref, tags_ref, own, other, columns_ref, n0, n1, n2, n3, f0, f3, out_ref, delta_ref
-):
-    groups, seq_len, share = columns_ref.shape
-    delta_ref[place_ref[1]] = own[...]
-    delta_ref[1 - place_ref[1]] = other[...]
-    delta = delta_ref[...].reshape(share, delta_ref.shape[2])
-    row = lax.broadcasted_iota(jnp.int32, (2 * groups, seq_len), 0)
+def near_kernel(place_ref, tags_ref, delta_ref, columns_ref, n0, n1, n2, n3, acc_ref):
+    groups, seq_len, _ = columns_ref.shape
+    row = lax.broadcasted_iota(jnp.int32, acc_ref.shape, 0)
+    lane = lax.broadcasted_iota(jnp.int32, acc_ref.shape, 1)
     me = seq_of(place_ref, 0, False)
-    acc = jnp.where(row == me + groups, tags_ref[0].astype(f32), 0.0)
-    near = [ref[...] for ref in (n0, n1, n2, n3)]
-    far = [f0[...]] + [f3[j] for j in range(3)]
-    acc = add_margins(acc, place_ref, columns_ref, delta, near, False)
-    acc = add_margins(acc, place_ref, columns_ref, delta, far, True)
+    tags = jnp.where(lane < seq_len // 2, tags_ref[0], tags_ref[1]).astype(f32)
+    acc = jnp.where(row == me + groups, tags, 0.0)
+    reads = [ref[...] for ref in (n0, n1, n2, n3)]
+    acc_ref[...] = add_margins(acc, place_ref, columns_ref, delta_ref[...], reads, False)
+
+
+def far_kernel(place_ref, acc_ref, delta_ref, columns_ref, f0, f3, out_ref):
+    reads = [f0[...]] + [f3[j] for j in range(3)]
+    acc = add_margins(acc_ref[...], place_ref, columns_ref, delta_ref[...], reads, True)
     for g in range(out_ref.shape[0]):
         out_ref[g] = acc
 
 
-def margin_call(place, labels, deltas, columns, near, far):
+def margin_call(place, tags, delta, columns, near, far):
     groups, seq_len, _ = columns.shape
-    return pl.pallas_call(
-        margin_kernel,
-        in_specs=[SMEM, SMEM] + [VMEM] * 9,
+    params = pltpu.CompilerParams(vmem_limit_bytes=VMEM_LIMIT)
+    acc = pl.pallas_call(
+        near_kernel,
+        in_specs=[SMEM, SMEM] + [VMEM] * 6,
+        out_specs=VMEM,
+        out_shape=jax.ShapeDtypeStruct((2 * groups, seq_len), f32),
+        compiler_params=params,
+    )(place, tags, delta, columns, *near)
+    return pl.pallas_call(
+        far_kernel,
+        in_specs=[SMEM] + [VMEM] * 5,
         out_specs=VMEM,
         out_shape=jax.ShapeDtypeStruct((groups, 2 * groups, seq_len), f32),
-        scratch_shapes=[pltpu.VMEM((2,) + deltas[0].shape, bf16)],
-        compiler_params=pltpu.CompilerParams(vmem_limit_bytes=VMEM_LIMIT),
-    )(place, labels, *deltas, columns, *near, *far)
+        compiler_params=params,
+    )(place, acc, delta, columns, *far)
 
 
 def grad_kernel(
@@ -152,19 +147,22 @@
     small = small_ref[0]
     for g in range(1, groups):
         small = small + small_ref[g]
-    margin = small[:groups]
+    label, length = small[groups:, :1], small[groups:, seq_len - 1 :]
+    lane = lax.broadcasted_iota(jnp.int32, (groups, seq_len), 1).astype(f32)
+    margin = jnp.where(lane < length, small[:groups], 0.0)
     margin_ref[...] = margin
-    label = small[groups:, :1]
     total = jnp.sum(beta_scale * margin, axis=1, keepdims=True)
     weight = beta_scale * (1.0 / (1.0 + jnp.exp(-total)) - label)
     row = lax.broadcasted_iota(jnp.int32, weight.shape, 0)
+    position = lax.broadcasted_iota(jnp.int32, (seq_len, 1), 0).astype(f32)
     near = [ref[...] for ref in (n0, n1, n2, n3)]
     far = [f0[...]] + [f3[j] for j in range(3)]
     for swapped, reads in ((False, near), (True, far)):
         for j in range(4):
             seq = seq_of(place_ref, j, swapped)
             w = jnp.sum(jnp.where(row == seq, weight, 0.0), axis=0, keepdims=True)
-            slope_ref[seq] = (w * reads[j].astype(f32)).astype(bf16)
+            live = position < jnp.sum(jnp.where(row == seq, length, 0.0), axis=0, keepdims=True)
+            slope_ref[seq] = (jnp.where(live, w, 0.0) * reads[j].astype(f32)).astype(bf16)
     columns = columns_ref[...].reshape(groups * seq_len, share)
     slope = slope_ref[...].reshape(groups * seq_len, slope_ref.shape[2])
     grad = lax.dot_general(
@@ -210,19 +208,24 @@
     me = 2 * x + core
     place = jnp.stack([x, y_lo, core]).astype(jnp.int32)
     swap = [(0, 1), (1, 0)]
-    pieces, masked = norm_call(lengths, hidden[0], norm_gain[None], readout[0], group)
+    pieces = norm_call(hidden[0], norm_gain[None], group)
     columns = exchange(pieces, GROUP)
     expanded = jnp.repeat(scale_ref.T, head_size, axis=1)
     ref_local = (quant_ref.astype(f32) * expanded).astype(bf16)
     delta = (weight_prm.astype(f32) - ref_local.astype(f32)).astype(bf16)
     delta_other = lax.ppermute(delta, "yl", swap)
-    near = shifted(masked, ("x",))
-    far_own = lax.ppermute(masked, "c", swap)
+    own, _, _ = lax.optimization_barrier((readout[0], pieces, delta))
+    pair = [jnp.where(y_lo == k, delta, delta_other) for k in range(2)]
+    delta = jnp.concatenate(pair, axis=0)
+    near = shifted(own, ("x",))
+    far_own = lax.ppermute(own, "c", swap)
+    tags = jnp.concatenate([labels, lengths])
     moved = jnp.stack(near[1:])
-    moved, delta_other, far_own = lax.optimization_barrier((moved, delta_other, far_own))
+    moved, delta, far_own, place, tags = lax.optimization_barrier(
+        (moved, delta, far_own, place, tags)
+    )
     far = [far_own, lax.ppermute(moved, "c", swap)]
-    deltas = [delta, delta_other]
-    small = exchange(margin_call(place, labels, deltas, columns, near, far), GROUP)
+    small = exchange(margin_call(place, tags, delta, columns, near, far), GROUP)
     grad, margin = grad_call(place, small, columns, near, far)
     grad = wide_sum(exchange(grad, ("yh", "yl"))).astype(bf16)
     zl = lax.axis_size("zl")

time: 118 us -> 117 us (level)
  blocking collectives: 60.1 us -> 57.9 us
    all_to_all x4, blocking collectives: 60.1 us -> 57.9 us  [exchange(): return lax.all_to_all(pieces, axes, 0, 0, tiled=False)]
    pallas_call x2 -> x3, Pallas kernels: 4.45 us -> 5.12 us  [the longest x1 2.73 us: norm_call(): pl.pallas_call(norm_kernel, grid=(seq_len // block,), in_specs=[pl.BlockS...]
  transfers between devices with their start and end apart: 8 -> 8, of which waited for: 5 -> 4; matrix products, arithmetic and copies ran while one was open for 1% -> 1% of each run, Pallas kernels for 0% -> 1%
where the time goes in v4:
time: 117 us
  blocking collectives  57.9 us (49%)
  starting transfers between devices  31.5 us (27%)
  waiting for transfers between devices  14.6 us (12%)
  Pallas kernels  7.89 us (7%)
  between operations  2.13 us (2%)
  local copies, waits for them, and re-layouts  1.42 us (1%)
  other arithmetic  1.31 us (1%)
    all_to_all x4, blocking collectives, exchange(): return lax.all_to_all(pieces, axes, 0, 0, tiled=False)  57.9 us
    ppermute x3, starting transfers between devices, shifted(): return [block] + [lax.ppermute(block, axes, pair) for pair in pairs]  11.1 us
    all_to_all x2, waiting for transfers between devices, exchange(): return lax.all_to_all(pieces, axes, 0, 0, tiled=False)  9.87 us
    all_to_all x2, starting transfers between devices, exchange(): return lax.all_to_all(pieces, axes, 0, 0, tiled=False)  9.43 us
    ppermute x1, starting transfers between devices, on_device(): delta_other = lax.ppermute(delta, 'yl', swap)  7.04 us
    ppermute x3, waiting for transfers between devices, shifted(): return [block] + [lax.ppermute(block, axes, pair) for pair in pairs]  4.21 us
    pallas_call x1, Pallas kernels, norm_call(): pl.pallas_call(norm_kernel, grid=(seq_len // block,), in_specs=[pl.BlockS...  2.73 us
  transfers between devices with their start and end apart: 8, of which 4 were waited for; matrix products, arithmetic and copies ran while one was open for 1% of the time, Pallas kernels for 1%

profile of v4, /device:TPU:8, one launch (start us, length us, event | category | flops | bytes accessed | tf_op | source)
XLA Modules:
  0.0 116.7 jit_solution(15279730678993355611)
XLA Ops:
  0.6 2.7 %shard_map.104 = bf16[8,128,640]{2,1,0:T(8,128)(2,1)} custom-call(bf16[128,5120]{1,0:T(8,128)(2,1)} %bitcast.38, f32[1,5120]{1,0:T(1,128)} %bitcast.40), custom_call_target="tpu_custom_call" | custom-call | tf_op jit(solution)/shard_map/pallas_call | solution.py:55
  3.4 0.0 copy-start.3
  3.4 0.0 copy-start.1
  3.4 0.0 copy-start.2
  3.4 4.4 %all-to-all-start = ((bf16[8,128,640]{2,1,0:T(8,128)(2,1)}), bf16[8,128,640]{2,1,0:T(8,128)(2,1)S(1)}, u32[]{:S(2)}, u32[]{:S(2)}) async-start(bf16[8,128,640]{2,1,0:T(8,128)(2,1)} %shard_map.104), calls=%async_computation | async-start | bytes 2621440 | tf_op jit(solution)/shard_map/all_to_all | solution.py:23
  7.8 0.0 copy-done.3
  7.8 0.0 copy-start
  7.8 0.1 copy.14
  8.0 0.4 broadcast_in_dim.29
  8.4 0.0 copy-done.1
  8.4 0.0 copy-done.2
  8.4 0.2 subtract_convert_fusion
  8.6 7.0 %collective-permute-start.3 = (bf16[320,512]{1,0:T(8,128)(2,1)S(1)}, bf16[320,512]{1,0:T(8,128)(2,1)S(1)}, u32[]{:S(2)}, u32[]{:S(2)}) collective-permute-start(bf16[320,512]{1,0:T(8,128)(2,1)S(1)} %subtract_convert_fusion), channel_id=1, source_target_pairs={{0,8},{8,0},{1,9},{9,1},{2,10},{10,2},{3,11},{11,3},{4,12},{12,4},... | collective-permute-start | bytes 983048 | tf_op jit(solution)/shard_map/ppermute | solution.py:216
  15.6 0.0 copy-done
  15.6 2.0 %collective-permute-start.4 = (bf16[128,512]{1,0:T(8,128)(2,1)S(1)}, bf16[128,512]{1,0:T(8,128)(2,1)S(1)}, u32[]{:S(2)}, u32[]{:S(2)}) collective-permute-start(bf16[128,512]{1,0:T(8,128)(2,1)S(1)} %bitcast.31), channel_id=1, source_target_pairs={{0,1},{1,0},{2,3},{3,2},{4,5},{5,4},{6,7},{7,6},{8,9},{9,8},{10,11... | collective-permute-start | bytes 393224 | tf_op jit(solution)/shard_map/ppermute | solution.py:221
  17.6 5.2 %collective-permute-start.2 = (bf16[128,512]{1,0:T(8,128)(2,1)S(1)}, bf16[128,512]{1,0:T(8,128)(2,1)S(1)}, u32[]{:S(2)}, u32[]{:S(2)}) collective-permute-start(bf16[128,512]{1,0:T(8,128)(2,1)S(1)} %bitcast.32), channel_id=1, source_target_pairs={{0,4},{2,6},{4,0},{6,2},{1,5},{3,7},{5,1},{7,3},{8,12},{10,14},{12... | collective-permute-start | bytes 393224 | tf_op jit(solution)/shard_map/ppermute | solution.py:196
  22.9 3.1 %collective-permute-start.1 = (bf16[128,512]{1,0:T(8,128)(2,1)S(1)}, bf16[128,512]{1,0:T(8,128)(2,1)S(1)}, u32[]{:S(2)}, u32[]{:S(2)}) collective-permute-start(bf16[128,512]{1,0:T(8,128)(2,1)S(1)} %bitcast.33), channel_id=1, source_target_pairs={{0,6},{2,0},{4,2},{6,4},{1,7},{3,1},{5,3},{7,5},{8,14},{10,8},{12,... | collective-permute-start | bytes 393224 | tf_op jit(solution)/shard_map/ppermute | solution.py:196
  25.9 2.8 %collective-permute-start = (bf16[128,512]{1,0:T(8,128)(2,1)S(1)}, bf16[128,512]{1,0:T(8,128)(2,1)S(1)}, u32[]{:S(2)}, u32[]{:S(2)}) collective-permute-start(bf16[128,512]{1,0:T(8,128)(2,1)S(1)} %bitcast.34), channel_id=1, source_target_pairs={{0,2},{2,4},{4,6},{6,0},{1,3},{3,5},{5,7},{7,1},{8,10},{10,12},{12... | collective-permute-start | bytes 393224 | tf_op jit(solution)/shard_map/ppermute | solution.py:196
  30.0 0.1 pad_add_fusion.1.tags_ref
  30.1 0.1 pad_add_fusion.place_ref
  30.2 0.0 collective-permute-done.2.n3
  30.2 0.5 collective-permute-done.1.n2
  30.7 3.7 %collective-permute-done.n1 = bf16[128,512]{1,0:T(8,128)(2,1)S(1)} collective-permute-done((bf16[128,512]{1,0:T(8,128)(2,1)S(1)}, bf16[128,512]{1,0:T(8,128)(2,1)S(1)}, u32[]{:S(2)}, u32[]{:S(2)}) %collective-permute-start) | collective-permute-done | bytes 131104 | tf_op jit(solution)/shard_map/ppermute | solution.py:196
  34.4 0.0 collective-permute-done.3
  34.6 0.0 collective-permute-done.4.f0
  34.6 1.9 %collective-permute-start.5 = (bf16[3,128,512]{2,1,0:T(8,128)(2,1)S(1)}, bf16[3,128,512]{2,1,0:T(8,128)(2,1)S(1)}, u32[]{:S(2)}, u32[]{:S(2)}) collective-permute-start(bf16[3,128,512]{2,1,0:T(8,128)(2,1)S(1)} %pad_maximum_fusion.1), channel_id=1, source_target_pairs={{0,1},{1,0},{2,3},{3,2},{4,5},{5,4},{6,7},{7,6},{8,9},{9,8},{10,11... | collective-permute-start | bytes 1179656 | tf_op jit(solution)/shard_map/ppermute | solution.py:227
  36.5 0.0 all-to-all-done.columns_ref
  36.5 1.2 %shard_map.105.acc_ref = f32[16,128]{1,0:T(8,128)S(1)} custom-call(s32[3]{0:T(128)S(1)} %pad_add_fusion.place_ref, s32[2]{0:T(128)S(1)} %pad_add_fusion.1.tags_ref, bf16[640,512]{1,0:T(8,128)(2,1)S(1)} %pad_maximum_fusion.delta_ref, bf16[8,128,640]{2,1,0:T(8,128)(2,1)S(1)} %all-to-all-done.columns_ref, bf16[128,512]{1,0:T(8,128)(2,1)S(1)} %bitcast.35, ...), custom_call_target="tpu_custom_call" | custom-call | tf_op jit(solution)/shard_map/pallas_call | solution.py:127
  37.7 0.5 collective-permute-done.5.f3
  38.2 1.2 %shard_map.106 = f32[8,16,128]{2,1,0:T(8,128)S(1)} custom-call(s32[3]{0:T(128)S(1)} %pad_add_fusion.place_ref, f32[16,128]{1,0:T(8,128)S(1)} %shard_map.105.acc_ref, bf16[640,512]{1,0:T(8,128)(2,1)S(1)} %pad_maximum_fusion.delta_ref, bf16[8,128,640]{2,1,0:T(8,128)(2,1)S(1)} %all-to-all-done.columns_ref, bf16[128,512]{1,0:T(8,128)(2,1)S(1)} %collective-permute-done.4.f0, ...), custom_call_target="tpu_custom_call" | custom-call | tf_op jit(solution)/shard_map/pallas_call | solution.py:134
  39.4 8.0 %all_to_all.30.small_ref = f32[8,16,128]{2,1,0:T(8,128)S(1)} all-to-all(f32[8,16,128]{2,1,0:T(8,128)S(1)} %shard_map.106), channel_id=1, replica_groups=mesh['yh'=2,'zh'=4,'zl'=4,'yl'=2,'x'=4,'c'=2] {'x','c'}, dimensions={0} | all-to-all | bytes 131072 | tf_op jit(solution)/shard_map/all_to_all | solution.py:23
  47.4 1.9 %shard_map.107 = (bf16[4,160,512]{2,1,0:T(8,128)(2,1)S(1)}, f32[8,128]{1,0:T(8,128)S(1)}) custom-call(s32[3]{0:T(128)S(1)} %pad_add_fusion.place_ref, f32[8,16,128]{2,1,0:T(8,128)S(1)} %all_to_all.30.small_ref, bf16[8,128,640]{2,1,0:T(8,128)(2,1)S(1)} %all-to-all-done.columns_ref, bf16[128,512]{1,0:T(8,128)(2,1)S(1)} %bitcast.36, ...), custom_call_target="tpu_custom_call" | custom-call | tf_op jit(solution)/shard_map/pallas_call | solution.py:181
  49.3 14.8 %all_to_all.31 = bf16[4,160,512]{2,1,0:T(8,128)(2,1)S(1)} all-to-all(bf16[4,160,512]{2,1,0:T(8,128)(2,1)S(1)} %get-tuple-element.17), channel_id=1, replica_groups=mesh['yh'=2,'zh'=4,'zl'=4,'yl'=2,'x'=4,'c'=2] {'yh','yl'}, dimensions={0} | all-to-all | bytes 1310720 | tf_op jit(solution)/shard_map/all_to_all | solution.py:23
  64.1 0.1 add_convert_fusion
  64.3 0.0 copy-start.4
  64.3 9.4 %all_to_all.32 = bf16[4,160,128]{2,1,0:T(8,128)(2,1)S(1)} all-to-all(bf16[4,160,128]{2,1,0:T(8,128)(2,1)S(1)} %bitcast.39), channel_id=1, replica_groups=mesh['yh'=2,'zh'=4,'zl'=4,'yl'=2,'x'=4,'c'=2] {'zl'}, dimensions={0} | all-to-all | bytes 327680 | tf_op jit(solution)/shard_map/all_to_all | solution.py:23
  73.8 25.7 %all_to_all.33 = bf16[4,160,128]{2,1,0:T(8,128)(2,1)S(1)} all-to-all(bf16[4,160,128]{2,1,0:T(8,128)(2,1)S(1)} %broadcast_in_dim.32), channel_id=1, replica_groups=mesh['yh'=2,'zh'=4,'zl'=4,'yl'=2,'x'=4,'c'=2] {'zh'}, dimensions={0} | all-to-all | bytes 327680 | tf_op jit(solution)/shard_map/all_to_all | solution.py:23
  99.5 0.8 broadcast_in_dim.34
  100.3 5.0 %all-to-all-start.5 = ((bf16[8,160,128]{2,1,0:T(8,128)(2,1)}), bf16[8,160,128]{2,1,0:T(8,128)(2,1)S(1)}, u32[]{:S(2)}, u32[]{:S(2)}) async-start(bf16[8,160,128]{2,1,0:T(8,128)(2,1)} %broadcast_in_dim.34), calls=%async_computation.5 | async-start | bytes 655360 | tf_op jit(solution)/shard_map/all_to_all | solution.py:23
  105.2 0.0 copy-done.4
  105.2 0.1 convert_reduce_fusion
  105.3 0.6 select_reduce_fusion
  106.0 9.9 %all-to-all-done.5.pieces_ref = bf16[8,160,128]{2,1,0:T(8,128)(2,1)S(1)} async-done(((bf16[8,160,128]{2,1,0:T(8,128)(2,1)}), bf16[8,160,128]{2,1,0:T(8,128)(2,1)S(1)}, u32[]{:S(2)}, u32[]{:S(2)}) %all-to-all-start.5) | async-done | bytes 327712 | tf_op jit(solution)/shard_map/all_to_all | solution.py:23
  115.8 0.9 shard_map.108
  (10 shorter events, 0.3 us)
Async XLA Ops:
  3.4 4.5 %copy-start.3 = (f32[4,320]{1,0:T(4,128)S(1)}, f32[4,320]{1,0:T(4,128)}, u32[]{:S(2)}) copy-start(f32[4,320]{1,0:T(4,128)} %param.12) | copy-start | bytes 15364
  3.4 5.0 %copy-start.1 = (bf16[320,512]{1,0:T(8,128)(2,1)S(1)}, bf16[320,512]{1,0:T(8,128)(2,1)}, u32[]{:S(2)}) copy-start(bf16[320,512]{1,0:T(8,128)(2,1)} %param.13) | copy-start | bytes 983044
  3.4 5.0 %copy-start.2 = (bf16[320,512]{1,0:T(8,128)(2,1)S(1)}, bf16[320,512]{1,0:T(8,128)(2,1)}, u32[]{:S(2)}) copy-start(bf16[320,512]{1,0:T(8,128)(2,1)} %param.11) | copy-start | bytes 983044
  3.4 33.1 %all-to-all-start = ((bf16[8,128,640]{2,1,0:T(8,128)(2,1)}), bf16[8,128,640]{2,1,0:T(8,128)(2,1)S(1)}, u32[]{:S(2)}, u32[]{:S(2)}) async-start(bf16[8,128,640]{2,1,0:T(8,128)(2,1)} %shard_map.104), calls=%async_computation | async-start | bytes 2621440 | tf_op jit(solution)/shard_map/all_to_all | solution.py:23
  7.8 7.8 %copy-start = (bf16[1,128,512]{2,1,0:T(8,128)(2,1)S(1)}, bf16[1,128,512]{2,1,0:T(8,128)(2,1)}, u32[]{:S(2)}) copy-start(bf16[1,128,512]{2,1,0:T(8,128)(2,1)} %param.14) | copy-start | bytes 393220
  8.6 25.9 %collective-permute-start.3 = (bf16[320,512]{1,0:T(8,128)(2,1)S(1)}, bf16[320,512]{1,0:T(8,128)(2,1)S(1)}, u32[]{:S(2)}, u32[]{:S(2)}) collective-permute-start(bf16[320,512]{1,0:T(8,128)(2,1)S(1)} %subtract_convert_fusion), channel_id=1, source_target_pairs={{0,8},{8,0},{1,9},{9,1},{2,10},{10,2},{3,11},{11,3},{4,12},{12,4},... | collective-permute-start | bytes 983048 | tf_op jit(solution)/shard_map/ppermute | solution.py:216
  15.6 18.9 %collective-permute-start.4 = (bf16[128,512]{1,0:T(8,128)(2,1)S(1)}, bf16[128,512]{1,0:T(8,128)(2,1)S(1)}, u32[]{:S(2)}, u32[]{:S(2)}) collective-permute-start(bf16[128,512]{1,0:T(8,128)(2,1)S(1)} %bitcast.31), channel_id=1, source_target_pairs={{0,1},{1,0},{2,3},{3,2},{4,5},{5,4},{6,7},{7,6},{8,9},{9,8},{10,11... | collective-permute-start | bytes 393224 | tf_op jit(solution)/shard_map/ppermute | solution.py:221
  17.6 12.6 %collective-permute-start.2 = (bf16[128,512]{1,0:T(8,128)(2,1)S(1)}, bf16[128,512]{1,0:T(8,128)(2,1)S(1)}, u32[]{:S(2)}, u32[]{:S(2)}) collective-permute-start(bf16[128,512]{1,0:T(8,128)(2,1)S(1)} %bitcast.32), channel_id=1, source_target_pairs={{0,4},{2,6},{4,0},{6,2},{1,5},{3,7},{5,1},{7,3},{8,12},{10,14},{12... | collective-permute-start | bytes 393224 | tf_op jit(solution)/shard_map/ppermute | solution.py:196
  22.9 7.8 %collective-permute-start.1 = (bf16[128,512]{1,0:T(8,128)(2,1)S(1)}, bf16[128,512]{1,0:T(8,128)(2,1)S(1)}, u32[]{:S(2)}, u32[]{:S(2)}) collective-permute-start(bf16[128,512]{1,0:T(8,128)(2,1)S(1)} %bitcast.33), channel_id=1, source_target_pairs={{0,6},{2,0},{4,2},{6,4},{1,7},{3,1},{5,3},{7,5},{8,14},{10,8},{12,... | collective-permute-start | bytes 393224 | tf_op jit(solution)/shard_map/ppermute | solution.py:196
  25.9 8.4 %collective-permute-start = (bf16[128,512]{1,0:T(8,128)(2,1)S(1)}, bf16[128,512]{1,0:T(8,128)(2,1)S(1)}, u32[]{:S(2)}, u32[]{:S(2)}) collective-permute-start(bf16[128,512]{1,0:T(8,128)(2,1)S(1)} %bitcast.34), channel_id=1, source_target_pairs={{0,2},{2,4},{4,6},{6,0},{1,3},{3,5},{5,7},{7,1},{8,10},{10,12},{12... | collective-permute-start | bytes 393224 | tf_op jit(solution)/shard_map/ppermute | solution.py:196
  34.6 3.6 %collective-permute-start.5 = (bf16[3,128,512]{2,1,0:T(8,128)(2,1)S(1)}, bf16[3,128,512]{2,1,0:T(8,128)(2,1)S(1)}, u32[]{:S(2)}, u32[]{:S(2)}) collective-permute-start(bf16[3,128,512]{2,1,0:T(8,128)(2,1)S(1)} %pad_maximum_fusion.1), channel_id=1, source_target_pairs={{0,1},{1,0},{2,3},{3,2},{4,5},{5,4},{6,7},{7,6},{8,9},{9,8},{10,11... | collective-permute-start | bytes 1179656 | tf_op jit(solution)/shard_map/ppermute | solution.py:227
  64.3 41.0 %copy-start.4 = (s32[1,8]{1,0:T(1,128)S(1)}, s32[1,8]{1,0:T(1,128)}, u32[]{:S(2)}) copy-start(s32[1,8]{1,0:T(1,128)} %param.16) | copy-start | bytes 100
  100.3 15.6 %all-to-all-start.5 = ((bf16[8,160,128]{2,1,0:T(8,128)(2,1)}), bf16[8,160,128]{2,1,0:T(8,128)(2,1)S(1)}, u32[]{:S(2)}, u32[]{:S(2)}) async-start(bf16[8,160,128]{2,1,0:T(8,128)(2,1)} %broadcast_in_dim.34), calls=%async_computation.5 | async-start | bytes 655360 | tf_op jit(solution)/shard_map/all_to_all | solution.py:23

commit v5 on v4

--- a/solution.py
+++ b/solution.py
@@ -231,7 +231,7 @@
     zl = lax.axis_size("zl")
     grad = grad.reshape(grad.shape[0], zl, features // zl).transpose(1, 0, 2)
     grad = wide_sum(exchange(grad, ("zl",))).astype(bf16)
-    grad = wide_sum(spread(grad, ("zh",))).astype(bf16)
+    grad = wide_sum(lax.all_gather(grad, "zh")).astype(bf16)
     grad = place_call(spread(grad, ("yh", "zl")), lax.axis_size("yh"))
     position = jnp.arange(seq_len, dtype=jnp.int32)
     reward = beta_scale * lax.dynamic_slice_in_dim(margin, me, 1, axis=0)

time: 117 us -> 114 us (0.974)
  the two profiles are of different devices: /device:TPU:8 before, /device:TPU:2 now
where the time goes in v5:
time: 114 us
  blocking collectives  55.2 us (48%)
  starting transfers between devices  28.7 us (25%)
  waiting for transfers between devices  17.2 us (15%)
  Pallas kernels  7.88 us (7%)
  between operations  2.13 us (2%)
  local copies, waits for them, and re-layouts  1.4 us (1%)
  other arithmetic  1.31 us (1%)
    all_to_all x3, blocking collectives, exchange(): return lax.all_to_all(pieces, axes, 0, 0, tiled=False)  30.9 us
    all_gather x1, blocking collectives, on_device(): grad = wide_sum(lax.all_gather(grad, 'zh')).astype(bf16)  24.3 us
    all_to_all x2, starting transfers between devices, exchange(): return lax.all_to_all(pieces, axes, 0, 0, tiled=False)  13 us
    ppermute x3, starting transfers between devices, shifted(): return [block] + [lax.ppermute(block, axes, pair) for pair in pairs]  9.86 us
    all_to_all x2, waiting for transfers between devices, exchange(): return lax.all_to_all(pieces, axes, 0, 0, tiled=False)  9.8 us
    ppermute x3, waiting for transfers between devices, shifted(): return [block] + [lax.ppermute(block, axes, pair) for pair in pairs]  6.87 us
    pallas_call x1, Pallas kernels, norm_call(): pl.pallas_call(norm_kernel, grid=(seq_len // block,), in_specs=[pl.BlockS...  2.73 us
  transfers between devices with their start and end apart: 8, of which 4 were waited for; matrix products, arithmetic and copies ran while one was open for 2% of the time, Pallas kernels for 1%

profile of v5, /device:TPU:2, one launch (start us, length us, event | category | flops | bytes accessed | tf_op | source)
XLA Modules:
  0.0 113.8 jit_solution(10184219785008094731)
XLA Ops:
  0.6 2.7 %shard_map.104 = bf16[8,128,640]{2,1,0:T(8,128)(2,1)} custom-call(bf16[128,5120]{1,0:T(8,128)(2,1)} %bitcast.36, f32[1,5120]{1,0:T(1,128)} %bitcast.38), custom_call_target="tpu_custom_call" | custom-call | tf_op jit(solution)/shard_map/pallas_call | solution.py:55
  3.4 0.0 copy-start.3
  3.4 0.0 copy-start.1
  3.4 0.0 copy-start.2
  3.4 9.5 %all-to-all-start = ((bf16[8,128,640]{2,1,0:T(8,128)(2,1)}), bf16[8,128,640]{2,1,0:T(8,128)(2,1)S(1)}, u32[]{:S(2)}, u32[]{:S(2)}) async-start(bf16[8,128,640]{2,1,0:T(8,128)(2,1)} %shard_map.104), calls=%async_computation | async-start | bytes 2621440 | tf_op jit(solution)/shard_map/all_to_all | solution.py:23
  12.9 0.0 copy-done.3
  12.9 0.0 copy-start
  12.9 0.1 copy.15
  13.1 0.4 broadcast_in_dim.21
  13.5 0.0 copy-done.1
  13.5 0.0 copy-done.2
  13.5 0.2 subtract_convert_fusion
  13.6 1.9 %collective-permute-start.3 = (bf16[320,512]{1,0:T(8,128)(2,1)S(1)}, bf16[320,512]{1,0:T(8,128)(2,1)S(1)}, u32[]{:S(2)}, u32[]{:S(2)}) collective-permute-start(bf16[320,512]{1,0:T(8,128)(2,1)S(1)} %subtract_convert_fusion), channel_id=1, source_target_pairs={{0,8},{8,0},{1,9},{9,1},{2,10},{10,2},{3,11},{11,3},{4,12},{12,4},... | collective-permute-start | bytes 983048 | tf_op jit(solution)/shard_map/ppermute | solution.py:216
  15.6 0.0 copy-done
  15.6 2.1 %collective-permute-start.4 = (bf16[128,512]{1,0:T(8,128)(2,1)S(1)}, bf16[128,512]{1,0:T(8,128)(2,1)S(1)}, u32[]{:S(2)}, u32[]{:S(2)}) collective-permute-start(bf16[128,512]{1,0:T(8,128)(2,1)S(1)} %bitcast.29), channel_id=1, source_target_pairs={{0,1},{1,0},{2,3},{3,2},{4,5},{5,4},{6,7},{7,6},{8,9},{9,8},{10,11... | collective-permute-start | bytes 393224 | tf_op jit(solution)/shard_map/ppermute | solution.py:221
  17.6 4.0 %collective-permute-start.2 = (bf16[128,512]{1,0:T(8,128)(2,1)S(1)}, bf16[128,512]{1,0:T(8,128)(2,1)S(1)}, u32[]{:S(2)}, u32[]{:S(2)}) collective-permute-start(bf16[128,512]{1,0:T(8,128)(2,1)S(1)} %bitcast.30), channel_id=1, source_target_pairs={{0,4},{2,6},{4,0},{6,2},{1,5},{3,7},{5,1},{7,3},{8,12},{10,14},{12... | collective-permute-start | bytes 393224 | tf_op jit(solution)/shard_map/ppermute | solution.py:196
  21.7 3.4 %collective-permute-start.1 = (bf16[128,512]{1,0:T(8,128)(2,1)S(1)}, bf16[128,512]{1,0:T(8,128)(2,1)S(1)}, u32[]{:S(2)}, u32[]{:S(2)}) collective-permute-start(bf16[128,512]{1,0:T(8,128)(2,1)S(1)} %bitcast.31), channel_id=1, source_target_pairs={{0,6},{2,0},{4,2},{6,4},{1,7},{3,1},{5,3},{7,5},{8,14},{10,8},{12,... | collective-permute-start | bytes 393224 | tf_op jit(solution)/shard_map/ppermute | solution.py:196
  25.0 2.5 %collective-permute-start = (bf16[128,512]{1,0:T(8,128)(2,1)S(1)}, bf16[128,512]{1,0:T(8,128)(2,1)S(1)}, u32[]{:S(2)}, u32[]{:S(2)}) collective-permute-start(bf16[128,512]{1,0:T(8,128)(2,1)S(1)} %bitcast.32), channel_id=1, source_target_pairs={{0,2},{2,4},{4,6},{6,0},{1,3},{3,5},{5,7},{7,1},{8,10},{10,12},{12... | collective-permute-start | bytes 393224 | tf_op jit(solution)/shard_map/ppermute | solution.py:196
  28.8 0.1 pad_add_fusion.1.tags_ref
  28.9 0.1 pad_add_fusion.place_ref
  29.0 4.6 %collective-permute-done.2.n3 = bf16[128,512]{1,0:T(8,128)(2,1)S(1)} collective-permute-done((bf16[128,512]{1,0:T(8,128)(2,1)S(1)}, bf16[128,512]{1,0:T(8,128)(2,1)S(1)}, u32[]{:S(2)}, u32[]{:S(2)}) %collective-permute-start.2) | collective-permute-done | bytes 131104 | tf_op jit(solution)/shard_map/ppermute | solution.py:196
  33.6 2.3 %collective-permute-done.1.n2 = bf16[128,512]{1,0:T(8,128)(2,1)S(1)} collective-permute-done((bf16[128,512]{1,0:T(8,128)(2,1)S(1)}, bf16[128,512]{1,0:T(8,128)(2,1)S(1)}, u32[]{:S(2)}, u32[]{:S(2)}) %collective-permute-start.1) | collective-permute-done | bytes 131104 | tf_op jit(solution)/shard_map/ppermute | solution.py:196
  35.8 0.0 collective-permute-done.n1
  35.9 0.0 collective-permute-done.3
  36.0 0.0 collective-permute-done.4.f0
  36.0 1.9 %collective-permute-start.5 = (bf16[3,128,512]{2,1,0:T(8,128)(2,1)S(1)}, bf16[3,128,512]{2,1,0:T(8,128)(2,1)S(1)}, u32[]{:S(2)}, u32[]{:S(2)}) collective-permute-start(bf16[3,128,512]{2,1,0:T(8,128)(2,1)S(1)} %pad_maximum_fusion.1), channel_id=1, source_target_pairs={{0,1},{1,0},{2,3},{3,2},{4,5},{5,4},{6,7},{7,6},{8,9},{9,8},{10,11... | collective-permute-start | bytes 1179656 | tf_op jit(solution)/shard_map/ppermute | solution.py:227
  38.0 0.0 all-to-all-done.columns_ref
  38.0 1.2 %shard_map.105.acc_ref = f32[16,128]{1,0:T(8,128)S(1)} custom-call(s32[3]{0:T(128)S(1)} %pad_add_fusion.place_ref, s32[2]{0:T(128)S(1)} %pad_add_fusion.1.tags_ref, bf16[640,512]{1,0:T(8,128)(2,1)S(1)} %pad_maximum_fusion.delta_ref, bf16[8,128,640]{2,1,0:T(8,128)(2,1)S(1)} %all-to-all-done.columns_ref, bf16[128,512]{1,0:T(8,128)(2,1)S(1)} %bitcast.33, ...), custom_call_target="tpu_custom_call" | custom-call | tf_op jit(solution)/shard_map/pallas_call | solution.py:127
  39.2 0.5 collective-permute-done.5.f3
  39.6 1.2 %shard_map.106 = f32[8,16,128]{2,1,0:T(8,128)S(1)} custom-call(s32[3]{0:T(128)S(1)} %pad_add_fusion.place_ref, f32[16,128]{1,0:T(8,128)S(1)} %shard_map.105.acc_ref, bf16[640,512]{1,0:T(8,128)(2,1)S(1)} %pad_maximum_fusion.delta_ref, bf16[8,128,640]{2,1,0:T(8,128)(2,1)S(1)} %all-to-all-done.columns_ref, bf16[128,512]{1,0:T(8,128)(2,1)S(1)} %collective-permute-done.4.f0, ...), custom_call_target="tpu_custom_call" | custom-call | tf_op jit(solution)/shard_map/pallas_call | solution.py:134
  40.8 8.0 %all_to_all.25.small_ref = f32[8,16,128]{2,1,0:T(8,128)S(1)} all-to-all(f32[8,16,128]{2,1,0:T(8,128)S(1)} %shard_map.106), channel_id=1, replica_groups=mesh['yh'=2,'zh'=4,'zl'=4,'yl'=2,'x'=4,'c'=2] {'x','c'}, dimensions={0} | all-to-all | bytes 131072 | tf_op jit(solution)/shard_map/all_to_all | solution.py:23
  48.8 1.9 %shard_map.107 = (bf16[4,160,512]{2,1,0:T(8,128)(2,1)S(1)}, f32[8,128]{1,0:T(8,128)S(1)}) custom-call(s32[3]{0:T(128)S(1)} %pad_add_fusion.place_ref, f32[8,16,128]{2,1,0:T(8,128)S(1)} %all_to_all.25.small_ref, bf16[8,128,640]{2,1,0:T(8,128)(2,1)S(1)} %all-to-all-done.columns_ref, bf16[128,512]{1,0:T(8,128)(2,1)S(1)} %bitcast.34, ...), custom_call_target="tpu_custom_call" | custom-call | tf_op jit(solution)/shard_map/pallas_call | solution.py:181
  50.8 13.5 %all_to_all.26 = bf16[4,160,512]{2,1,0:T(8,128)(2,1)S(1)} all-to-all(bf16[4,160,512]{2,1,0:T(8,128)(2,1)S(1)} %get-tuple-element.17), channel_id=1, replica_groups=mesh['yh'=2,'zh'=4,'zl'=4,'yl'=2,'x'=4,'c'=2] {'yh','yl'}, dimensions={0} | all-to-all | bytes 1310720 | tf_op jit(solution)/shard_map/all_to_all | solution.py:23
  64.2 0.1 add_convert_fusion
  64.3 0.0 copy-start.4
  64.4 9.4 %all_to_all.27 = bf16[4,160,128]{2,1,0:T(8,128)(2,1)S(1)} all-to-all(bf16[4,160,128]{2,1,0:T(8,128)(2,1)S(1)} %bitcast.37), channel_id=1, replica_groups=mesh['yh'=2,'zh'=4,'zl'=4,'yl'=2,'x'=4,'c'=2] {'zl'}, dimensions={0} | all-to-all | bytes 327680 | tf_op jit(solution)/shard_map/all_to_all | solution.py:23
  73.8 24.3 %all_gather.4 = bf16[4,160,128]{2,1,0:T(8,128)(2,1)S(1)} all-gather(bf16[1,160,128]{2,1,0:T(8,128)(2,1)S(1)} %add_convert_fusion.2), channel_id=1, replica_groups=mesh['yh'=2,'zh'=4,'zl'=4,'yl'=2,'x'=4,'c'=2] {'zh'}, dimensions={0}, use_global_device_ids=true | all-gather | bytes 204800 | tf_op jit(solution)/shard_map/all_gather | solution.py:234
  98.2 0.8 broadcast_in_dim.24
  98.9 3.4 %all-to-all-start.4 = ((bf16[8,160,128]{2,1,0:T(8,128)(2,1)}), bf16[8,160,128]{2,1,0:T(8,128)(2,1)S(1)}, u32[]{:S(2)}, u32[]{:S(2)}) async-start(bf16[8,160,128]{2,1,0:T(8,128)(2,1)} %broadcast_in_dim.24), calls=%async_computation.4 | async-start | bytes 655360 | tf_op jit(solution)/shard_map/all_to_all | solution.py:23
  102.4 0.0 copy-done.4
  102.4 0.1 convert_reduce_fusion
  102.5 0.6 select_reduce_fusion
  103.1 9.8 %all-to-all-done.4.pieces_ref = bf16[8,160,128]{2,1,0:T(8,128)(2,1)S(1)} async-done(((bf16[8,160,128]{2,1,0:T(8,128)(2,1)}), bf16[8,160,128]{2,1,0:T(8,128)(2,1)S(1)}, u32[]{:S(2)}, u32[]{:S(2)}) %all-to-all-start.4) | async-done | bytes 327712 | tf_op jit(solution)/shard_map/all_to_all | solution.py:23
  112.9 0.9 shard_map.108
  (9 shorter events, 0.3 us)
Async XLA Ops:
  3.4 9.5 %copy-start.3 = (f32[4,320]{1,0:T(4,128)S(1)}, f32[4,320]{1,0:T(4,128)}, u32[]{:S(2)}) copy-start(f32[4,320]{1,0:T(4,128)} %param.12) | copy-start | bytes 15364
  3.4 10.1 %copy-start.1 = (bf16[320,512]{1,0:T(8,128)(2,1)S(1)}, bf16[320,512]{1,0:T(8,128)(2,1)}, u32[]{:S(2)}) copy-start(bf16[320,512]{1,0:T(8,128)(2,1)} %param.13) | copy-start | bytes 983044
  3.4 10.1 %copy-start.2 = (bf16[320,512]{1,0:T(8,128)(2,1)S(1)}, bf16[320,512]{1,0:T(8,128)(2,1)}, u32[]{:S(2)}) copy-start(bf16[320,512]{1,0:T(8,128)(2,1)} %param.11) | copy-start | bytes 983044
  3.4 34.6 %all-to-all-start = ((bf16[8,128,640]{2,1,0:T(8,128)(2,1)}), bf16[8,128,640]{2,1,0:T(8,128)(2,1)S(1)}, u32[]{:S(2)}, u32[]{:S(2)}) async-start(bf16[8,128,640]{2,1,0:T(8,128)(2,1)} %shard_map.104), calls=%async_computation | async-start | bytes 2621440 | tf_op jit(solution)/shard_map/all_to_all | solution.py:23
  12.9 2.7 %copy-start = (bf16[1,128,512]{2,1,0:T(8,128)(2,1)S(1)}, bf16[1,128,512]{2,1,0:T(8,128)(2,1)}, u32[]{:S(2)}) copy-start(bf16[1,128,512]{2,1,0:T(8,128)(2,1)} %param.14) | copy-start | bytes 393220
  13.6 22.3 %collective-permute-start.3 = (bf16[320,512]{1,0:T(8,128)(2,1)S(1)}, bf16[320,512]{1,0:T(8,128)(2,1)S(1)}, u32[]{:S(2)}, u32[]{:S(2)}) collective-permute-start(bf16[320,512]{1,0:T(8,128)(2,1)S(1)} %subtract_convert_fusion), channel_id=1, source_target_pairs={{0,8},{8,0},{1,9},{9,1},{2,10},{10,2},{3,11},{11,3},{4,12},{12,4},... | collective-permute-start | bytes 983048 | tf_op jit(solution)/shard_map/ppermute | solution.py:216
  15.6 20.4 %collective-permute-start.4 = (bf16[128,512]{1,0:T(8,128)(2,1)S(1)}, bf16[128,512]{1,0:T(8,128)(2,1)S(1)}, u32[]{:S(2)}, u32[]{:S(2)}) collective-permute-start(bf16[128,512]{1,0:T(8,128)(2,1)S(1)} %bitcast.29), channel_id=1, source_target_pairs={{0,1},{1,0},{2,3},{3,2},{4,5},{5,4},{6,7},{7,6},{8,9},{9,8},{10,11... | collective-permute-start | bytes 393224 | tf_op jit(solution)/shard_map/ppermute | solution.py:221
  17.6 15.9 %collective-permute-start.2 = (bf16[128,512]{1,0:T(8,128)(2,1)S(1)}, bf16[128,512]{1,0:T(8,128)(2,1)S(1)}, u32[]{:S(2)}, u32[]{:S(2)}) collective-permute-start(bf16[128,512]{1,0:T(8,128)(2,1)S(1)} %bitcast.30), channel_id=1, source_target_pairs={{0,4},{2,6},{4,0},{6,2},{1,5},{3,7},{5,1},{7,3},{8,12},{10,14},{12... | collective-permute-start | bytes 393224 | tf_op jit(solution)/shard_map/ppermute | solution.py:196
  21.7 14.2 %collective-permute-start.1 = (bf16[128,512]{1,0:T(8,128)(2,1)S(1)}, bf16[128,512]{1,0:T(8,128)(2,1)S(1)}, u32[]{:S(2)}, u32[]{:S(2)}) collective-permute-start(bf16[128,512]{1,0:T(8,128)(2,1)S(1)} %bitcast.31), channel_id=1, source_target_pairs={{0,6},{2,0},{4,2},{6,4},{1,7},{3,1},{5,3},{7,5},{8,14},{10,8},{12,... | collective-permute-start | bytes 393224 | tf_op jit(solution)/shard_map/ppermute | solution.py:196
  25.0 10.8 %collective-permute-start = (bf16[128,512]{1,0:T(8,128)(2,1)S(1)}, bf16[128,512]{1,0:T(8,128)(2,1)S(1)}, u32[]{:S(2)}, u32[]{:S(2)}) collective-permute-start(bf16[128,512]{1,0:T(8,128)(2,1)S(1)} %bitcast.32), channel_id=1, source_target_pairs={{0,2},{2,4},{4,6},{6,0},{1,3},{3,5},{5,7},{7,1},{8,10},{10,12},{12... | collective-permute-start | bytes 393224 | tf_op jit(solution)/shard_map/ppermute | solution.py:196
  36.0 3.6 %collective-permute-start.5 = (bf16[3,128,512]{2,1,0:T(8,128)(2,1)S(1)}, bf16[3,128,512]{2,1,0:T(8,128)(2,1)S(1)}, u32[]{:S(2)}, u32[]{:S(2)}) collective-permute-start(bf16[3,128,512]{2,1,0:T(8,128)(2,1)S(1)} %pad_maximum_fusion.1), channel_id=1, source_target_pairs={{0,1},{1,0},{2,3},{3,2},{4,5},{5,4},{6,7},{7,6},{8,9},{9,8},{10,11... | collective-permute-start | bytes 1179656 | tf_op jit(solution)/shard_map/ppermute | solution.py:227
  64.3 38.1 %copy-start.4 = (s32[1,8]{1,0:T(1,128)S(1)}, s32[1,8]{1,0:T(1,128)}, u32[]{:S(2)}) copy-start(s32[1,8]{1,0:T(1,128)} %param.16) | copy-start | bytes 100
  98.9 14.0 %all-to-all-start.4 = ((bf16[8,160,128]{2,1,0:T(8,128)(2,1)}), bf16[8,160,128]{2,1,0:T(8,128)(2,1)S(1)}, u32[]{:S(2)}, u32[]{:S(2)}) async-start(bf16[8,160,128]{2,1,0:T(8,128)(2,1)} %broadcast_in_dim.24), calls=%async_computation.4 | async-start | bytes 655360 | tf_op jit(solution)/shard_map/all_to_all | solution.py:23

commit v6 on v5

--- a/solution.py
+++ b/solution.py
@@ -83,65 +83,49 @@
     )(pieces)
 
 
-def seq_of(place_ref, j, swapped):
-    x_from = lax.rem(place_ref[0] + (OFFSETS[j] + 4), 4)
-    core = place_ref[2]
-    return 2 * x_from + (1 - core if swapped else core)
-
-
-def add_margins(acc, place_ref, columns_ref, delta, reads, swapped):
-    row = lax.broadcasted_iota(jnp.int32, acc.shape, 0)
-    for j in range(4):
-        seq = seq_of(place_ref, j, swapped)
+def held_rows(place_ref, own_ref, far_ref, moved_ref):
+    x, core = place_ref[0], place_ref[2]
+    held = [(2 * x + core, own_ref), (2 * x + 1 - core, far_ref)]
+    for j, offset in enumerate(OFFSETS[1:]):
+        x_from = lax.rem(x + (offset + 4), 4)
+        held += [(2 * x_from + c, moved_ref.at[c, j]) for c in range(2)]
+    return held
+
+
+def margin_kernel(place_ref, tags_ref, delta_ref, columns_ref, own_ref, far_ref, moved_ref, out_ref):
+    groups, seq_len, _ = columns_ref.shape
+    shape = (2 * groups, seq_len)
+    row = lax.broadcasted_iota(jnp.int32, shape, 0)
+    lane = lax.broadcasted_iota(jnp.int32, shape, 1)
+    me = 2 * place_ref[0] + place_ref[2]
+    tags = jnp.where(lane < seq_len // 2, tags_ref[0], tags_ref[1]).astype(f32)
+    acc = jnp.where(row == me + groups, tags, 0.0)
+    delta = delta_ref[...]
+    for seq, read_ref in held_rows(place_ref, own_ref, far_ref, moved_ref):
         value = jnp.dot(columns_ref[seq], delta, preferred_element_type=f32)
-        prod = value * reads[j].astype(f32)
+        prod = value * read_ref[...].astype(f32)
         part = prod[:, :128]
         for k in range(1, prod.shape[1] // 128):
             part = part + prod[:, 128 * k : 128 * (k + 1)]
         line = jnp.sum(part.T, axis=0, keepdims=True)
         acc = jnp.where(row == seq, line, acc)
-    return acc
-
-
-def near_kernel(place_ref, tags_ref, delta_ref, columns_ref, n0, n1, n2, n3, acc_ref):
-    groups, seq_len, _ = columns_ref.shape
-    row = lax.broadcasted_iota(jnp.int32, acc_ref.shape, 0)
-    lane = lax.broadcasted_iota(jnp.int32, acc_ref.shape, 1)
-    me = seq_of(place_ref, 0, False)
-    tags = jnp.where(lane < seq_len // 2, tags_ref[0], tags_ref[1]).astype(f32)
-    acc = jnp.where(row == me + groups, tags, 0.0)
-    reads = [ref[...] for ref in (n0, n1, n2, n3)]
-    acc_ref[...] = add_margins(acc, place_ref, columns_ref, delta_ref[...], reads, False)
-
-
-def far_kernel(place_ref, acc_ref, delta_ref, columns_ref, f0, f3, out_ref):
-    reads = [f0[...]] + [f3[j] for j in range(3)]
-    acc = add_margins(acc_ref[...], place_ref, columns_ref, delta_ref[...], reads, True)
     for g in range(out_ref.shape[0]):
         out_ref[g] = acc
 
 
-def margin_call(place, tags, delta, columns, near, far):
+def margin_call(place, tags, delta, columns, reads):
     groups, seq_len, _ = columns.shape
-    params = pltpu.CompilerParams(vmem_limit_bytes=VMEM_LIMIT)
-    acc = pl.pallas_call(
-        near_kernel,
-        in_specs=[SMEM, SMEM] + [VMEM] * 6,
-        out_specs=VMEM,
-        out_shape=jax.ShapeDtypeStruct((2 * groups, seq_len), f32),
-        compiler_params=params,
-    )(place, tags, delta, columns, *near)
-    return pl.pallas_call(
-        far_kernel,
-        in_specs=[SMEM] + [VMEM] * 5,
+    return pl.pallas_call(
+        margin_kernel,
+        in_specs=[SMEM, SMEM] + [VMEM] * 5,
         out_specs=VMEM,
         out_shape=jax.ShapeDtypeStruct((groups, 2 * groups, seq_len), f32),
-        compiler_params=params,
-    )(place, acc, delta, columns, *far)
+        compiler_params=pltpu.CompilerParams(vmem_limit_bytes=VMEM_LIMIT),
+    )(place, tags, delta, columns, *reads)
 
 
 def grad_kernel(
-    place_ref, small_ref, columns_ref, n0, n1, n2, n3, f0, f3, grad_ref, margin_ref, slope_ref
+    place_ref, small_ref, columns_ref, own_ref, far_ref, moved_ref, grad_ref, margin_ref, slope_ref
 ):
     groups, seq_len, share = columns_ref.shape
     small = small_ref[0]
@@ -155,14 +139,10 @@
     weight = beta_scale * (1.0 / (1.0 + jnp.exp(-total)) - label)
     row = lax.broadcasted_iota(jnp.int32, weight.shape, 0)
     position = lax.broadcasted_iota(jnp.int32, (seq_len, 1), 0).astype(f32)
-    near = [ref[...] for ref in (n0, n1, n2, n3)]
-    far = [f0[...]] + [f3[j] for j in range(3)]
-    for swapped, reads in ((False, near), (True, far)):
-        for j in range(4):
-            seq = seq_of(place_ref, j, swapped)
-            w = jnp.sum(jnp.where(row == seq, weight, 0.0), axis=0, keepdims=True)
-            live = position < jnp.sum(jnp.where(row == seq, length, 0.0), axis=0, keepdims=True)
-            slope_ref[seq] = (jnp.where(live, w, 0.0) * reads[j].astype(f32)).astype(bf16)
+    for seq, read_ref in held_rows(place_ref, own_ref, far_ref, moved_ref):
+        w = jnp.sum(jnp.where(row == seq, weight, 0.0), axis=0, keepdims=True)
+        live = position < jnp.sum(jnp.where(row == seq, length, 0.0), axis=0, keepdims=True)
+        slope_ref[seq] = (jnp.where(live, w, 0.0) * read_ref[...].astype(f32)).astype(bf16)
     columns = columns_ref[...].reshape(groups * seq_len, share)
     slope = slope_ref[...].reshape(groups * seq_len, slope_ref.shape[2])
     grad = lax.dot_general(
@@ -175,12 +155,12 @@
             grad_ref[2 * yh + yl] = grad[at : at + part]
 
 
-def grad_call(place, small, columns, near, far):
+def grad_call(place, small, columns, reads):
     groups, seq_len, share = columns.shape
-    features = near[0].shape[1]
+    features = reads[0].shape[1]
     return pl.pallas_call(
         grad_kernel,
-        in_specs=[SMEM] + [VMEM] * 8,
+        in_specs=[SMEM] + [VMEM] * 5,
         out_specs=[VMEM, VMEM],
         out_shape=[
             jax.ShapeDtypeStruct((4, share // 4, features), bf16),
@@ -188,7 +168,7 @@
         ],
         scratch_shapes=[pltpu.VMEM((groups, seq_len, features), bf16)],
         compiler_params=pltpu.CompilerParams(vmem_limit_bytes=VMEM_LIMIT),
-    )(place, small, columns, *near, *far)
+    )(place, small, columns, *reads)
 
 
 def shifted(block, axes):
@@ -224,9 +204,9 @@
     moved, delta, far_own, place, tags = lax.optimization_barrier(
         (moved, delta, far_own, place, tags)
     )
-    far = [far_own, lax.ppermute(moved, "c", swap)]
-    small = exchange(margin_call(place, tags, delta, columns, near, far), GROUP)
-    grad, margin = grad_call(place, small, columns, near, far)
+    reads = [own, far_own, lax.all_gather(moved, "c")]
+    small = exchange(margin_call(place, tags, delta, columns, reads), GROUP)
+    grad, margin = grad_call(place, small, columns, reads)
     grad = wide_sum(exchange(grad, ("yh", "yl"))).astype(bf16)
     zl = lax.axis_size("zl")
     grad = grad.reshape(grad.shape[0], zl, features // zl).transpose(1, 0, 2)

time: 114 us -> 114 us (level)
  the two profiles are of different devices: /device:TPU:2 before, /device:TPU:8 now
where the time goes in v6:
time: 114 us; the launch traced here: 113 us
  blocking collectives  59 us (52%)
  starting transfers between devices  28 us (25%)
  waiting for transfers between devices  14 us (12%)
  Pallas kernels  7.15 us (6%)
  between operations  2.13 us (2%)
  local copies, waits for them, and re-layouts  1.4 us (1%)
  other arithmetic  1.31 us (1%)
    all_to_all x3, blocking collectives, exchange(): return lax.all_to_all(pieces, axes, 0, 0, tiled=False)  32.3 us
    all_gather x1, blocking collectives, on_device(): grad = wide_sum(lax.all_gather(grad, 'zh')).astype(bf16)  24.4 us
    ppermute x3, starting transfers between devices, shifted(): return [block] + [lax.ppermute(block, axes, pair) for pair in pairs]  11.1 us
    all_to_all x2, waiting for transfers between devices, exchange(): return lax.all_to_all(pieces, axes, 0, 0, tiled=False)  9.8 us
    all_to_all x2, starting transfers between devices, exchange(): return lax.all_to_all(pieces, axes, 0, 0, tiled=False)  7.88 us
    ppermute x1, starting transfers between devices, on_device(): delta_other = lax.ppermute(delta, 'yl', swap)  7.04 us
    ppermute x3, waiting for transfers between devices, shifted(): return [block] + [lax.ppermute(block, axes, pair) for pair in pairs]  4.21 us
    pallas_call x1, Pallas kernels, norm_call(): pl.pallas_call(norm_kernel, grid=(seq_len // block,), in_specs=[pl.BlockS...  2.74 us
  transfers between devices with their start and end apart: 7, of which 3 were waited for; matrix products, arithmetic and copies ran while one was open for 2% of the time, Pallas kernels for 0%

profile of v6, /device:TPU:8, one launch (start us, length us, event | category | flops | bytes accessed | tf_op | source)
XLA Modules:
  0.0 113.0 jit_solution(8516733813841370694)
XLA Ops:
  0.6 2.7 %shard_map.104 = bf16[8,128,640]{2,1,0:T(8,128)(2,1)} custom-call(bf16[128,5120]{1,0:T(8,128)(2,1)} %bitcast.36, f32[1,5120]{1,0:T(1,128)} %bitcast.41), custom_call_target="tpu_custom_call" | custom-call | tf_op jit(solution)/shard_map/pallas_call | solution.py:55
  3.4 0.0 copy-start.3
  3.4 0.0 copy-start.1
  3.4 0.0 copy-start.2
  3.4 4.4 %all-to-all-start = ((bf16[8,128,640]{2,1,0:T(8,128)(2,1)}), bf16[8,128,640]{2,1,0:T(8,128)(2,1)S(1)}, u32[]{:S(2)}, u32[]{:S(2)}) async-start(bf16[8,128,640]{2,1,0:T(8,128)(2,1)} %shard_map.104), calls=%async_computation | async-start | bytes 2621440 | tf_op jit(solution)/shard_map/all_to_all | solution.py:23
  7.8 0.0 copy-done.3
  7.8 0.0 copy-start
  7.8 0.1 copy.15
  8.0 0.4 broadcast_in_dim.21
  8.4 0.0 copy-done.1
  8.4 0.0 copy-done.2
  8.4 0.2 subtract_convert_fusion
  8.6 7.0 %collective-permute-start.3 = (bf16[320,512]{1,0:T(8,128)(2,1)S(1)}, bf16[320,512]{1,0:T(8,128)(2,1)S(1)}, u32[]{:S(2)}, u32[]{:S(2)}) collective-permute-start(bf16[320,512]{1,0:T(8,128)(2,1)S(1)} %subtract_convert_fusion), channel_id=1, source_target_pairs={{0,8},{8,0},{1,9},{9,1},{2,10},{10,2},{3,11},{11,3},{4,12},{12,4},... | collective-permute-start | bytes 983048 | tf_op jit(solution)/shard_map/ppermute | solution.py:196
  15.6 0.0 copy-done
  15.6 2.0 %collective-permute-start.4 = (bf16[128,512]{1,0:T(8,128)(2,1)S(1)}, bf16[128,512]{1,0:T(8,128)(2,1)S(1)}, u32[]{:S(2)}, u32[]{:S(2)}) collective-permute-start(bf16[128,512]{1,0:T(8,128)(2,1)S(1)} %bitcast.29), channel_id=1, source_target_pairs={{0,1},{1,0},{2,3},{3,2},{4,5},{5,4},{6,7},{7,6},{8,9},{9,8},{10,11... | collective-permute-start | bytes 393224 | tf_op jit(solution)/shard_map/ppermute | solution.py:201
  17.6 5.2 %collective-permute-start.2 = (bf16[128,512]{1,0:T(8,128)(2,1)S(1)}, bf16[128,512]{1,0:T(8,128)(2,1)S(1)}, u32[]{:S(2)}, u32[]{:S(2)}) collective-permute-start(bf16[128,512]{1,0:T(8,128)(2,1)S(1)} %bitcast.30), channel_id=1, source_target_pairs={{0,4},{2,6},{4,0},{6,2},{1,5},{3,7},{5,1},{7,3},{8,12},{10,14},{12... | collective-permute-start | bytes 393224 | tf_op jit(solution)/shard_map/ppermute | solution.py:176
  22.9 3.1 %collective-permute-start.1 = (bf16[128,512]{1,0:T(8,128)(2,1)S(1)}, bf16[128,512]{1,0:T(8,128)(2,1)S(1)}, u32[]{:S(2)}, u32[]{:S(2)}) collective-permute-start(bf16[128,512]{1,0:T(8,128)(2,1)S(1)} %bitcast.31), channel_id=1, source_target_pairs={{0,6},{2,0},{4,2},{6,4},{1,7},{3,1},{5,3},{7,5},{8,14},{10,8},{12,... | collective-permute-start | bytes 393224 | tf_op jit(solution)/shard_map/ppermute | solution.py:176
  25.9 2.8 %collective-permute-start = (bf16[128,512]{1,0:T(8,128)(2,1)S(1)}, bf16[128,512]{1,0:T(8,128)(2,1)S(1)}, u32[]{:S(2)}, u32[]{:S(2)}) collective-permute-start(bf16[128,512]{1,0:T(8,128)(2,1)S(1)} %bitcast.32), channel_id=1, source_target_pairs={{0,2},{2,4},{4,6},{6,0},{1,3},{3,5},{5,7},{7,1},{8,10},{10,12},{12... | collective-permute-start | bytes 393224 | tf_op jit(solution)/shard_map/ppermute | solution.py:176
  30.0 0.1 pad_add_fusion.1.tags_ref
  30.1 0.1 pad_add_fusion.place_ref
  30.2 0.0 collective-permute-done.2
  30.2 0.5 collective-permute-done.1
  30.7 3.7 %collective-permute-done = bf16[128,512]{1,0:T(8,128)(2,1)S(1)} collective-permute-done((bf16[128,512]{1,0:T(8,128)(2,1)S(1)}, bf16[128,512]{1,0:T(8,128)(2,1)S(1)}, u32[]{:S(2)}, u32[]{:S(2)}) %collective-permute-start) | collective-permute-done | bytes 131104 | tf_op jit(solution)/shard_map/ppermute | solution.py:176
  34.4 0.0 collective-permute-done.3
  34.6 0.0 collective-permute-done.4.far_ref
  34.6 2.4 %all-gather = bf16[6,128,512]{2,1,0:T(8,128)(2,1)S(1)} all-gather(bf16[3,128,512]{2,1,0:T(8,128)(2,1)S(1)} %pad_maximum_fusion.1), channel_id=2, replica_groups=mesh['yh'=2,'zh'=4,'zl'=4,'yl'=2,'x'=4,'c'=2] {'c'}, dimensions={0}, use_global_device_ids=true | all-gather | bytes 1179648 | tf_op jit(solution)/shard_map/all_gather | solution.py:207
  36.9 0.0 all-to-all-done.columns_ref
  36.9 1.6 %shard_map.105 = f32[8,16,128]{2,1,0:T(8,128)S(1)} custom-call(s32[3]{0:T(128)S(1)} %pad_add_fusion.place_ref, s32[2]{0:T(128)S(1)} %pad_add_fusion.1.tags_ref, bf16[640,512]{1,0:T(8,128)(2,1)S(1)} %pad_maximum_fusion.delta_ref, bf16[8,128,640]{2,1,0:T(8,128)(2,1)S(1)} %all-to-all-done.columns_ref, bf16[128,512]{1,0:T(8,128)(2,1)S(1)} %bitcast.33, ...), custom_call_target="tpu_custom_call" | custom-call | tf_op jit(solution)/shard_map/pallas_call | solution.py:118
  38.6 8.0 %all_to_all.25.small_ref = f32[8,16,128]{2,1,0:T(8,128)S(1)} all-to-all(f32[8,16,128]{2,1,0:T(8,128)S(1)} %shard_map.105), channel_id=1, replica_groups=mesh['yh'=2,'zh'=4,'zl'=4,'yl'=2,'x'=4,'c'=2] {'x','c'}, dimensions={0} | all-to-all | bytes 131072 | tf_op jit(solution)/shard_map/all_to_all | solution.py:23
  46.6 1.9 %shard_map.106 = (bf16[4,160,512]{2,1,0:T(8,128)(2,1)S(1)}, f32[8,128]{1,0:T(8,128)S(1)}) custom-call(s32[3]{0:T(128)S(1)} %pad_add_fusion.place_ref, f32[8,16,128]{2,1,0:T(8,128)S(1)} %all_to_all.25.small_ref, bf16[8,128,640]{2,1,0:T(8,128)(2,1)S(1)} %all-to-all-done.columns_ref, bf16[128,512]{1,0:T(8,128)(2,1)S(1)} %bitcast.34, ...), custom_call_target="tpu_custom_call" | custom-call | tf_op jit(solution)/shard_map/pallas_call | solution.py:161
  48.5 14.8 %all_to_all.26 = bf16[4,160,512]{2,1,0:T(8,128)(2,1)S(1)} all-to-all(bf16[4,160,512]{2,1,0:T(8,128)(2,1)S(1)} %get-tuple-element.17), channel_id=1, replica_groups=mesh['yh'=2,'zh'=4,'zl'=4,'yl'=2,'x'=4,'c'=2] {'yh','yl'}, dimensions={0} | all-to-all | bytes 1310720 | tf_op jit(solution)/shard_map/all_to_all | solution.py:23
  63.3 0.1 add_convert_fusion
  63.4 0.0 copy-start.4
  63.5 9.4 %all_to_all.27 = bf16[4,160,128]{2,1,0:T(8,128)(2,1)S(1)} all-to-all(bf16[4,160,128]{2,1,0:T(8,128)(2,1)S(1)} %bitcast.37), channel_id=1, replica_groups=mesh['yh'=2,'zh'=4,'zl'=4,'yl'=2,'x'=4,'c'=2] {'zl'}, dimensions={0} | all-to-all | bytes 327680 | tf_op jit(solution)/shard_map/all_to_all | solution.py:23
  73.0 24.4 %all_gather.12 = bf16[4,160,128]{2,1,0:T(8,128)(2,1)S(1)} all-gather(bf16[1,160,128]{2,1,0:T(8,128)(2,1)S(1)} %add_convert_fusion.2), channel_id=1, replica_groups=mesh['yh'=2,'zh'=4,'zl'=4,'yl'=2,'x'=4,'c'=2] {'zh'}, dimensions={0}, use_global_device_ids=true | all-gather | bytes 204800 | tf_op jit(solution)/shard_map/all_gather | solution.py:214
  97.4 0.8 broadcast_in_dim.24
  98.2 3.4 %all-to-all-start.4 = ((bf16[8,160,128]{2,1,0:T(8,128)(2,1)}), bf16[8,160,128]{2,1,0:T(8,128)(2,1)S(1)}, u32[]{:S(2)}, u32[]{:S(2)}) async-start(bf16[8,160,128]{2,1,0:T(8,128)(2,1)} %broadcast_in_dim.24), calls=%async_computation.4 | async-start | bytes 655360 | tf_op jit(solution)/shard_map/all_to_all | solution.py:23
  101.6 0.0 copy-done.4
  101.6 0.1 convert_reduce_fusion
  101.7 0.6 select_reduce_fusion
  102.3 9.8 %all-to-all-done.4.pieces_ref = bf16[8,160,128]{2,1,0:T(8,128)(2,1)S(1)} async-done(((bf16[8,160,128]{2,1,0:T(8,128)(2,1)}), bf16[8,160,128]{2,1,0:T(8,128)(2,1)S(1)}, u32[]{:S(2)}, u32[]{:S(2)}) %all-to-all-start.4) | async-done | bytes 327712 | tf_op jit(solution)/shard_map/all_to_all | solution.py:23
  112.1 0.9 shard_map.107
  (9 shorter events, 0.3 us)
Async XLA Ops:
  3.4 4.5 %copy-start.3 = (f32[4,320]{1,0:T(4,128)S(1)}, f32[4,320]{1,0:T(4,128)}, u32[]{:S(2)}) copy-start(f32[4,320]{1,0:T(4,128)} %param.12) | copy-start | bytes 15364
  3.4 5.0 %copy-start.1 = (bf16[320,512]{1,0:T(8,128)(2,1)S(1)}, bf16[320,512]{1,0:T(8,128)(2,1)}, u32[]{:S(2)}) copy-start(bf16[320,512]{1,0:T(8,128)(2,1)} %param.13) | copy-start | bytes 983044
  3.4 5.0 %copy-start.2 = (bf16[320,512]{1,0:T(8,128)(2,1)S(1)}, bf16[320,512]{1,0:T(8,128)(2,1)}, u32[]{:S(2)}) copy-start(bf16[320,512]{1,0:T(8,128)(2,1)} %param.11) | copy-start | bytes 983044
  3.4 33.6 %all-to-all-start = ((bf16[8,128,640]{2,1,0:T(8,128)(2,1)}), bf16[8,128,640]{2,1,0:T(8,128)(2,1)S(1)}, u32[]{:S(2)}, u32[]{:S(2)}) async-start(bf16[8,128,640]{2,1,0:T(8,128)(2,1)} %shard_map.104), calls=%async_computation | async-start | bytes 2621440 | tf_op jit(solution)/shard_map/all_to_all | solution.py:23
  7.8 7.8 %copy-start = (bf16[1,128,512]{2,1,0:T(8,128)(2,1)S(1)}, bf16[1,128,512]{2,1,0:T(8,128)(2,1)}, u32[]{:S(2)}) copy-start(bf16[1,128,512]{2,1,0:T(8,128)(2,1)} %param.14) | copy-start | bytes 393220
  8.6 25.9 %collective-permute-start.3 = (bf16[320,512]{1,0:T(8,128)(2,1)S(1)}, bf16[320,512]{1,0:T(8,128)(2,1)S(1)}, u32[]{:S(2)}, u32[]{:S(2)}) collective-permute-start(bf16[320,512]{1,0:T(8,128)(2,1)S(1)} %subtract_convert_fusion), channel_id=1, source_target_pairs={{0,8},{8,0},{1,9},{9,1},{2,10},{10,2},{3,11},{11,3},{4,12},{12,4},... | collective-permute-start | bytes 983048 | tf_op jit(solution)/shard_map/ppermute | solution.py:196
  15.6 18.9 %collective-permute-start.4 = (bf16[128,512]{1,0:T(8,128)(2,1)S(1)}, bf16[128,512]{1,0:T(8,128)(2,1)S(1)}, u32[]{:S(2)}, u32[]{:S(2)}) collective-permute-start(bf16[128,512]{1,0:T(8,128)(2,1)S(1)} %bitcast.29), channel_id=1, source_target_pairs={{0,1},{1,0},{2,3},{3,2},{4,5},{5,4},{6,7},{7,6},{8,9},{9,8},{10,11... | collective-permute-start | bytes 393224 | tf_op jit(solution)/shard_map/ppermute | solution.py:201
  17.6 12.6 %collective-permute-start.2 = (bf16[128,512]{1,0:T(8,128)(2,1)S(1)}, bf16[128,512]{1,0:T(8,128)(2,1)S(1)}, u32[]{:S(2)}, u32[]{:S(2)}) collective-permute-start(bf16[128,512]{1,0:T(8,128)(2,1)S(1)} %bitcast.30), channel_id=1, source_target_pairs={{0,4},{2,6},{4,0},{6,2},{1,5},{3,7},{5,1},{7,3},{8,12},{10,14},{12... | collective-permute-start | bytes 393224 | tf_op jit(solution)/shard_map/ppermute | solution.py:176
  22.9 7.8 %collective-permute-start.1 = (bf16[128,512]{1,0:T(8,128)(2,1)S(1)}, bf16[128,512]{1,0:T(8,128)(2,1)S(1)}, u32[]{:S(2)}, u32[]{:S(2)}) collective-permute-start(bf16[128,512]{1,0:T(8,128)(2,1)S(1)} %bitcast.31), channel_id=1, source_target_pairs={{0,6},{2,0},{4,2},{6,4},{1,7},{3,1},{5,3},{7,5},{8,14},{10,8},{12,... | collective-permute-start | bytes 393224 | tf_op jit(solution)/shard_map/ppermute | solution.py:176
  25.9 8.4 %collective-permute-start = (bf16[128,512]{1,0:T(8,128)(2,1)S(1)}, bf16[128,512]{1,0:T(8,128)(2,1)S(1)}, u32[]{:S(2)}, u32[]{:S(2)}) collective-permute-start(bf16[128,512]{1,0:T(8,128)(2,1)S(1)} %bitcast.32), channel_id=1, source_target_pairs={{0,2},{2,4},{4,6},{6,0},{1,3},{3,5},{5,7},{7,1},{8,10},{10,12},{12... | collective-permute-start | bytes 393224 | tf_op jit(solution)/shard_map/ppermute | solution.py:176
  63.4 38.2 %copy-start.4 = (s32[1,8]{1,0:T(1,128)S(1)}, s32[1,8]{1,0:T(1,128)}, u32[]{:S(2)}) copy-start(s32[1,8]{1,0:T(1,128)} %param.16) | copy-start | bytes 100
  98.2 14.0 %all-to-all-start.4 = ((bf16[8,160,128]{2,1,0:T(8,128)(2,1)}), bf16[8,160,128]{2,1,0:T(8,128)(2,1)S(1)}, u32[]{:S(2)}, u32[]{:S(2)}) async-start(bf16[8,160,128]{2,1,0:T(8,128)(2,1)} %broadcast_in_dim.24), calls=%async_computation.4 | async-start | bytes 655360 | tf_op jit(solution)/shard_map/all_to_all | solution.py:23

commit v7 on v6

--- a/solution.py
+++ b/solution.py
@@ -65,22 +65,37 @@
     )(hidden, gain)
 
 
-def place_kernel(pieces_ref, out_ref):
+def place_kernel(sums_ref, pieces_ref, out_ref, steps_ref):
     for k in range(pieces_ref.shape[0]):
         out_ref[:, 128 * k : 128 * (k + 1)] = pieces_ref[k].astype(f32)
-
-
-def place_call(pieces, halves):
+    count = steps_ref.shape[1]
+    sums = sums_ref[...][:, :count]
+    row = lax.broadcasted_iota(jnp.int32, (count, count), 0)
+    column = lax.broadcasted_iota(jnp.int32, (count, count), 1)
+    steps_ref[...] = jnp.sum(jnp.where(row == column, sums, 0.0), axis=0, keepdims=True)
+
+
+def place_call(sums, pieces, halves):
     count, part, lanes = pieces.shape
     across = count // halves
+    steps = (1, sums.shape[0])
     return pl.pallas_call(
         place_kernel,
         grid=(halves,),
-        in_specs=[pl.BlockSpec((across, part, lanes), lambda i: (i, 0, 0))],
-        out_specs=pl.BlockSpec((part, across * lanes), lambda i: (i, 0)),
-        out_shape=jax.ShapeDtypeStruct((halves * part, across * lanes), f32),
+        in_specs=[
+            pl.BlockSpec(sums.shape, lambda i: (0, 0)),
+            pl.BlockSpec((across, part, lanes), lambda i: (i, 0, 0)),
+        ],
+        out_specs=[
+            pl.BlockSpec((part, across * lanes), lambda i: (i, 0)),
+            pl.BlockSpec(steps, lambda i: (0, 0)),
+        ],
+        out_shape=[
+            jax.ShapeDtypeStruct((halves * part, across * lanes), f32),
+            jax.ShapeDtypeStruct(steps, f32),
+        ],
         compiler_params=pltpu.CompilerParams(vmem_limit_bytes=VMEM_LIMIT),
-    )(pieces)
+    )(sums, pieces)
 
 
 def held_rows(place_ref, own_ref, far_ref, moved_ref):
@@ -125,7 +140,8 @@
 
 
 def grad_kernel(
-    place_ref, small_ref, columns_ref, own_ref, far_ref, moved_ref, grad_ref, margin_ref, slope_ref
+    place_ref, bounds_ref, small_ref, columns_ref, own_ref, far_ref, moved_ref,
+    grad_ref, sums_ref, slope_ref
 ):
     groups, seq_len, share = columns_ref.shape
     small = small_ref[0]
@@ -134,7 +150,20 @@
     label, length = small[groups:, :1], small[groups:, seq_len - 1 :]
     lane = lax.broadcasted_iota(jnp.int32, (groups, seq_len), 1).astype(f32)
     margin = jnp.where(lane < length, small[:groups], 0.0)
-    margin_ref[...] = margin
+    own = lax.broadcasted_iota(jnp.int32, margin.shape, 0) == 2 * place_ref[0] + place_ref[2]
+    reward = beta_scale * jnp.sum(jnp.where(own, margin, 0.0), axis=0, keepdims=True)
+    steps = bounds_ref.shape[1]
+    square = (steps, steps)
+    step = lax.broadcasted_iota(jnp.int32, square, 0)
+    column = lax.broadcasted_iota(jnp.int32, square, 1)
+    first = jnp.broadcast_to(bounds_ref[...].astype(f32), square)
+    begin = jnp.sum(jnp.where(column == step, first, 0.0), axis=1, keepdims=True)
+    end = jnp.sum(jnp.where(column == step + 1, first, 0.0), axis=1, keepdims=True)
+    end = jnp.where(step[:, :1] == steps - 1, float(seq_len), end)
+    at = lax.broadcasted_iota(jnp.int32, (steps, seq_len), 1).astype(f32)
+    inside = (at >= begin) & (at < end)
+    sums = jnp.sum(jnp.where(inside, reward, 0.0), axis=1, keepdims=True)
+    sums_ref[...] = jnp.broadcast_to(sums, sums_ref.shape)
     total = jnp.sum(beta_scale * margin, axis=1, keepdims=True)
     weight = beta_scale * (1.0 / (1.0 + jnp.exp(-total)) - label)
     row = lax.broadcasted_iota(jnp.int32, weight.shape, 0)
@@ -155,20 +184,20 @@
             grad_ref[2 * yh + yl] = grad[at : at + part]
 
 
-def grad_call(place, small, columns, reads):
+def grad_call(place, bounds, small, columns, reads):
     groups, seq_len, share = columns.shape
     features = reads[0].shape[1]
     return pl.pallas_call(
         grad_kernel,
-        in_specs=[SMEM] + [VMEM] * 5,
+        in_specs=[SMEM] + [VMEM] * 6,
         out_specs=[VMEM, VMEM],
         out_shape=[
             jax.ShapeDtypeStruct((4, share // 4, features), bf16),
-            jax.ShapeDtypeStruct((groups, seq_len), f32),
+            jax.ShapeDtypeStruct((bounds.shape[1], seq_len), f32),
         ],
         scratch_shapes=[pltpu.VMEM((groups, seq_len, features), bf16)],
         compiler_params=pltpu.CompilerParams(vmem_limit_bytes=VMEM_LIMIT),
-    )(place, small, columns, *reads)
+    )(place, bounds, small, columns, *reads)
 
 
 def shifted(block, axes):
@@ -182,10 +211,8 @@
     seq_len, width = hidden.shape[1:]
     features = readout.shape[2]
     head_size = features // scale_ref.shape[0]
-    steps_count = bounds.shape[1]
     group = lax.axis_size(GROUP)
     x, y_lo, core = lax.axis_index("x"), lax.axis_index("yl"), lax.axis_index("c")
-    me = 2 * x + core
     place = jnp.stack([x, y_lo, core]).astype(jnp.int32)
     swap = [(0, 1), (1, 0)]
     pieces = norm_call(hidden[0], norm_gain[None], group)
@@ -206,18 +233,14 @@
     )
     reads = [own, far_own, lax.all_gather(moved, "c")]
     small = exchange(margin_call(place, tags, delta, columns, reads), GROUP)
-    grad, margin = grad_call(place, small, columns, reads)
+    grad, sums = grad_call(place, bounds, small, columns, reads)
     grad = wide_sum(exchange(grad, ("yh", "yl"))).astype(bf16)
     zl = lax.axis_size("zl")
     grad = grad.reshape(grad.shape[0], zl, features // zl).transpose(1, 0, 2)
     grad = wide_sum(exchange(grad, ("zl",))).astype(bf16)
     grad = wide_sum(lax.all_gather(grad, "zh")).astype(bf16)
-    grad = place_call(spread(grad, ("yh", "zl")), lax.axis_size("yh"))
-    position = jnp.arange(seq_len, dtype=jnp.int32)
-    reward = beta_scale * lax.dynamic_slice_in_dim(margin, me, 1, axis=0)
-    step_index = jnp.sum((position[:, None] >= bounds[0][None, :]).astype(jnp.int32), axis=-1) - 1
-    onehot = (step_index[:, None] == jnp.arange(steps_count)[None, :]).astype(f32)
-    step_rewards = jnp.sum(reward[0][:, None] * onehot, axis=0)[None]
+    grad = spread(grad, ("yh", "zl"))
+    grad, step_rewards = place_call(sums, grad, lax.axis_size("yh"))
     return step_rewards, grad
 
 

time: 114 us -> 112 us (0.982)
  blocking collectives: 59 us -> 72.5 us
  waiting for transfers between devices: 14 us -> 4.22 us
  starting transfers between devices: 28 us -> 24.6 us
    all_to_all x3 -> x4, blocking collectives: 32.3 us -> 45.9 us  [exchange(): return lax.all_to_all(pieces, axes, 0, 0, tiled=False)]
    all_to_all x2 -> x1, waiting for transfers between devices: 9.8 us -> 0.01 us  [exchange(): return lax.all_to_all(pieces, axes, 0, 0, tiled=False)]
    all_to_all x2 -> x1, starting transfers between devices: 7.88 us -> 4.44 us  [exchange(): return lax.all_to_all(pieces, axes, 0, 0, tiled=False)]
  transfers between devices with their start and end apart: 7 -> 6, of which waited for: 3 -> 2; matrix products, arithmetic and copies ran while one was open for 2% -> 1% of each run, Pallas kernels for 0% -> 0%
where the time goes in v7:
time: 112 us
  blocking collectives  72.5 us (65%)
  starting transfers between devices  24.6 us (22%)
  Pallas kernels  7.2 us (6%)
  waiting for transfers between devices  4.22 us (4%)
  between operations  2.1 us (2%)
    all_to_all x4, blocking collectives, exchange(): return lax.all_to_all(pieces, axes, 0, 0, tiled=False)  45.9 us
    all_gather x1, blocking collectives, on_device(): grad = wide_sum(lax.all_gather(grad, 'zh')).astype(bf16)  24.3 us
    ppermute x3, starting transfers between devices, shifted(): return [block] + [lax.ppermute(block, axes, pair) for pair in pairs]  11.1 us
    ppermute x1, starting transfers between devices, on_device(): delta_other = lax.ppermute(delta, 'yl', swap)  7.04 us
    all_to_all x1, starting transfers between devices, exchange(): return lax.all_to_all(pieces, axes, 0, 0, tiled=False)  4.44 us
    ppermute x3, waiting for transfers between devices, shifted(): return [block] + [lax.ppermute(block, axes, pair) for pair in pairs]  4.21 us
    pallas_call x1, Pallas kernels, norm_call(): pl.pallas_call(norm_kernel, grid=(seq_len // block,), in_specs=[pl.BlockS...  2.78 us
    all_gather x1, blocking collectives, on_device(): reads = [own, far_own, lax.all_gather(moved, 'c')]  2.37 us
  transfers between devices with their start and end apart: 6, of which 2 were waited for; matrix products, arithmetic and copies ran while one was open for 1% of the time, Pallas kernels for 0%

profile of v7, /device:TPU:8, one launch (start us, length us, event | category | flops | bytes accessed | tf_op | source)
XLA Modules:
  0.0 111.9 jit_solution(15179518892149095945)
XLA Ops:
  0.6 2.8 %shard_map.104 = bf16[8,128,640]{2,1,0:T(8,128)(2,1)} custom-call(bf16[128,5120]{1,0:T(8,128)(2,1)} %bitcast.32, f32[1,5120]{1,0:T(1,128)} %bitcast.37), custom_call_target="tpu_custom_call" | custom-call | tf_op jit(solution)/shard_map/pallas_call | solution.py:55
  3.4 0.0 copy-start.4
  3.4 0.0 copy-start.2
  3.4 0.0 copy-start.3
  3.4 4.4 %all-to-all-start = ((bf16[8,128,640]{2,1,0:T(8,128)(2,1)}), bf16[8,128,640]{2,1,0:T(8,128)(2,1)S(1)}, u32[]{:S(2)}, u32[]{:S(2)}) async-start(bf16[8,128,640]{2,1,0:T(8,128)(2,1)} %shard_map.104), calls=%async_computation | async-start | bytes 2621440 | tf_op jit(solution)/shard_map/all_to_all | solution.py:23
  7.9 0.0 copy-done.4
  7.9 0.0 copy-start
  7.9 0.1 copy.13
  8.0 0.4 broadcast_in_dim.15
  8.4 0.0 copy-done.2
  8.4 0.0 copy-done.3
  8.4 0.2 subtract_convert_fusion
  8.6 7.0 %collective-permute-start.3 = (bf16[320,512]{1,0:T(8,128)(2,1)S(1)}, bf16[320,512]{1,0:T(8,128)(2,1)S(1)}, u32[]{:S(2)}, u32[]{:S(2)}) collective-permute-start(bf16[320,512]{1,0:T(8,128)(2,1)S(1)} %subtract_convert_fusion), channel_id=1, source_target_pairs={{0,8},{8,0},{1,9},{9,1},{2,10},{10,2},{3,11},{11,3},{4,12},{12,4},... | collective-permute-start | bytes 983048 | tf_op jit(solution)/shard_map/ppermute | solution.py:223
  15.7 0.0 copy-done
  15.7 2.0 %collective-permute-start.4 = (bf16[128,512]{1,0:T(8,128)(2,1)S(1)}, bf16[128,512]{1,0:T(8,128)(2,1)S(1)}, u32[]{:S(2)}, u32[]{:S(2)}) collective-permute-start(bf16[128,512]{1,0:T(8,128)(2,1)S(1)} %bitcast.25), channel_id=1, source_target_pairs={{0,1},{1,0},{2,3},{3,2},{4,5},{5,4},{6,7},{7,6},{8,9},{9,8},{10,11... | collective-permute-start | bytes 393224 | tf_op jit(solution)/shard_map/ppermute | solution.py:228
  17.7 5.2 %collective-permute-start.2 = (bf16[128,512]{1,0:T(8,128)(2,1)S(1)}, bf16[128,512]{1,0:T(8,128)(2,1)S(1)}, u32[]{:S(2)}, u32[]{:S(2)}) collective-permute-start(bf16[128,512]{1,0:T(8,128)(2,1)S(1)} %bitcast.26), channel_id=1, source_target_pairs={{0,4},{2,6},{4,0},{6,2},{1,5},{3,7},{5,1},{7,3},{8,12},{10,14},{12... | collective-permute-start | bytes 393224 | tf_op jit(solution)/shard_map/ppermute | solution.py:205
  22.9 3.1 %collective-permute-start.1 = (bf16[128,512]{1,0:T(8,128)(2,1)S(1)}, bf16[128,512]{1,0:T(8,128)(2,1)S(1)}, u32[]{:S(2)}, u32[]{:S(2)}) collective-permute-start(bf16[128,512]{1,0:T(8,128)(2,1)S(1)} %bitcast.27), channel_id=1, source_target_pairs={{0,6},{2,0},{4,2},{6,4},{1,7},{3,1},{5,3},{7,5},{8,14},{10,8},{12,... | collective-permute-start | bytes 393224 | tf_op jit(solution)/shard_map/ppermute | solution.py:205
  26.0 2.8 %collective-permute-start = (bf16[128,512]{1,0:T(8,128)(2,1)S(1)}, bf16[128,512]{1,0:T(8,128)(2,1)S(1)}, u32[]{:S(2)}, u32[]{:S(2)}) collective-permute-start(bf16[128,512]{1,0:T(8,128)(2,1)S(1)} %bitcast.28), channel_id=1, source_target_pairs={{0,2},{2,4},{4,6},{6,0},{1,3},{3,5},{5,7},{7,1},{8,10},{10,12},{12... | collective-permute-start | bytes 393224 | tf_op jit(solution)/shard_map/ppermute | solution.py:205
  30.1 0.1 pad_add_fusion.1.tags_ref
  30.1 0.1 pad_add_fusion.place_ref
  30.2 0.0 collective-permute-done.2
  30.2 0.5 collective-permute-done.1
  30.8 3.7 %collective-permute-done = bf16[128,512]{1,0:T(8,128)(2,1)S(1)} collective-permute-done((bf16[128,512]{1,0:T(8,128)(2,1)S(1)}, bf16[128,512]{1,0:T(8,128)(2,1)S(1)}, u32[]{:S(2)}, u32[]{:S(2)}) %collective-permute-start) | collective-permute-done | bytes 131104 | tf_op jit(solution)/shard_map/ppermute | solution.py:205
  34.5 0.0 collective-permute-done.3
  34.6 0.0 collective-permute-done.4.far_ref
  34.6 2.4 %all-gather = bf16[6,128,512]{2,1,0:T(8,128)(2,1)S(1)} all-gather(bf16[3,128,512]{2,1,0:T(8,128)(2,1)S(1)} %pad_maximum_fusion.1), channel_id=2, replica_groups=mesh['yh'=2,'zh'=4,'zl'=4,'yl'=2,'x'=4,'c'=2] {'c'}, dimensions={0}, use_global_device_ids=true | all-gather | bytes 1179648 | tf_op jit(solution)/shard_map/all_gather | solution.py:234
  37.0 0.0 all-to-all-done.columns_ref
  37.0 0.0 copy-start.1
  37.0 1.6 %shard_map.105 = f32[8,16,128]{2,1,0:T(8,128)S(1)} custom-call(s32[3]{0:T(128)S(1)} %pad_add_fusion.place_ref, s32[2]{0:T(128)S(1)} %pad_add_fusion.1.tags_ref, bf16[640,512]{1,0:T(8,128)(2,1)S(1)} %pad_maximum_fusion.delta_ref, bf16[8,128,640]{2,1,0:T(8,128)(2,1)S(1)} %all-to-all-done.columns_ref, bf16[128,512]{1,0:T(8,128)(2,1)S(1)} %bitcast.29, ...), custom_call_target="tpu_custom_call" | custom-call | tf_op jit(solution)/shard_map/pallas_call | solution.py:133
  38.6 8.0 %all_to_all.25.small_ref = f32[8,16,128]{2,1,0:T(8,128)S(1)} all-to-all(f32[8,16,128]{2,1,0:T(8,128)S(1)} %shard_map.105), channel_id=1, replica_groups=mesh['yh'=2,'zh'=4,'zl'=4,'yl'=2,'x'=4,'c'=2] {'x','c'}, dimensions={0} | all-to-all | bytes 131072 | tf_op jit(solution)/shard_map/all_to_all | solution.py:23
  46.6 0.0 copy-done.1
  46.6 1.9 %shard_map.106 = (bf16[4,160,512]{2,1,0:T(8,128)(2,1)S(1)}, f32[8,128]{1,0:T(8,128)S(1)}) custom-call(s32[3]{0:T(128)S(1)} %pad_add_fusion.place_ref, s32[1,8]{1,0:T(1,128)S(1)} %copy-done.1, f32[8,16,128]{2,1,0:T(8,128)S(1)} %all_to_all.25.small_ref, bf16[8,128,640]{2,1,0:T(8,128)(2,1)S(1)} %all-to-all-done.columns_ref, bf16[128,512]{1,0:T(8,128)(2,1)S(1)} %bitcast.30, ...), custom_call_target="tpu_custom_call" | custom-call | tf_op jit(solution)/shard_map/pallas_call | solution.py:190
  48.5 14.8 %all_to_all.26 = bf16[4,160,512]{2,1,0:T(8,128)(2,1)S(1)} all-to-all(bf16[4,160,512]{2,1,0:T(8,128)(2,1)S(1)} %get-tuple-element.19), channel_id=1, replica_groups=mesh['yh'=2,'zh'=4,'zl'=4,'yl'=2,'x'=4,'c'=2] {'yh','yl'}, dimensions={0} | all-to-all | bytes 1310720 | tf_op jit(solution)/shard_map/all_to_all | solution.py:23
  63.4 0.1 add_convert_fusion
  63.6 9.4 %all_to_all.27 = bf16[4,160,128]{2,1,0:T(8,128)(2,1)S(1)} all-to-all(bf16[4,160,128]{2,1,0:T(8,128)(2,1)S(1)} %bitcast.33), channel_id=1, replica_groups=mesh['yh'=2,'zh'=4,'zl'=4,'yl'=2,'x'=4,'c'=2] {'zl'}, dimensions={0} | all-to-all | bytes 327680 | tf_op jit(solution)/shard_map/all_to_all | solution.py:23
  73.0 24.3 %all_gather.12 = bf16[4,160,128]{2,1,0:T(8,128)(2,1)S(1)} all-gather(bf16[1,160,128]{2,1,0:T(8,128)(2,1)S(1)} %add_convert_fusion.2), channel_id=1, replica_groups=mesh['yh'=2,'zh'=4,'zl'=4,'yl'=2,'x'=4,'c'=2] {'zh'}, dimensions={0}, use_global_device_ids=true | all-gather | bytes 204800 | tf_op jit(solution)/shard_map/all_gather | solution.py:241
  97.4 13.6 %all_to_all.28.pieces_ref = bf16[8,160,128]{2,1,0:T(8,128)(2,1)S(1)} all-to-all(bf16[8,160,128]{2,1,0:T(8,128)(2,1)S(1)} %broadcast_in_dim.17), channel_id=1, replica_groups=mesh['yh'=2,'zh'=4,'zl'=4,'yl'=2,'x'=4,'c'=2] {'yh','zl'}, dimensions={0} | all-to-all | bytes 655360 | tf_op jit(solution)/shard_map/all_to_all | solution.py:23
  111.0 0.9 shard_map.107
  (8 shorter events, 0.3 us)
Async XLA Ops:
  3.4 4.5 %copy-start.4 = (f32[4,320]{1,0:T(4,128)S(1)}, f32[4,320]{1,0:T(4,128)}, u32[]{:S(2)}) copy-start(f32[4,320]{1,0:T(4,128)} %param.12) | copy-start | bytes 15364
  3.4 5.0 %copy-start.2 = (bf16[320,512]{1,0:T(8,128)(2,1)S(1)}, bf16[320,512]{1,0:T(8,128)(2,1)}, u32[]{:S(2)}) copy-start(bf16[320,512]{1,0:T(8,128)(2,1)} %param.13) | copy-start | bytes 983044
  3.4 5.0 %copy-start.3 = (bf16[320,512]{1,0:T(8,128)(2,1)S(1)}, bf16[320,512]{1,0:T(8,128)(2,1)}, u32[]{:S(2)}) copy-start(bf16[320,512]{1,0:T(8,128)(2,1)} %param.11) | copy-start | bytes 983044
  3.4 33.6 %all-to-all-start = ((bf16[8,128,640]{2,1,0:T(8,128)(2,1)}), bf16[8,128,640]{2,1,0:T(8,128)(2,1)S(1)}, u32[]{:S(2)}, u32[]{:S(2)}) async-start(bf16[8,128,640]{2,1,0:T(8,128)(2,1)} %shard_map.104), calls=%async_computation | async-start | bytes 2621440 | tf_op jit(solution)/shard_map/all_to_all | solution.py:23
  7.9 7.8 %copy-start = (bf16[1,128,512]{2,1,0:T(8,128)(2,1)S(1)}, bf16[1,128,512]{2,1,0:T(8,128)(2,1)}, u32[]{:S(2)}) copy-start(bf16[1,128,512]{2,1,0:T(8,128)(2,1)} %param.14) | copy-start | bytes 393220
  8.6 25.9 %collective-permute-start.3 = (bf16[320,512]{1,0:T(8,128)(2,1)S(1)}, bf16[320,512]{1,0:T(8,128)(2,1)S(1)}, u32[]{:S(2)}, u32[]{:S(2)}) collective-permute-start(bf16[320,512]{1,0:T(8,128)(2,1)S(1)} %subtract_convert_fusion), channel_id=1, source_target_pairs={{0,8},{8,0},{1,9},{9,1},{2,10},{10,2},{3,11},{11,3},{4,12},{12,4},... | collective-permute-start | bytes 983048 | tf_op jit(solution)/shard_map/ppermute | solution.py:223
  15.7 18.9 %collective-permute-start.4 = (bf16[128,512]{1,0:T(8,128)(2,1)S(1)}, bf16[128,512]{1,0:T(8,128)(2,1)S(1)}, u32[]{:S(2)}, u32[]{:S(2)}) collective-permute-start(bf16[128,512]{1,0:T(8,128)(2,1)S(1)} %bitcast.25), channel_id=1, source_target_pairs={{0,1},{1,0},{2,3},{3,2},{4,5},{5,4},{6,7},{7,6},{8,9},{9,8},{10,11... | collective-permute-start | bytes 393224 | tf_op jit(solution)/shard_map/ppermute | solution.py:228
  17.7 12.6 %collective-permute-start.2 = (bf16[128,512]{1,0:T(8,128)(2,1)S(1)}, bf16[128,512]{1,0:T(8,128)(2,1)S(1)}, u32[]{:S(2)}, u32[]{:S(2)}) collective-permute-start(bf16[128,512]{1,0:T(8,128)(2,1)S(1)} %bitcast.26), channel_id=1, source_target_pairs={{0,4},{2,6},{4,0},{6,2},{1,5},{3,7},{5,1},{7,3},{8,12},{10,14},{12... | collective-permute-start | bytes 393224 | tf_op jit(solution)/shard_map/ppermute | solution.py:205
  22.9 7.8 %collective-permute-start.1 = (bf16[128,512]{1,0:T(8,128)(2,1)S(1)}, bf16[128,512]{1,0:T(8,128)(2,1)S(1)}, u32[]{:S(2)}, u32[]{:S(2)}) collective-permute-start(bf16[128,512]{1,0:T(8,128)(2,1)S(1)} %bitcast.27), channel_id=1, source_target_pairs={{0,6},{2,0},{4,2},{6,4},{1,7},{3,1},{5,3},{7,5},{8,14},{10,8},{12,... | collective-permute-start | bytes 393224 | tf_op jit(solution)/shard_map/ppermute | solution.py:205
  26.0 8.4 %collective-permute-start = (bf16[128,512]{1,0:T(8,128)(2,1)S(1)}, bf16[128,512]{1,0:T(8,128)(2,1)S(1)}, u32[]{:S(2)}, u32[]{:S(2)}) collective-permute-start(bf16[128,512]{1,0:T(8,128)(2,1)S(1)} %bitcast.28), channel_id=1, source_target_pairs={{0,2},{2,4},{4,6},{6,0},{1,3},{3,5},{5,7},{7,1},{8,10},{10,12},{12... | collective-permute-start | bytes 393224 | tf_op jit(solution)/shard_map/ppermute | solution.py:205
  37.0 9.6 %copy-start.1 = (s32[1,8]{1,0:T(1,128)S(1)}, s32[1,8]{1,0:T(1,128)}, u32[]{:S(2)}) copy-start(s32[1,8]{1,0:T(1,128)} %bounds_ref.1) | copy-start | bytes 100

commit v8 on v7

--- a/solution.py
+++ b/solution.py
@@ -98,16 +98,19 @@
     )(sums, pieces)
 
 
-def held_rows(place_ref, own_ref, far_ref, moved_ref):
+def held_rows(place_ref, own_ref, far_ref, moved_ref, across_ref):
     x, core = place_ref[0], place_ref[2]
     held = [(2 * x + core, own_ref), (2 * x + 1 - core, far_ref)]
     for j, offset in enumerate(OFFSETS[1:]):
         x_from = lax.rem(x + (offset + 4), 4)
-        held += [(2 * x_from + c, moved_ref.at[c, j]) for c in range(2)]
+        refs = [across_ref.at[c] if offset == 2 else moved_ref.at[c, j] for c in range(2)]
+        held += [(2 * x_from + c, refs[c]) for c in range(2)]
     return held
 
 
-def margin_kernel(place_ref, tags_ref, delta_ref, columns_ref, own_ref, far_ref, moved_ref, out_ref):
+def margin_kernel(
+    place_ref, tags_ref, delta_ref, columns_ref, own_ref, far_ref, moved_ref, across_ref, out_ref
+):
     groups, seq_len, _ = columns_ref.shape
     shape = (2 * groups, seq_len)
     row = lax.broadcasted_iota(jnp.int32, shape, 0)
@@ -116,7 +119,7 @@
     tags = jnp.where(lane < seq_len // 2, tags_ref[0], tags_ref[1]).astype(f32)
     acc = jnp.where(row == me + groups, tags, 0.0)
     delta = delta_ref[...]
-    for seq, read_ref in held_rows(place_ref, own_ref, far_ref, moved_ref):
+    for seq, read_ref in held_rows(place_ref, own_ref, far_ref, moved_ref, across_ref):
         value = jnp.dot(columns_ref[seq], delta, preferred_element_type=f32)
         prod = value * read_ref[...].astype(f32)
         part = prod[:, :128]
@@ -132,7 +135,7 @@
     groups, seq_len, _ = columns.shape
     return pl.pallas_call(
         margin_kernel,
-        in_specs=[SMEM, SMEM] + [VMEM] * 5,
+        in_specs=[SMEM, SMEM] + [VMEM] * 6,
         out_specs=VMEM,
         out_shape=jax.ShapeDtypeStruct((groups, 2 * groups, seq_len), f32),
         compiler_params=pltpu.CompilerParams(vmem_limit_bytes=VMEM_LIMIT),
@@ -140,7 +143,7 @@
 
 
 def grad_kernel(
-    place_ref, bounds_ref, small_ref, columns_ref, own_ref, far_ref, moved_ref,
+    place_ref, bounds_ref, small_ref, columns_ref, own_ref, far_ref, moved_ref, across_ref,
     grad_ref, sums_ref, slope_ref
 ):
     groups, seq_len, share = columns_ref.shape
@@ -168,7 +171,7 @@
     weight = beta_scale * (1.0 / (1.0 + jnp.exp(-total)) - label)
     row = lax.broadcasted_iota(jnp.int32, weight.shape, 0)
     position = lax.broadcasted_iota(jnp.int32, (seq_len, 1), 0).astype(f32)
-    for seq, read_ref in held_rows(place_ref, own_ref, far_ref, moved_ref):
+    for seq, read_ref in held_rows(place_ref, own_ref, far_ref, moved_ref, across_ref):
         w = jnp.sum(jnp.where(row == seq, weight, 0.0), axis=0, keepdims=True)
         live = position < jnp.sum(jnp.where(row == seq, length, 0.0), axis=0, keepdims=True)
         slope_ref[seq] = (jnp.where(live, w, 0.0) * read_ref[...].astype(f32)).astype(bf16)
@@ -189,7 +192,7 @@
     features = reads[0].shape[1]
     return pl.pallas_call(
         grad_kernel,
-        in_specs=[SMEM] + [VMEM] * 6,
+        in_specs=[SMEM] + [VMEM] * 7,
         out_specs=[VMEM, VMEM],
         out_shape=[
             jax.ShapeDtypeStruct((4, share // 4, features), bf16),
@@ -217,6 +220,7 @@
     swap = [(0, 1), (1, 0)]
     pieces = norm_call(hidden[0], norm_gain[None], group)
     columns = exchange(pieces, GROUP)
+    weight_prm, _ = lax.optimization_barrier((weight_prm, pieces))
     expanded = jnp.repeat(scale_ref.T, head_size, axis=1)
     ref_local = (quant_ref.astype(f32) * expanded).astype(bf16)
     delta = (weight_prm.astype(f32) - ref_local.astype(f32)).astype(bf16)
@@ -225,13 +229,15 @@
     pair = [jnp.where(y_lo == k, delta, delta_other) for k in range(2)]
     delta = jnp.concatenate(pair, axis=0)
     near = shifted(own, ("x",))
-    far_own = lax.ppermute(own, "c", swap)
+    late, _ = lax.optimization_barrier((own, delta))
+    far_own = lax.ppermute(late, "c", swap)
     tags = jnp.concatenate([labels, lengths])
-    moved = jnp.stack(near[1:])
-    moved, delta, far_own, place, tags = lax.optimization_barrier(
-        (moved, delta, far_own, place, tags)
+    across = lax.all_gather(near[3], "c")
+    moved = jnp.stack(near[1:3])
+    moved, across, delta, far_own, place, tags = lax.optimization_barrier(
+        (moved, across, delta, far_own, place, tags)
     )
-    reads = [own, far_own, lax.all_gather(moved, "c")]
+    reads = [own, far_own, lax.all_gather(moved, "c"), across]
     small = exchange(margin_call(place, tags, delta, columns, reads), GROUP)
     grad, sums = grad_call(place, bounds, small, columns, reads)
     grad = wide_sum(exchange(grad, ("yh", "yl"))).astype(bf16)

time: 112 us -> 112 us (level)
  waiting for transfers between devices: 4.22 us -> 0.02 us
  blocking collectives: 72.5 us -> 76.3 us
    ppermute x3, waiting for transfers between devices: 4.21 us -> 0.01 us  [shifted(): return [block] + [lax.ppermute(block, axes, pair) for pair in pairs]]
    all_gather x1 -> x2, blocking collectives: 2.37 us -> 4.31 us  [the longest x1 2.18 us: on_device(): reads = [own, far_own, lax.all_gather(moved, 'c'), across]]
    all_to_all x4, blocking collectives: 45.9 us -> 47.8 us  [exchange(): return lax.all_to_all(pieces, axes, 0, 0, tiled=False)]
  transfers between devices with their start and end apart: 6 -> 6, of which waited for: 2 -> 0; matrix products, arithmetic and copies ran while one was open for 1% -> 1% of each run, Pallas kernels for 0% -> 0%
where the time goes in v8:
time: 112 us; the launch traced here: 111 us
  blocking collectives  76.3 us (68%)
  starting transfers between devices  24.6 us (22%)
  Pallas kernels  7.21 us (6%)
  between operations  2.11 us (2%)
    all_to_all x4, blocking collectives, exchange(): return lax.all_to_all(pieces, axes, 0, 0, tiled=False)  47.8 us
    all_gather x1, blocking collectives, on_device(): grad = wide_sum(lax.all_gather(grad, 'zh')).astype(bf16)  24.3 us
    ppermute x3, starting transfers between devices, shifted(): return [block] + [lax.ppermute(block, axes, pair) for pair in pairs]  11.2 us
    ppermute x1, starting transfers between devices, on_device(): delta_other = lax.ppermute(delta, 'yl', swap)  7.04 us
    all_to_all x1, starting transfers between devices, exchange(): return lax.all_to_all(pieces, axes, 0, 0, tiled=False)  4.44 us
    pallas_call x1, Pallas kernels, norm_call(): pl.pallas_call(norm_kernel, grid=(seq_len // block,), in_specs=[pl.BlockS...  2.78 us
  transfers between devices with their start and end apart: 6, of which 0 were waited for; matrix products, arithmetic and copies ran while one was open for 1% of the time, Pallas kernels for 0%

profile of v8, /device:TPU:8, one launch (start us, length us, event | category | flops | bytes accessed | tf_op | source)
XLA Modules:
  0.0 111.5 jit_solution(8513644970235412387)
XLA Ops:
  0.6 2.8 %shard_map.104 = bf16[8,128,640]{2,1,0:T(8,128)(2,1)} custom-call(bf16[128,5120]{1,0:T(8,128)(2,1)} %bitcast.34, f32[1,5120]{1,0:T(1,128)} %bitcast.38), custom_call_target="tpu_custom_call" | custom-call | tf_op jit(solution)/shard_map/pallas_call | solution.py:55
  3.4 0.0 copy-start.4
  3.4 0.0 copy-start.2
  3.4 0.0 copy-start.3
  3.4 4.4 %all-to-all-start = ((bf16[8,128,640]{2,1,0:T(8,128)(2,1)}), bf16[8,128,640]{2,1,0:T(8,128)(2,1)S(1)}, u32[]{:S(2)}, u32[]{:S(2)}) async-start(bf16[8,128,640]{2,1,0:T(8,128)(2,1)} %shard_map.104), calls=%async_computation | async-start | bytes 2621440 | tf_op jit(solution)/shard_map/all_to_all | solution.py:23
  7.9 0.0 copy-done.4
  7.9 0.0 copy-start
  7.9 0.1 copy.13
  8.0 0.4 broadcast_in_dim.15
  8.4 0.0 copy-done.2
  8.4 0.0 copy-done.3
  8.4 0.2 subtract_convert_fusion
  8.6 7.0 %collective-permute-start.3 = (bf16[320,512]{1,0:T(8,128)(2,1)S(1)}, bf16[320,512]{1,0:T(8,128)(2,1)S(1)}, u32[]{:S(2)}, u32[]{:S(2)}) collective-permute-start(bf16[320,512]{1,0:T(8,128)(2,1)S(1)} %subtract_convert_fusion), channel_id=1, source_target_pairs={{0,8},{8,0},{1,9},{9,1},{2,10},{10,2},{3,11},{11,3},{4,12},{12,4},... | collective-permute-start | bytes 983048 | tf_op jit(solution)/shard_map/ppermute | solution.py:227
  15.7 0.0 copy-done
  15.7 5.3 %collective-permute-start.2 = (bf16[128,512]{1,0:T(8,128)(2,1)S(1)}, bf16[128,512]{1,0:T(8,128)(2,1)S(1)}, u32[]{:S(2)}, u32[]{:S(2)}) collective-permute-start(bf16[128,512]{1,0:T(8,128)(2,1)S(1)} %bitcast.27), channel_id=1, source_target_pairs={{0,4},{2,6},{4,0},{6,2},{1,5},{3,7},{5,1},{7,3},{8,12},{10,14},{12... | collective-permute-start | bytes 393224 | tf_op jit(solution)/shard_map/ppermute | solution.py:208
  21.0 3.1 %collective-permute-start.1 = (bf16[128,512]{1,0:T(8,128)(2,1)S(1)}, bf16[128,512]{1,0:T(8,128)(2,1)S(1)}, u32[]{:S(2)}, u32[]{:S(2)}) collective-permute-start(bf16[128,512]{1,0:T(8,128)(2,1)S(1)} %bitcast.28), channel_id=1, source_target_pairs={{0,6},{2,0},{4,2},{6,4},{1,7},{3,1},{5,3},{7,5},{8,14},{10,8},{12,... | collective-permute-start | bytes 393224 | tf_op jit(solution)/shard_map/ppermute | solution.py:208
  24.1 2.8 %collective-permute-start = (bf16[128,512]{1,0:T(8,128)(2,1)S(1)}, bf16[128,512]{1,0:T(8,128)(2,1)S(1)}, u32[]{:S(2)}, u32[]{:S(2)}) collective-permute-start(bf16[128,512]{1,0:T(8,128)(2,1)S(1)} %bitcast.29), channel_id=1, source_target_pairs={{0,2},{2,4},{4,6},{6,0},{1,3},{3,5},{5,7},{7,1},{8,10},{10,12},{12... | collective-permute-start | bytes 393224 | tf_op jit(solution)/shard_map/ppermute | solution.py:208
  28.1 0.1 pad_add_fusion.1.tags_ref
  28.2 0.1 pad_add_fusion.place_ref
  28.3 0.0 collective-permute-done.3
  28.4 1.9 %collective-permute-start.4 = (bf16[128,512]{1,0:T(8,128)(2,1)S(1)}, bf16[128,512]{1,0:T(8,128)(2,1)S(1)}, u32[]{:S(2)}, u32[]{:S(2)}) collective-permute-start(bf16[128,512]{1,0:T(8,128)(2,1)S(1)} %bitcast.30), channel_id=1, source_target_pairs={{0,1},{1,0},{2,3},{3,2},{4,5},{5,4},{6,7},{7,6},{8,9},{9,8},{10,11... | collective-permute-start | bytes 393224 | tf_op jit(solution)/shard_map/ppermute | solution.py:233
  30.3 0.0 collective-permute-done.2
  30.3 2.1 %all-gather = bf16[256,512]{1,0:T(8,128)(2,1)S(1)} all-gather(bf16[128,512]{1,0:T(8,128)(2,1)S(1)} %collective-permute-done.2), channel_id=2, replica_groups=mesh['yh'=2,'zh'=4,'zl'=4,'yl'=2,'x'=4,'c'=2] {'c'}, dimensions={0}, use_global_device_ids=true | all-gather | bytes 393216 | tf_op jit(solution)/shard_map/all_gather | solution.py:235
  32.5 0.0 collective-permute-done.1
  32.5 0.0 collective-permute-done
  32.5 0.0 collective-permute-done.4.far_ref
  32.5 2.2 %all-gather.1 = bf16[4,128,512]{2,1,0:T(8,128)(2,1)S(1)} all-gather(bf16[2,128,512]{2,1,0:T(8,128)(2,1)S(1)} %pad_maximum_fusion.1), channel_id=3, replica_groups=mesh['yh'=2,'zh'=4,'zl'=4,'yl'=2,'x'=4,'c'=2] {'c'}, dimensions={0}, use_global_device_ids=true | all-gather | bytes 786432 | tf_op jit(solution)/shard_map/all_gather | solution.py:240
  34.7 0.0 all-to-all-done.columns_ref
  34.7 0.0 copy-start.1
  34.7 1.6 %shard_map.105 = f32[8,16,128]{2,1,0:T(8,128)S(1)} custom-call(s32[3]{0:T(128)S(1)} %pad_add_fusion.place_ref, s32[2]{0:T(128)S(1)} %pad_add_fusion.1.tags_ref, bf16[640,512]{1,0:T(8,128)(2,1)S(1)} %pad_maximum_fusion.delta_ref, bf16[8,128,640]{2,1,0:T(8,128)(2,1)S(1)} %all-to-all-done.columns_ref, bf16[128,512]{1,0:T(8,128)(2,1)S(1)} %bitcast.31, ...), custom_call_target="tpu_custom_call" | custom-call | tf_op jit(solution)/shard_map/pallas_call | solution.py:136
  36.3 9.1 %all_to_all.25.small_ref = f32[8,16,128]{2,1,0:T(8,128)S(1)} all-to-all(f32[8,16,128]{2,1,0:T(8,128)S(1)} %shard_map.105), channel_id=1, replica_groups=mesh['yh'=2,'zh'=4,'zl'=4,'yl'=2,'x'=4,'c'=2] {'x','c'}, dimensions={0} | all-to-all | bytes 131072 | tf_op jit(solution)/shard_map/all_to_all | solution.py:23
  45.4 0.0 copy-done.1
  45.4 1.9 %shard_map.106 = (bf16[4,160,512]{2,1,0:T(8,128)(2,1)S(1)}, f32[8,128]{1,0:T(8,128)S(1)}) custom-call(s32[3]{0:T(128)S(1)} %pad_add_fusion.place_ref, s32[1,8]{1,0:T(1,128)S(1)} %copy-done.1, f32[8,16,128]{2,1,0:T(8,128)S(1)} %all_to_all.25.small_ref, bf16[8,128,640]{2,1,0:T(8,128)(2,1)S(1)} %all-to-all-done.columns_ref, bf16[128,512]{1,0:T(8,128)(2,1)S(1)} %bitcast.32, ...), custom_call_target="tpu_custom_call" | custom-call | tf_op jit(solution)/shard_map/pallas_call | solution.py:193
  47.4 15.7 %all_to_all.26 = bf16[4,160,512]{2,1,0:T(8,128)(2,1)S(1)} all-to-all(bf16[4,160,512]{2,1,0:T(8,128)(2,1)S(1)} %get-tuple-element.25), channel_id=1, replica_groups=mesh['yh'=2,'zh'=4,'zl'=4,'yl'=2,'x'=4,'c'=2] {'yh','yl'}, dimensions={0} | all-to-all | bytes 1310720 | tf_op jit(solution)/shard_map/all_to_all | solution.py:23
  63.1 0.1 add_convert_fusion
  63.2 9.4 %all_to_all.27 = bf16[4,160,128]{2,1,0:T(8,128)(2,1)S(1)} all-to-all(bf16[4,160,128]{2,1,0:T(8,128)(2,1)S(1)} %bitcast.35), channel_id=1, replica_groups=mesh['yh'=2,'zh'=4,'zl'=4,'yl'=2,'x'=4,'c'=2] {'zl'}, dimensions={0} | all-to-all | bytes 327680 | tf_op jit(solution)/shard_map/all_to_all | solution.py:23
  72.7 24.3 %all_gather.20 = bf16[4,160,128]{2,1,0:T(8,128)(2,1)S(1)} all-gather(bf16[1,160,128]{2,1,0:T(8,128)(2,1)S(1)} %add_convert_fusion.2), channel_id=1, replica_groups=mesh['yh'=2,'zh'=4,'zl'=4,'yl'=2,'x'=4,'c'=2] {'zh'}, dimensions={0}, use_global_device_ids=true | all-gather | bytes 204800 | tf_op jit(solution)/shard_map/all_gather | solution.py:247
  97.0 13.6 %all_to_all.28.pieces_ref = bf16[8,160,128]{2,1,0:T(8,128)(2,1)S(1)} all-to-all(bf16[8,160,128]{2,1,0:T(8,128)(2,1)S(1)} %broadcast_in_dim.17), channel_id=1, replica_groups=mesh['yh'=2,'zh'=4,'zl'=4,'yl'=2,'x'=4,'c'=2] {'yh','zl'}, dimensions={0} | all-to-all | bytes 655360 | tf_op jit(solution)/shard_map/all_to_all | solution.py:23
  110.6 0.9 shard_map.107
  (8 shorter events, 0.3 us)
Async XLA Ops:
  3.4 4.5 %copy-start.4 = (f32[4,320]{1,0:T(4,128)S(1)}, f32[4,320]{1,0:T(4,128)}, u32[]{:S(2)}) copy-start(f32[4,320]{1,0:T(4,128)} %param.12) | copy-start | bytes 15364
  3.4 5.0 %copy-start.2 = (bf16[320,512]{1,0:T(8,128)(2,1)S(1)}, bf16[320,512]{1,0:T(8,128)(2,1)}, u32[]{:S(2)}) copy-start(bf16[320,512]{1,0:T(8,128)(2,1)} %param.13) | copy-start | bytes 983044
  3.4 5.0 %copy-start.3 = (bf16[320,512]{1,0:T(8,128)(2,1)S(1)}, bf16[320,512]{1,0:T(8,128)(2,1)}, u32[]{:S(2)}) copy-start(bf16[320,512]{1,0:T(8,128)(2,1)} %param.11) | copy-start | bytes 983044
  3.4 31.3 %all-to-all-start = ((bf16[8,128,640]{2,1,0:T(8,128)(2,1)}), bf16[8,128,640]{2,1,0:T(8,128)(2,1)S(1)}, u32[]{:S(2)}, u32[]{:S(2)}) async-start(bf16[8,128,640]{2,1,0:T(8,128)(2,1)} %shard_map.104), calls=%async_computation | async-start | bytes 2621440 | tf_op jit(solution)/shard_map/all_to_all | solution.py:23
  7.9 7.8 %copy-start = (bf16[1,128,512]{2,1,0:T(8,128)(2,1)S(1)}, bf16[1,128,512]{2,1,0:T(8,128)(2,1)}, u32[]{:S(2)}) copy-start(bf16[1,128,512]{2,1,0:T(8,128)(2,1)} %param.14) | copy-start | bytes 393220
  8.6 19.7 %collective-permute-start.3 = (bf16[320,512]{1,0:T(8,128)(2,1)S(1)}, bf16[320,512]{1,0:T(8,128)(2,1)S(1)}, u32[]{:S(2)}, u32[]{:S(2)}) collective-permute-start(bf16[320,512]{1,0:T(8,128)(2,1)S(1)} %subtract_convert_fusion), channel_id=1, source_target_pairs={{0,8},{8,0},{1,9},{9,1},{2,10},{10,2},{3,11},{11,3},{4,12},{12,4},... | collective-permute-start | bytes 983048 | tf_op jit(solution)/shard_map/ppermute | solution.py:227
  15.7 14.7 %collective-permute-start.2 = (bf16[128,512]{1,0:T(8,128)(2,1)S(1)}, bf16[128,512]{1,0:T(8,128)(2,1)S(1)}, u32[]{:S(2)}, u32[]{:S(2)}) collective-permute-start(bf16[128,512]{1,0:T(8,128)(2,1)S(1)} %bitcast.27), channel_id=1, source_target_pairs={{0,4},{2,6},{4,0},{6,2},{1,5},{3,7},{5,1},{7,3},{8,12},{10,14},{12... | collective-permute-start | bytes 393224 | tf_op jit(solution)/shard_map/ppermute | solution.py:208
  21.0 11.5 %collective-permute-start.1 = (bf16[128,512]{1,0:T(8,128)(2,1)S(1)}, bf16[128,512]{1,0:T(8,128)(2,1)S(1)}, u32[]{:S(2)}, u32[]{:S(2)}) collective-permute-start(bf16[128,512]{1,0:T(8,128)(2,1)S(1)} %bitcast.28), channel_id=1, source_target_pairs={{0,6},{2,0},{4,2},{6,4},{1,7},{3,1},{5,3},{7,5},{8,14},{10,8},{12,... | collective-permute-start | bytes 393224 | tf_op jit(solution)/shard_map/ppermute | solution.py:208
  24.1 8.4 %collective-permute-start = (bf16[128,512]{1,0:T(8,128)(2,1)S(1)}, bf16[128,512]{1,0:T(8,128)(2,1)S(1)}, u32[]{:S(2)}, u32[]{:S(2)}) collective-permute-start(bf16[128,512]{1,0:T(8,128)(2,1)S(1)} %bitcast.29), channel_id=1, source_target_pairs={{0,2},{2,4},{4,6},{6,0},{1,3},{3,5},{5,7},{7,1},{8,10},{10,12},{12... | collective-permute-start | bytes 393224 | tf_op jit(solution)/shard_map/ppermute | solution.py:208
  28.4 4.1 %collective-permute-start.4 = (bf16[128,512]{1,0:T(8,128)(2,1)S(1)}, bf16[128,512]{1,0:T(8,128)(2,1)S(1)}, u32[]{:S(2)}, u32[]{:S(2)}) collective-permute-start(bf16[128,512]{1,0:T(8,128)(2,1)S(1)} %bitcast.30), channel_id=1, source_target_pairs={{0,1},{1,0},{2,3},{3,2},{4,5},{5,4},{6,7},{7,6},{8,9},{9,8},{10,11... | collective-permute-start | bytes 393224 | tf_op jit(solution)/shard_map/ppermute | solution.py:233
  34.7 10.7 %copy-start.1 = (s32[1,8]{1,0:T(1,128)S(1)}, s32[1,8]{1,0:T(1,128)}, u32[]{:S(2)}) copy-start(s32[1,8]{1,0:T(1,128)} %bounds_ref.1) | copy-start | bytes 100

commit v9 on v8

--- a/solution.py
+++ b/solution.py
@@ -184,7 +184,9 @@
     for yh in range(2):
         for yl in range(2):
             at = (2 * yl + yh) * part
-            grad_ref[2 * yh + yl] = grad[at : at + part]
+            for zl in range(4):
+                piece = grad[at : at + part, 128 * zl : 128 * (zl + 1)]
+                grad_ref[8 * yh + 4 * yl + zl] = piece
 
 
 def grad_call(place, bounds, small, columns, reads):
@@ -195,7 +197,7 @@
         in_specs=[SMEM] + [VMEM] * 7,
         out_specs=[VMEM, VMEM],
         out_shape=[
-            jax.ShapeDtypeStruct((4, share // 4, features), bf16),
+            jax.ShapeDtypeStruct((16, share // 4, features // 4), bf16),
             jax.ShapeDtypeStruct((bounds.shape[1], seq_len), f32),
         ],
         scratch_shapes=[pltpu.VMEM((groups, seq_len, features), bf16)],
@@ -240,10 +242,7 @@
     reads = [own, far_own, lax.all_gather(moved, "c"), across]
     small = exchange(margin_call(place, tags, delta, columns, reads), GROUP)
     grad, sums = grad_call(place, bounds, small, columns, reads)
-    grad = wide_sum(exchange(grad, ("yh", "yl"))).astype(bf16)
-    zl = lax.axis_size("zl")
-    grad = grad.reshape(grad.shape[0], zl, features // zl).transpose(1, 0, 2)
-    grad = wide_sum(exchange(grad, ("zl",))).astype(bf16)
+    grad = wide_sum(exchange(grad, ("yh", "yl", "zl"))).astype(bf16)
     grad = wide_sum(lax.all_gather(grad, "zh")).astype(bf16)
     grad = spread(grad, ("yh", "zl"))
     grad, step_rewards = place_call(sums, grad, lax.axis_size("yh"))

time: 112 us -> 112 us (level)
  the two profiles are of different devices: /device:TPU:8 before, /device:TPU:2 now
where the time goes in v9:
time: 112 us
  blocking collectives  73.5 us (66%)
  starting transfers between devices  23.2 us (21%)
  Pallas kernels  7.2 us (6%)
  waiting for transfers between devices  4.65 us (4%)
  between operations  2.08 us (2%)
    all_to_all x3, blocking collectives, exchange(): return lax.all_to_all(pieces, axes, 0, 0, tiled=False)  44.4 us
    all_gather x1, blocking collectives, on_device(): grad = wide_sum(lax.all_gather(grad, 'zh')).astype(bf16)  24.9 us
    ppermute x3, starting transfers between devices, shifted(): return [block] + [lax.ppermute(block, axes, pair) for pair in pairs]  9.85 us
    all_to_all x1, starting transfers between devices, exchange(): return lax.all_to_all(pieces, axes, 0, 0, tiled=False)  9.53 us
    ppermute x3, waiting for transfers between devices, shifted(): return [block] + [lax.ppermute(block, axes, pair) for pair in pairs]  4.64 us
    pallas_call x1, Pallas kernels, norm_call(): pl.pallas_call(norm_kernel, grid=(seq_len // block,), in_specs=[pl.BlockS...  2.78 us
  transfers between devices with their start and end apart: 6, of which 1 were waited for; matrix products, arithmetic and copies ran while one was open for 1% of the time, Pallas kernels for 0%

profile of v9, /device:TPU:2, one launch (start us, length us, event | category | flops | bytes accessed | tf_op | source)
XLA Modules:
  0.0 111.7 jit_solution(9029184049918817751)
XLA Ops:
  0.6 2.8 %shard_map.104 = bf16[8,128,640]{2,1,0:T(8,128)(2,1)} custom-call(bf16[128,5120]{1,0:T(8,128)(2,1)} %bitcast.31, f32[1,5120]{1,0:T(1,128)} %bitcast.34), custom_call_target="tpu_custom_call" | custom-call | tf_op jit(solution)/shard_map/pallas_call | solution.py:55
  3.4 0.0 copy-start.4
  3.4 0.0 copy-start.2
  3.4 0.0 copy-start.3
  3.4 9.5 %all-to-all-start = ((bf16[8,128,640]{2,1,0:T(8,128)(2,1)}), bf16[8,128,640]{2,1,0:T(8,128)(2,1)S(1)}, u32[]{:S(2)}, u32[]{:S(2)}) async-start(bf16[8,128,640]{2,1,0:T(8,128)(2,1)} %shard_map.104), calls=%async_computation | async-start | bytes 2621440 | tf_op jit(solution)/shard_map/all_to_all | solution.py:23
  12.9 0.0 copy-done.4
  13.0 0.0 copy-start
  13.0 0.1 copy.12
  13.1 0.4 broadcast_in_dim.15
  13.5 0.0 copy-done.2
  13.5 0.0 copy-done.3
  13.5 0.2 subtract_convert_fusion
  13.7 1.9 %collective-permute-start.3 = (bf16[320,512]{1,0:T(8,128)(2,1)S(1)}, bf16[320,512]{1,0:T(8,128)(2,1)S(1)}, u32[]{:S(2)}, u32[]{:S(2)}) collective-permute-start(bf16[320,512]{1,0:T(8,128)(2,1)S(1)} %subtract_convert_fusion), channel_id=1, source_target_pairs={{0,8},{8,0},{1,9},{9,1},{2,10},{10,2},{3,11},{11,3},{4,12},{12,4},... | collective-permute-start | bytes 983048 | tf_op jit(solution)/shard_map/ppermute | solution.py:229
  15.6 0.0 copy-done
  15.6 4.0 %collective-permute-start.2 = (bf16[128,512]{1,0:T(8,128)(2,1)S(1)}, bf16[128,512]{1,0:T(8,128)(2,1)S(1)}, u32[]{:S(2)}, u32[]{:S(2)}) collective-permute-start(bf16[128,512]{1,0:T(8,128)(2,1)S(1)} %bitcast.24), channel_id=1, source_target_pairs={{0,4},{2,6},{4,0},{6,2},{1,5},{3,7},{5,1},{7,3},{8,12},{10,14},{12... | collective-permute-start | bytes 393224 | tf_op jit(solution)/shard_map/ppermute | solution.py:210
  19.6 3.4 %collective-permute-start.1 = (bf16[128,512]{1,0:T(8,128)(2,1)S(1)}, bf16[128,512]{1,0:T(8,128)(2,1)S(1)}, u32[]{:S(2)}, u32[]{:S(2)}) collective-permute-start(bf16[128,512]{1,0:T(8,128)(2,1)S(1)} %bitcast.25), channel_id=1, source_target_pairs={{0,6},{2,0},{4,2},{6,4},{1,7},{3,1},{5,3},{7,5},{8,14},{10,8},{12,... | collective-permute-start | bytes 393224 | tf_op jit(solution)/shard_map/ppermute | solution.py:210
  23.0 2.5 %collective-permute-start = (bf16[128,512]{1,0:T(8,128)(2,1)S(1)}, bf16[128,512]{1,0:T(8,128)(2,1)S(1)}, u32[]{:S(2)}, u32[]{:S(2)}) collective-permute-start(bf16[128,512]{1,0:T(8,128)(2,1)S(1)} %bitcast.26), channel_id=1, source_target_pairs={{0,2},{2,4},{4,6},{6,0},{1,3},{3,5},{5,7},{7,1},{8,10},{10,12},{12... | collective-permute-start | bytes 393224 | tf_op jit(solution)/shard_map/ppermute | solution.py:210
  26.8 0.1 pad_add_fusion.1.tags_ref
  26.9 0.1 pad_add_fusion.place_ref
  26.9 0.0 collective-permute-done.3
  27.1 1.9 %collective-permute-start.4 = (bf16[128,512]{1,0:T(8,128)(2,1)S(1)}, bf16[128,512]{1,0:T(8,128)(2,1)S(1)}, u32[]{:S(2)}, u32[]{:S(2)}) collective-permute-start(bf16[128,512]{1,0:T(8,128)(2,1)S(1)} %bitcast.27), channel_id=1, source_target_pairs={{0,1},{1,0},{2,3},{3,2},{4,5},{5,4},{6,7},{7,6},{8,9},{9,8},{10,11... | collective-permute-start | bytes 393224 | tf_op jit(solution)/shard_map/ppermute | solution.py:235
  29.0 4.6 %collective-permute-done.2 = bf16[128,512]{1,0:T(8,128)(2,1)S(1)} collective-permute-done((bf16[128,512]{1,0:T(8,128)(2,1)S(1)}, bf16[128,512]{1,0:T(8,128)(2,1)S(1)}, u32[]{:S(2)}, u32[]{:S(2)}) %collective-permute-start.2) | collective-permute-done | bytes 131104 | tf_op jit(solution)/shard_map/ppermute | solution.py:210
  33.6 2.0 %all-gather = bf16[256,512]{1,0:T(8,128)(2,1)S(1)} all-gather(bf16[128,512]{1,0:T(8,128)(2,1)S(1)} %collective-permute-done.2), channel_id=2, replica_groups=mesh['yh'=2,'zh'=4,'zl'=4,'yl'=2,'x'=4,'c'=2] {'c'}, dimensions={0}, use_global_device_ids=true | all-gather | bytes 393216 | tf_op jit(solution)/shard_map/all_gather | solution.py:237
  35.6 0.0 collective-permute-done.1
  35.6 0.0 collective-permute-done
  35.6 0.0 collective-permute-done.4.far_ref
  35.6 2.2 %all-gather.1 = bf16[4,128,512]{2,1,0:T(8,128)(2,1)S(1)} all-gather(bf16[2,128,512]{2,1,0:T(8,128)(2,1)S(1)} %pad_maximum_fusion.1), channel_id=3, replica_groups=mesh['yh'=2,'zh'=4,'zl'=4,'yl'=2,'x'=4,'c'=2] {'c'}, dimensions={0}, use_global_device_ids=true | all-gather | bytes 786432 | tf_op jit(solution)/shard_map/all_gather | solution.py:242
  37.8 0.0 all-to-all-done.columns_ref
  37.8 0.0 copy-start.1
  37.8 1.6 %shard_map.105 = f32[8,16,128]{2,1,0:T(8,128)S(1)} custom-call(s32[3]{0:T(128)S(1)} %pad_add_fusion.place_ref, s32[2]{0:T(128)S(1)} %pad_add_fusion.1.tags_ref, bf16[640,512]{1,0:T(8,128)(2,1)S(1)} %pad_maximum_fusion.delta_ref, bf16[8,128,640]{2,1,0:T(8,128)(2,1)S(1)} %all-to-all-done.columns_ref, bf16[128,512]{1,0:T(8,128)(2,1)S(1)} %bitcast.28, ...), custom_call_target="tpu_custom_call" | custom-call | tf_op jit(solution)/shard_map/pallas_call | solution.py:136
  39.4 8.3 %all_to_all.20.small_ref = f32[8,16,128]{2,1,0:T(8,128)S(1)} all-to-all(f32[8,16,128]{2,1,0:T(8,128)S(1)} %shard_map.105), channel_id=1, replica_groups=mesh['yh'=2,'zh'=4,'zl'=4,'yl'=2,'x'=4,'c'=2] {'x','c'}, dimensions={0} | all-to-all | bytes 131072 | tf_op jit(solution)/shard_map/all_to_all | solution.py:23
  47.7 0.0 copy-done.1
  47.7 1.9 %shard_map.106 = (bf16[16,160,128]{2,1,0:T(8,128)(2,1)S(1)}, f32[8,128]{1,0:T(8,128)S(1)}) custom-call(s32[3]{0:T(128)S(1)} %pad_add_fusion.place_ref, s32[1,8]{1,0:T(1,128)S(1)} %copy-done.1, f32[8,16,128]{2,1,0:T(8,128)S(1)} %all_to_all.20.small_ref, bf16[8,128,640]{2,1,0:T(8,128)(2,1)S(1)} %all-to-all-done.columns_ref, bf16[128,512]{1,0:T(8,128)(2,1)S(1)} %bitcast.29, ...), custom_call_target="tpu_custom_call" | custom-call | tf_op jit(solution)/shard_map/pallas_call | solution.py:195
  49.7 23.1 %all_to_all.21 = bf16[16,160,128]{2,1,0:T(8,128)(2,1)S(1)} all-to-all(bf16[16,160,128]{2,1,0:T(8,128)(2,1)S(1)} %get-tuple-element.25), channel_id=1, replica_groups=mesh['yh'=2,'zh'=4,'zl'=4,'yl'=2,'x'=4,'c'=2] {'yh','yl','zl'}, dimensions={0} | all-to-all | bytes 1310720 | tf_op jit(solution)/shard_map/all_to_all | solution.py:23
  72.8 0.1 add_convert_fusion.1
  72.9 24.9 %all_gather.20 = bf16[4,160,128]{2,1,0:T(8,128)(2,1)S(1)} all-gather(bf16[1,160,128]{2,1,0:T(8,128)(2,1)S(1)} %add_convert_fusion.1), channel_id=1, replica_groups=mesh['yh'=2,'zh'=4,'zl'=4,'yl'=2,'x'=4,'c'=2] {'zh'}, dimensions={0}, use_global_device_ids=true | all-gather | bytes 204800 | tf_op jit(solution)/shard_map/all_gather | solution.py:246
  97.8 13.0 %all_to_all.22.pieces_ref = bf16[8,160,128]{2,1,0:T(8,128)(2,1)S(1)} all-to-all(bf16[8,160,128]{2,1,0:T(8,128)(2,1)S(1)} %broadcast_in_dim.17), channel_id=1, replica_groups=mesh['yh'=2,'zh'=4,'zl'=4,'yl'=2,'x'=4,'c'=2] {'yh','zl'}, dimensions={0} | all-to-all | bytes 655360 | tf_op jit(solution)/shard_map/all_to_all | solution.py:23
  110.9 0.9 shard_map.107
  (5 shorter events, 0.2 us)
Async XLA Ops:
  3.4 9.5 %copy-start.4 = (f32[4,320]{1,0:T(4,128)S(1)}, f32[4,320]{1,0:T(4,128)}, u32[]{:S(2)}) copy-start(f32[4,320]{1,0:T(4,128)} %param.12) | copy-start | bytes 15364
  3.4 10.1 %copy-start.2 = (bf16[320,512]{1,0:T(8,128)(2,1)S(1)}, bf16[320,512]{1,0:T(8,128)(2,1)}, u32[]{:S(2)}) copy-start(bf16[320,512]{1,0:T(8,128)(2,1)} %param.13) | copy-start | bytes 983044
  3.4 10.1 %copy-start.3 = (bf16[320,512]{1,0:T(8,128)(2,1)S(1)}, bf16[320,512]{1,0:T(8,128)(2,1)}, u32[]{:S(2)}) copy-start(bf16[320,512]{1,0:T(8,128)(2,1)} %param.11) | copy-start | bytes 983044
  3.4 34.4 %all-to-all-start = ((bf16[8,128,640]{2,1,0:T(8,128)(2,1)}), bf16[8,128,640]{2,1,0:T(8,128)(2,1)S(1)}, u32[]{:S(2)}, u32[]{:S(2)}) async-start(bf16[8,128,640]{2,1,0:T(8,128)(2,1)} %shard_map.104), calls=%async_computation | async-start | bytes 2621440 | tf_op jit(solution)/shard_map/all_to_all | solution.py:23
  13.0 2.7 %copy-start = (bf16[1,128,512]{2,1,0:T(8,128)(2,1)S(1)}, bf16[1,128,512]{2,1,0:T(8,128)(2,1)}, u32[]{:S(2)}) copy-start(bf16[1,128,512]{2,1,0:T(8,128)(2,1)} %param.14) | copy-start | bytes 393220
  13.7 13.3 %collective-permute-start.3 = (bf16[320,512]{1,0:T(8,128)(2,1)S(1)}, bf16[320,512]{1,0:T(8,128)(2,1)S(1)}, u32[]{:S(2)}, u32[]{:S(2)}) collective-permute-start(bf16[320,512]{1,0:T(8,128)(2,1)S(1)} %subtract_convert_fusion), channel_id=1, source_target_pairs={{0,8},{8,0},{1,9},{9,1},{2,10},{10,2},{3,11},{11,3},{4,12},{12,4},... | collective-permute-start | bytes 983048 | tf_op jit(solution)/shard_map/ppermute | solution.py:229
  15.6 18.0 %collective-permute-start.2 = (bf16[128,512]{1,0:T(8,128)(2,1)S(1)}, bf16[128,512]{1,0:T(8,128)(2,1)S(1)}, u32[]{:S(2)}, u32[]{:S(2)}) collective-permute-start(bf16[128,512]{1,0:T(8,128)(2,1)S(1)} %bitcast.24), channel_id=1, source_target_pairs={{0,4},{2,6},{4,0},{6,2},{1,5},{3,7},{5,1},{7,3},{8,12},{10,14},{12... | collective-permute-start | bytes 393224 | tf_op jit(solution)/shard_map/ppermute | solution.py:210
  19.6 16.0 %collective-permute-start.1 = (bf16[128,512]{1,0:T(8,128)(2,1)S(1)}, bf16[128,512]{1,0:T(8,128)(2,1)S(1)}, u32[]{:S(2)}, u32[]{:S(2)}) collective-permute-start(bf16[128,512]{1,0:T(8,128)(2,1)S(1)} %bitcast.25), channel_id=1, source_target_pairs={{0,6},{2,0},{4,2},{6,4},{1,7},{3,1},{5,3},{7,5},{8,14},{10,8},{12,... | collective-permute-start | bytes 393224 | tf_op jit(solution)/shard_map/ppermute | solution.py:210
  23.0 12.6 %collective-permute-start = (bf16[128,512]{1,0:T(8,128)(2,1)S(1)}, bf16[128,512]{1,0:T(8,128)(2,1)S(1)}, u32[]{:S(2)}, u32[]{:S(2)}) collective-permute-start(bf16[128,512]{1,0:T(8,128)(2,1)S(1)} %bitcast.26), channel_id=1, source_target_pairs={{0,2},{2,4},{4,6},{6,0},{1,3},{3,5},{5,7},{7,1},{8,10},{10,12},{12... | collective-permute-start | bytes 393224 | tf_op jit(solution)/shard_map/ppermute | solution.py:210
  27.1 8.6 %collective-permute-start.4 = (bf16[128,512]{1,0:T(8,128)(2,1)S(1)}, bf16[128,512]{1,0:T(8,128)(2,1)S(1)}, u32[]{:S(2)}, u32[]{:S(2)}) collective-permute-start(bf16[128,512]{1,0:T(8,128)(2,1)S(1)} %bitcast.27), channel_id=1, source_target_pairs={{0,1},{1,0},{2,3},{3,2},{4,5},{5,4},{6,7},{7,6},{8,9},{9,8},{10,11... | collective-permute-start | bytes 393224 | tf_op jit(solution)/shard_map/ppermute | solution.py:235
  37.8 9.9 %copy-start.1 = (s32[1,8]{1,0:T(1,128)S(1)}, s32[1,8]{1,0:T(1,128)}, u32[]{:S(2)}) copy-start(s32[1,8]{1,0:T(1,128)} %bounds_ref.1) | copy-start | bytes 100

commit v10 on v9

--- a/solution.py
+++ b/solution.py
@@ -186,7 +186,7 @@
             at = (2 * yl + yh) * part
             for zl in range(4):
                 piece = grad[at : at + part, 128 * zl : 128 * (zl + 1)]
-                grad_ref[8 * yh + 4 * yl + zl] = piece
+                grad_ref[4 * zl + 2 * yh + yl] = piece
 
 
 def grad_call(place, bounds, small, columns, reads):
@@ -242,7 +242,7 @@
     reads = [own, far_own, lax.all_gather(moved, "c"), across]
     small = exchange(margin_call(place, tags, delta, columns, reads), GROUP)
     grad, sums = grad_call(place, bounds, small, columns, reads)
-    grad = wide_sum(exchange(grad, ("yh", "yl", "zl"))).astype(bf16)
+    grad = wide_sum(exchange(grad, ("zl", "yh", "yl"))).astype(bf16)
     grad = wide_sum(lax.all_gather(grad, "zh")).astype(bf16)
     grad = spread(grad, ("yh", "zl"))
     grad, step_rewards = place_call(sums, grad, lax.axis_size("yh"))

time: 112 us -> 112 us (level)
  no operation moved by 1% of the time
where the time goes in v10:
time: 112 us; the launch traced here: 111 us
  blocking collectives  73.2 us (65%)
  starting transfers between devices  23.2 us (21%)
  Pallas kernels  7.2 us (6%)
  waiting for transfers between devices  4.65 us (4%)
  between operations  2.08 us (2%)
    all_to_all x3, blocking collectives, exchange(): return lax.all_to_all(pieces, axes, 0, 0, tiled=False)  45 us
    all_gather x1, blocking collectives, on_device(): grad = wide_sum(lax.all_gather(grad, 'zh')).astype(bf16)  24 us
    ppermute x3, starting transfers between devices, shifted(): return [block] + [lax.ppermute(block, axes, pair) for pair in pairs]  9.85 us
    all_to_all x1, starting transfers between devices, exchange(): return lax.all_to_all(pieces, axes, 0, 0, tiled=False)  9.53 us
    ppermute x3, waiting for transfers between devices, shifted(): return [block] + [lax.ppermute(block, axes, pair) for pair in pairs]  4.64 us
    pallas_call x1, Pallas kernels, norm_call(): pl.pallas_call(norm_kernel, grid=(seq_len // block,), in_specs=[pl.BlockS...  2.78 us
  transfers between devices with their start and end apart: 6, of which 1 were waited for; matrix products, arithmetic and copies ran while one was open for 1% of the time, Pallas kernels for 0%

profile of v10, /device:TPU:2, one launch (start us, length us, event | category | flops | bytes accessed | tf_op | source)
XLA Modules:
  0.0 111.5 jit_solution(11087992647819853613)
XLA Ops:
  0.6 2.8 %shard_map.104 = bf16[8,128,640]{2,1,0:T(8,128)(2,1)} custom-call(bf16[128,5120]{1,0:T(8,128)(2,1)} %bitcast.31, f32[1,5120]{1,0:T(1,128)} %bitcast.34), custom_call_target="tpu_custom_call" | custom-call | tf_op jit(solution)/shard_map/pallas_call | solution.py:55
  3.4 0.0 copy-start.4
  3.4 0.0 copy-start.2
  3.4 0.0 copy-start.3
  3.4 9.5 %all-to-all-start = ((bf16[8,128,640]{2,1,0:T(8,128)(2,1)}), bf16[8,128,640]{2,1,0:T(8,128)(2,1)S(1)}, u32[]{:S(2)}, u32[]{:S(2)}) async-start(bf16[8,128,640]{2,1,0:T(8,128)(2,1)} %shard_map.104), calls=%async_computation | async-start | bytes 2621440 | tf_op jit(solution)/shard_map/all_to_all | solution.py:23
  12.9 0.0 copy-done.4
  13.0 0.0 copy-start
  13.0 0.1 copy.12
  13.1 0.4 broadcast_in_dim.15
  13.5 0.0 copy-done.2
  13.5 0.0 copy-done.3
  13.5 0.2 subtract_convert_fusion
  13.7 1.9 %collective-permute-start.3 = (bf16[320,512]{1,0:T(8,128)(2,1)S(1)}, bf16[320,512]{1,0:T(8,128)(2,1)S(1)}, u32[]{:S(2)}, u32[]{:S(2)}) collective-permute-start(bf16[320,512]{1,0:T(8,128)(2,1)S(1)} %subtract_convert_fusion), channel_id=1, source_target_pairs={{0,8},{8,0},{1,9},{9,1},{2,10},{10,2},{3,11},{11,3},{4,12},{12,4},... | collective-permute-start | bytes 983048 | tf_op jit(solution)/shard_map/ppermute | solution.py:229
  15.6 0.0 copy-done
  15.6 4.0 %collective-permute-start.2 = (bf16[128,512]{1,0:T(8,128)(2,1)S(1)}, bf16[128,512]{1,0:T(8,128)(2,1)S(1)}, u32[]{:S(2)}, u32[]{:S(2)}) collective-permute-start(bf16[128,512]{1,0:T(8,128)(2,1)S(1)} %bitcast.24), channel_id=1, source_target_pairs={{0,4},{2,6},{4,0},{6,2},{1,5},{3,7},{5,1},{7,3},{8,12},{10,14},{12... | collective-permute-start | bytes 393224 | tf_op jit(solution)/shard_map/ppermute | solution.py:210
  19.6 3.4 %collective-permute-start.1 = (bf16[128,512]{1,0:T(8,128)(2,1)S(1)}, bf16[128,512]{1,0:T(8,128)(2,1)S(1)}, u32[]{:S(2)}, u32[]{:S(2)}) collective-permute-start(bf16[128,512]{1,0:T(8,128)(2,1)S(1)} %bitcast.25), channel_id=1, source_target_pairs={{0,6},{2,0},{4,2},{6,4},{1,7},{3,1},{5,3},{7,5},{8,14},{10,8},{12,... | collective-permute-start | bytes 393224 | tf_op jit(solution)/shard_map/ppermute | solution.py:210
  23.0 2.5 %collective-permute-start = (bf16[128,512]{1,0:T(8,128)(2,1)S(1)}, bf16[128,512]{1,0:T(8,128)(2,1)S(1)}, u32[]{:S(2)}, u32[]{:S(2)}) collective-permute-start(bf16[128,512]{1,0:T(8,128)(2,1)S(1)} %bitcast.26), channel_id=1, source_target_pairs={{0,2},{2,4},{4,6},{6,0},{1,3},{3,5},{5,7},{7,1},{8,10},{10,12},{12... | collective-permute-start | bytes 393224 | tf_op jit(solution)/shard_map/ppermute | solution.py:210
  26.8 0.1 pad_add_fusion.1.tags_ref
  26.9 0.1 pad_add_fusion.place_ref
  26.9 0.0 collective-permute-done.3
  27.1 1.9 %collective-permute-start.4 = (bf16[128,512]{1,0:T(8,128)(2,1)S(1)}, bf16[128,512]{1,0:T(8,128)(2,1)S(1)}, u32[]{:S(2)}, u32[]{:S(2)}) collective-permute-start(bf16[128,512]{1,0:T(8,128)(2,1)S(1)} %bitcast.27), channel_id=1, source_target_pairs={{0,1},{1,0},{2,3},{3,2},{4,5},{5,4},{6,7},{7,6},{8,9},{9,8},{10,11... | collective-permute-start | bytes 393224 | tf_op jit(solution)/shard_map/ppermute | solution.py:235
  29.0 4.6 %collective-permute-done.2 = bf16[128,512]{1,0:T(8,128)(2,1)S(1)} collective-permute-done((bf16[128,512]{1,0:T(8,128)(2,1)S(1)}, bf16[128,512]{1,0:T(8,128)(2,1)S(1)}, u32[]{:S(2)}, u32[]{:S(2)}) %collective-permute-start.2) | collective-permute-done | bytes 131104 | tf_op jit(solution)/shard_map/ppermute | solution.py:210
  33.6 2.0 %all-gather = bf16[256,512]{1,0:T(8,128)(2,1)S(1)} all-gather(bf16[128,512]{1,0:T(8,128)(2,1)S(1)} %collective-permute-done.2), channel_id=2, replica_groups=mesh['yh'=2,'zh'=4,'zl'=4,'yl'=2,'x'=4,'c'=2] {'c'}, dimensions={0}, use_global_device_ids=true | all-gather | bytes 393216 | tf_op jit(solution)/shard_map/all_gather | solution.py:237
  35.6 0.0 collective-permute-done.1
  35.6 0.0 collective-permute-done
  35.6 0.0 collective-permute-done.4.far_ref
  35.6 2.2 %all-gather.1 = bf16[4,128,512]{2,1,0:T(8,128)(2,1)S(1)} all-gather(bf16[2,128,512]{2,1,0:T(8,128)(2,1)S(1)} %pad_maximum_fusion.1), channel_id=3, replica_groups=mesh['yh'=2,'zh'=4,'zl'=4,'yl'=2,'x'=4,'c'=2] {'c'}, dimensions={0}, use_global_device_ids=true | all-gather | bytes 786432 | tf_op jit(solution)/shard_map/all_gather | solution.py:242
  37.8 0.0 all-to-all-done.columns_ref
  37.8 0.0 copy-start.1
  37.8 1.6 %shard_map.105 = f32[8,16,128]{2,1,0:T(8,128)S(1)} custom-call(s32[3]{0:T(128)S(1)} %pad_add_fusion.place_ref, s32[2]{0:T(128)S(1)} %pad_add_fusion.1.tags_ref, bf16[640,512]{1,0:T(8,128)(2,1)S(1)} %pad_maximum_fusion.delta_ref, bf16[8,128,640]{2,1,0:T(8,128)(2,1)S(1)} %all-to-all-done.columns_ref, bf16[128,512]{1,0:T(8,128)(2,1)S(1)} %bitcast.28, ...), custom_call_target="tpu_custom_call" | custom-call | tf_op jit(solution)/shard_map/pallas_call | solution.py:136
  39.4 8.3 %all_to_all.20.small_ref = f32[8,16,128]{2,1,0:T(8,128)S(1)} all-to-all(f32[8,16,128]{2,1,0:T(8,128)S(1)} %shard_map.105), channel_id=1, replica_groups=mesh['yh'=2,'zh'=4,'zl'=4,'yl'=2,'x'=4,'c'=2] {'x','c'}, dimensions={0} | all-to-all | bytes 131072 | tf_op jit(solution)/shard_map/all_to_all | solution.py:23
  47.7 0.0 copy-done.1
  47.7 1.9 %shard_map.106 = (bf16[16,160,128]{2,1,0:T(8,128)(2,1)S(1)}, f32[8,128]{1,0:T(8,128)S(1)}) custom-call(s32[3]{0:T(128)S(1)} %pad_add_fusion.place_ref, s32[1,8]{1,0:T(1,128)S(1)} %copy-done.1, f32[8,16,128]{2,1,0:T(8,128)S(1)} %all_to_all.20.small_ref, bf16[8,128,640]{2,1,0:T(8,128)(2,1)S(1)} %all-to-all-done.columns_ref, bf16[128,512]{1,0:T(8,128)(2,1)S(1)} %bitcast.29, ...), custom_call_target="tpu_custom_call" | custom-call | tf_op jit(solution)/shard_map/pallas_call | solution.py:195
  49.7 22.8 %all_to_all.21 = bf16[16,160,128]{2,1,0:T(8,128)(2,1)S(1)} all-to-all(bf16[16,160,128]{2,1,0:T(8,128)(2,1)S(1)} %get-tuple-element.25), channel_id=1, replica_groups=mesh['yh'=2,'zh'=4,'zl'=4,'yl'=2,'x'=4,'c'=2] {'zl','yh','yl'}, dimensions={0} | all-to-all | bytes 1310720 | tf_op jit(solution)/shard_map/all_to_all | solution.py:23
  72.5 0.1 add_convert_fusion.1
  72.6 24.0 %all_gather.20 = bf16[4,160,128]{2,1,0:T(8,128)(2,1)S(1)} all-gather(bf16[1,160,128]{2,1,0:T(8,128)(2,1)S(1)} %add_convert_fusion.1), channel_id=1, replica_groups=mesh['yh'=2,'zh'=4,'zl'=4,'yl'=2,'x'=4,'c'=2] {'zh'}, dimensions={0}, use_global_device_ids=true | all-gather | bytes 204800 | tf_op jit(solution)/shard_map/all_gather | solution.py:246
  96.8 13.8 %all_to_all.22.pieces_ref = bf16[8,160,128]{2,1,0:T(8,128)(2,1)S(1)} all-to-all(bf16[8,160,128]{2,1,0:T(8,128)(2,1)S(1)} %broadcast_in_dim.17), channel_id=1, replica_groups=mesh['yh'=2,'zh'=4,'zl'=4,'yl'=2,'x'=4,'c'=2] {'yh','zl'}, dimensions={0} | all-to-all | bytes 655360 | tf_op jit(solution)/shard_map/all_to_all | solution.py:23
  110.6 0.9 shard_map.107
  (5 shorter events, 0.2 us)
Async XLA Ops:
  3.4 9.5 %copy-start.4 = (f32[4,320]{1,0:T(4,128)S(1)}, f32[4,320]{1,0:T(4,128)}, u32[]{:S(2)}) copy-start(f32[4,320]{1,0:T(4,128)} %param.12) | copy-start | bytes 15364
  3.4 10.1 %copy-start.2 = (bf16[320,512]{1,0:T(8,128)(2,1)S(1)}, bf16[320,512]{1,0:T(8,128)(2,1)}, u32[]{:S(2)}) copy-start(bf16[320,512]{1,0:T(8,128)(2,1)} %param.13) | copy-start | bytes 983044
  3.4 10.1 %copy-start.3 = (bf16[320,512]{1,0:T(8,128)(2,1)S(1)}, bf16[320,512]{1,0:T(8,128)(2,1)}, u32[]{:S(2)}) copy-start(bf16[320,512]{1,0:T(8,128)(2,1)} %param.11) | copy-start | bytes 983044
  3.4 34.4 %all-to-all-start = ((bf16[8,128,640]{2,1,0:T(8,128)(2,1)}), bf16[8,128,640]{2,1,0:T(8,128)(2,1)S(1)}, u32[]{:S(2)}, u32[]{:S(2)}) async-start(bf16[8,128,640]{2,1,0:T(8,128)(2,1)} %shard_map.104), calls=%async_computation | async-start | bytes 2621440 | tf_op jit(solution)/shard_map/all_to_all | solution.py:23
  13.0 2.7 %copy-start = (bf16[1,128,512]{2,1,0:T(8,128)(2,1)S(1)}, bf16[1,128,512]{2,1,0:T(8,128)(2,1)}, u32[]{:S(2)}) copy-start(bf16[1,128,512]{2,1,0:T(8,128)(2,1)} %param.14) | copy-start | bytes 393220
  13.7 13.3 %collective-permute-start.3 = (bf16[320,512]{1,0:T(8,128)(2,1)S(1)}, bf16[320,512]{1,0:T(8,128)(2,1)S(1)}, u32[]{:S(2)}, u32[]{:S(2)}) collective-permute-start(bf16[320,512]{1,0:T(8,128)(2,1)S(1)} %subtract_convert_fusion), channel_id=1, source_target_pairs={{0,8},{8,0},{1,9},{9,1},{2,10},{10,2},{3,11},{11,3},{4,12},{12,4},... | collective-permute-start | bytes 983048 | tf_op jit(solution)/shard_map/ppermute | solution.py:229
  15.6 18.0 %collective-permute-start.2 = (bf16[128,512]{1,0:T(8,128)(2,1)S(1)}, bf16[128,512]{1,0:T(8,128)(2,1)S(1)}, u32[]{:S(2)}, u32[]{:S(2)}) collective-permute-start(bf16[128,512]{1,0:T(8,128)(2,1)S(1)} %bitcast.24), channel_id=1, source_target_pairs={{0,4},{2,6},{4,0},{6,2},{1,5},{3,7},{5,1},{7,3},{8,12},{10,14},{12... | collective-permute-start | bytes 393224 | tf_op jit(solution)/shard_map/ppermute | solution.py:210
  19.6 16.0 %collective-permute-start.1 = (bf16[128,512]{1,0:T(8,128)(2,1)S(1)}, bf16[128,512]{1,0:T(8,128)(2,1)S(1)}, u32[]{:S(2)}, u32[]{:S(2)}) collective-permute-start(bf16[128,512]{1,0:T(8,128)(2,1)S(1)} %bitcast.25), channel_id=1, source_target_pairs={{0,6},{2,0},{4,2},{6,4},{1,7},{3,1},{5,3},{7,5},{8,14},{10,8},{12,... | collective-permute-start | bytes 393224 | tf_op jit(solution)/shard_map/ppermute | solution.py:210
  23.0 12.6 %collective-permute-start = (bf16[128,512]{1,0:T(8,128)(2,1)S(1)}, bf16[128,512]{1,0:T(8,128)(2,1)S(1)}, u32[]{:S(2)}, u32[]{:S(2)}) collective-permute-start(bf16[128,512]{1,0:T(8,128)(2,1)S(1)} %bitcast.26), channel_id=1, source_target_pairs={{0,2},{2,4},{4,6},{6,0},{1,3},{3,5},{5,7},{7,1},{8,10},{10,12},{12... | collective-permute-start | bytes 393224 | tf_op jit(solution)/shard_map/ppermute | solution.py:210
  27.1 8.6 %collective-permute-start.4 = (bf16[128,512]{1,0:T(8,128)(2,1)S(1)}, bf16[128,512]{1,0:T(8,128)(2,1)S(1)}, u32[]{:S(2)}, u32[]{:S(2)}) collective-permute-start(bf16[128,512]{1,0:T(8,128)(2,1)S(1)} %bitcast.27), channel_id=1, source_target_pairs={{0,1},{1,0},{2,3},{3,2},{4,5},{5,4},{6,7},{7,6},{8,9},{9,8},{10,11... | collective-permute-start | bytes 393224 | tf_op jit(solution)/shard_map/ppermute | solution.py:235
  37.8 9.9 %copy-start.1 = (s32[1,8]{1,0:T(1,128)S(1)}, s32[1,8]{1,0:T(1,128)}, u32[]{:S(2)}) copy-start(s32[1,8]{1,0:T(1,128)} %bounds_ref.1) | copy-start | bytes 100
